TPU v7x, 32 devices: a whole 2x2x4 slice. The times are simulated.
32 devices in a mesh: dp: 2 (over y), blk: 4 (over z), head: 4 (over x, core).
Axes of the slice: x: 2, y: 2, z: 4, core: 2. Of those that a mesh axis runs over, the one named last changes fastest.
Arguments:
- queries: bfloat16 [2048, 2048], P(('dp', 'blk', 'head')), parts along dimension 0, may hold values from -5 to 5
- key_states: bfloat16 [2048, 2048], P(('dp', 'blk', 'head')), parts along dimension 0, may hold values from -5 to 5
- value_states: bfloat16 [2048, 2048], P(('dp', 'blk', 'head')), parts along dimension 0, may hold values from -6 to 6
- upstream: bfloat16 [2048, 2048], P(('dp', 'blk'), 'head'), parts along dimension 0, may hold values from -6 to 6
- clip_lengths: int32 [8], P('dp'), parts along dimension 0, may hold values from 1 to 512, 1024 in all
Outputs:
- attended: bfloat16 [2048, 2048], P(('dp', 'blk'), 'head'), parts along dimension 0
- query_grads: bfloat16 [2048, 2048], P(('dp', 'blk'), 'head'), parts along dimension 0
- key_grads: bfloat16 [2048, 2048], P(('dp', 'blk'), 'head'), parts along dimension 0
- value_grads: bfloat16 [2048, 2048], P(('dp', 'blk'), 'head'), parts along dimension 0
There are 2 independent parts, one for each index of `dp`. A program takes and returns all parts, laid end to end along the dimension named above; each array names one. Nothing has to cross between parts.
Inputs may be any that keep to these rules, and one draw needn't show every extreme that they name: `clip_lengths`: 4 clip lengths that sum to 1024; the longest has exactly 512 tokens.
All inputs are finite; a program needn't handle non-finite values.
Results may differ from a plain program's by a relative error of at most 0.015.
Values may be sent and summed in bfloat16 or wider, within the bound.
No kernel may reach another device: no remote copies, remote signals or barrier semaphores. Data moves between devices by JAX's collectives and lax.ppermute only.
A program may use at most 64 MiB of HBM per device.

v0:
```python
import jax
import jax.numpy as jnp
from jax import lax
from jax.sharding import PartitionSpec as P

HEAD_DIM = 128


masked_fill = -1e30


def shifted(block, axis, distance):
    devices = range(lax.axis_size(axis))
    route = [(i - distance, i) for i in devices if i - distance in devices]
    return lax.ppermute(block, axis, route)


def clip_index(clip_ends, positions, seq_total):
    counted = jnp.sum((positions[:, None] >= clip_ends[None, :]).astype(jnp.int32), axis=1)
    inside = (positions >= 0) & (positions < seq_total)
    return jnp.where(inside, counted, -1)


def head_columns(rows, head_index):
    return rows[:, head_index * HEAD_DIM : (head_index + 1) * HEAD_DIM]


def head_window(query_head, key_head, value_head, upstream_head, same_clip, key_from):
    score_scale = HEAD_DIM ** (-0.5)
    scores = score_scale * jnp.einsum(
        "qe,ke->qk", query_head, key_head, preferred_element_type=jnp.float32
    )
    scores = jnp.where(same_clip, scores, masked_fill)
    row_max = jnp.max(scores, axis=1, keepdims=True)
    totals = jnp.sum(jnp.where(same_clip, jnp.exp(scores - row_max), 0.0), axis=1, keepdims=True)
    log_norm = row_max + jnp.log(totals)
    chances = jnp.where(same_clip, jnp.exp(scores - log_norm), 0.0)
    weights = chances.astype(jnp.bfloat16)
    attended = jnp.dot(weights, value_head, preferred_element_type=jnp.float32).astype(jnp.bfloat16)
    offsets = jnp.sum(upstream_head.astype(jnp.float32) * attended.astype(jnp.float32), axis=1)
    dchances = jnp.einsum(
        "qe,ke->qk", upstream_head, value_head, preferred_element_type=jnp.float32
    )
    dscores = (chances * (dchances - offsets[:, None])).astype(jnp.bfloat16)
    query_part = score_scale * jnp.dot(dscores, key_head, preferred_element_type=jnp.float32)
    key_part = score_scale * jnp.einsum(
        "qk,qe->ke", dscores[:, key_from:], query_head, preferred_element_type=jnp.float32
    )
    value_part = jnp.einsum(
        "qk,qe->ke", weights[:, key_from:], upstream_head, preferred_element_type=jnp.float32
    )
    return (attended, query_part, key_part, value_part, log_norm[:, 0], offsets)


def window_pass(query_rows, key_window, value_window, upstream, same_clip, key_from):
    heads_here = query_rows.shape[1] // HEAD_DIM
    collected = [[], [], [], [], [], []]
    for head_index in range(heads_here):
        outcome = head_window(
            head_columns(query_rows, head_index),
            head_columns(key_window, head_index),
            head_columns(value_window, head_index),
            head_columns(upstream, head_index),
            same_clip,
            key_from,
        )
        for field_index in range(6):
            collected[field_index].append(outcome[field_index])
    attended = jnp.concatenate(collected[0], axis=1)
    query_part = jnp.concatenate(collected[1], axis=1)
    key_part = jnp.concatenate(collected[2], axis=1)
    value_part = jnp.concatenate(collected[3], axis=1)
    return (
        attended,
        query_part,
        key_part,
        value_part,
        jnp.stack(collected[4]),
        jnp.stack(collected[5]),
    )


def head_neighbour(query_head, upstream_head, key_head, value_head, same_clip, log_norm, offsets):
    score_scale = HEAD_DIM ** (-0.5)
    scores = score_scale * jnp.einsum(
        "qe,ke->qk", query_head, key_head, preferred_element_type=jnp.float32
    )
    scores = jnp.where(same_clip, scores, masked_fill)
    chances = jnp.where(same_clip, jnp.exp(scores - log_norm[:, None]), 0.0)
    weights = chances.astype(jnp.bfloat16)
    dchances = jnp.einsum(
        "qe,ke->qk", upstream_head, value_head, preferred_element_type=jnp.float32
    )
    dscores = (chances * (dchances - offsets[:, None])).astype(jnp.bfloat16)
    key_part = score_scale * jnp.einsum(
        "qk,qe->ke", dscores, query_head, preferred_element_type=jnp.float32
    )
    value_part = jnp.einsum("qk,qe->ke", weights, upstream_head, preferred_element_type=jnp.float32)
    return (key_part, value_part)


def neighbour_pass(query_rows, upstream_rows, key_rows, value_rows, same_clip, log_norm, offsets):
    heads_here = query_rows.shape[1] // HEAD_DIM
    key_list = []
    value_list = []
    for head_index in range(heads_here):
        key_part, value_part = head_neighbour(
            head_columns(query_rows, head_index),
            head_columns(upstream_rows, head_index),
            head_columns(key_rows, head_index),
            head_columns(value_rows, head_index),
            same_clip,
            log_norm[head_index],
            offsets[head_index],
        )
        key_list.append(key_part)
        value_list.append(value_part)
    return (jnp.concatenate(key_list, axis=1), jnp.concatenate(value_list, axis=1))


def pass_keys(key_rows, value_rows):
    return shifted(jnp.stack([key_rows, value_rows]), "blk", 1)


def on_device(queries, key_states, value_states, upstream, clip_lengths):
    query_rows, key_rows, value_rows = (
        lax.all_to_all(queries, "head", split_axis=1, concat_axis=0, tiled=True),
        lax.all_to_all(key_states, "head", split_axis=1, concat_axis=0, tiled=True),
        lax.all_to_all(value_states, "head", split_axis=1, concat_axis=0, tiled=True),
    )
    previous = pass_keys(key_rows, value_rows)
    block_rows = upstream.shape[0]
    clip_ends = jnp.cumsum(clip_lengths)
    seq_total = block_rows * lax.axis_size("blk")
    first_row = lax.axis_index("blk") * block_rows
    positions = first_row - block_rows + jnp.arange(3 * block_rows, dtype=jnp.int32)
    all_ids = clip_index(clip_ends, positions, seq_total)
    window_ids = all_ids[: 2 * block_rows]
    own_ids = all_ids[block_rows : 2 * block_rows]
    next_ids = all_ids[2 * block_rows :]
    window_mask = own_ids[:, None] == window_ids[None, :]
    key_window = jnp.concatenate([previous[0], key_rows], axis=0)
    value_window = jnp.concatenate([previous[1], value_rows], axis=0)
    next_rows = shifted(jnp.stack([query_rows, upstream]), "blk", -1)
    attended, query_part, key_part, value_part, log_norm, offsets = window_pass(
        query_rows, key_window, value_window, upstream, window_mask, block_rows
    )
    next_stats = shifted(jnp.stack([log_norm, offsets]), "blk", -1)
    next_mask = next_ids[:, None] == own_ids[None, :]
    near_key, near_value = neighbour_pass(
        next_rows[0], next_rows[1], key_rows, value_rows, next_mask, next_stats[0], next_stats[1]
    )
    key_total = key_part + near_key
    value_total = value_part + near_value
    return (
        attended,
        query_part.astype(jnp.bfloat16),
        key_total.astype(jnp.bfloat16),
        value_total.astype(jnp.bfloat16),
    )


def solution(mesh):
    return jax.shard_map(
        on_device,
        mesh=mesh,
        in_specs=(
            P(("dp", "blk", "head"), None),
            P(("dp", "blk", "head"), None),
            P(("dp", "blk", "head"), None),
            P(("dp", "blk"), "head"),
            P("dp"),
        ),
        out_specs=(
            P(("dp", "blk"), "head"),
            P(("dp", "blk"), "head"),
            P(("dp", "blk"), "head"),
            P(("dp", "blk"), "head"),
        ),
        check_vma=False,
    )
```

profile of v0, /device:TPU:0, one launch (start us, length us, event | category | flops | bytes accessed | tf_op | source)
XLA Modules:
  0.0 58.9 jit_solution(947546516491335)
XLA Ops:
  0.6 1.7 %copy.73 = bf16[8,4,8,512]{3,2,0,1:T(8,128)(2,1)} copy(bf16[8,4,8,512]{3,2,1,0:T(8,128)(2,1)} %bitcast.144) | data formatting | bytes 524288 | tf_op jit(solution)/shard_map/all_to_all | solution.py:129
  2.3 4.3 %all-to-all-start.1 = ((bf16[64,4,512]{2,0,1:T(8,128)(2,1)}), bf16[64,4,512]{2,0,1:T(8,128)(2,1)S(1)}, u32[]{:S(2)}, u32[]{:S(2)}) async-start(bf16[64,4,512]{2,0,1:T(8,128)(2,1)} %bitcast.108), calls=%async_computation.1 | async-start | bytes 524288 | tf_op jit(solution)/shard_map/all_to_all | solution.py:129
  6.7 0.1 copy.65
  6.8 0.8 %copy-done.1 = bf16[64,2048]{1,0:T(8,128)(2,1)S(1)} copy-done((bf16[64,2048]{1,0:T(8,128)(2,1)S(1)}, bf16[64,2048]{1,0:T(8,128)(2,1)}, u32[]{:S(2)}) %copy-start.1) | copy-done | bytes 262168
  7.6 0.7 %copy.72 = bf16[8,4,8,512]{3,2,0,1:T(8,128)(2,1)} copy(bf16[8,4,8,512]{3,2,1,0:T(8,128)(2,1)S(1)} %bitcast.145) | data formatting | bytes 524288 | tf_op jit(solution)/shard_map/all_to_all | solution.py:127
  8.3 0.3 copy-done.2
  8.6 0.7 %copy.74 = bf16[8,4,8,512]{3,2,0,1:T(8,128)(2,1)} copy(bf16[8,4,8,512]{3,2,1,0:T(8,128)(2,1)S(1)} %bitcast.146) | data formatting | bytes 524288 | tf_op jit(solution)/shard_map/all_to_all | solution.py:128
  9.4 0.7 %copy-done.3 = s32[4]{0:T(128)S(1)} copy-done((s32[4]{0:T(128)S(1)}, s32[4]{0:T(128)}, u32[]{:S(2)}) %copy-start.3) | copy-done | bytes 40
  10.0 0.2 reduce-window.8
  10.2 2.5 %all-to-all-done.1 = bf16[64,4,512]{2,0,1:T(8,128)(2,1)S(1)} async-done(((bf16[64,4,512]{2,0,1:T(8,128)(2,1)}), bf16[64,4,512]{2,0,1:T(8,128)(2,1)S(1)}, u32[]{:S(2)}, u32[]{:S(2)}) %all-to-all-start.1) | async-done | bytes 262176 | tf_op jit(solution)/shard_map/all_to_all | solution.py:129
  12.7 3.4 %all-to-all-start = ((bf16[64,4,512]{2,0,1:T(8,128)(2,1)}), bf16[64,4,512]{2,0,1:T(8,128)(2,1)S(1)}, u32[]{:S(2)}, u32[]{:S(2)}) async-start(bf16[64,4,512]{2,0,1:T(8,128)(2,1)} %bitcast.109), calls=%async_computation | async-start | bytes 524288 | tf_op jit(solution)/shard_map/all_to_all | solution.py:128
  16.2 5.9 %all-to-all-done = bf16[64,4,512]{2,0,1:T(8,128)(2,1)S(1)} async-done(((bf16[64,4,512]{2,0,1:T(8,128)(2,1)}), bf16[64,4,512]{2,0,1:T(8,128)(2,1)S(1)}, u32[]{:S(2)}, u32[]{:S(2)}) %all-to-all-start) | async-done | bytes 262176 | tf_op jit(solution)/shard_map/all_to_all | solution.py:128
  22.1 3.4 %all-to-all-start.2 = ((bf16[64,4,512]{2,0,1:T(8,128)(2,1)}), bf16[64,4,512]{2,0,1:T(8,128)(2,1)S(1)}, u32[]{:S(2)}, u32[]{:S(2)}) async-start(bf16[64,4,512]{2,0,1:T(8,128)(2,1)} %bitcast.107), calls=%async_computation.2 | async-start | bytes 524288 | tf_op jit(solution)/shard_map/all_to_all | solution.py:127
  25.6 4.1 %collective-permute-start = (bf16[2,256,512]{2,1,0:T(8,128)(2,1)S(1)}, bf16[2,256,512]{2,1,0:T(8,128)(2,1)S(1)}, u32[]{:S(2)}, u32[]{:S(2)}) collective-permute-start(bf16[2,256,512]{2,1,0:T(8,128)(2,1)S(1)} %pad_maximum_fusion), channel_id=1, source_target_pairs={{0,4},{4,8},{8,12},{1,5},{5,9},{9,13},{2,6},{6,10},{10,14},{3,7},{... | collective-permute-start | bytes 1572872 | tf_op jit(solution)/shard_map/ppermute | solution.py:15
  29.7 0.1 copy.64
  29.9 0.1 copy.63
  30.0 0.1 copy.62
  30.1 1.4 %all-to-all-done.2 = bf16[64,4,512]{2,0,1:T(8,128)(2,1)S(1)} async-done(((bf16[64,4,512]{2,0,1:T(8,128)(2,1)}), bf16[64,4,512]{2,0,1:T(8,128)(2,1)S(1)}, u32[]{:S(2)}, u32[]{:S(2)}) %all-to-all-start.2) | async-done | bytes 262176 | tf_op jit(solution)/shard_map/all_to_all | solution.py:127
  31.6 1.3 %collective-permute-start.1 = (bf16[2,256,512]{2,1,0:T(8,128)(2,1)S(1)}, bf16[2,256,512]{2,1,0:T(8,128)(2,1)S(1)}, u32[]{:S(2)}, u32[]{:S(2)}) collective-permute-start(bf16[2,256,512]{2,1,0:T(8,128)(2,1)S(1)} %pad_maximum_fusion.1), channel_id=1, source_target_pairs={{4,0},{8,4},{12,8},{5,1},{9,5},{13,9},{6,2},{10,6},{14,10},{7,3},{... | collective-permute-start | bytes 1572872 | tf_op jit(solution)/shard_map/ppermute | solution.py:15
  32.9 8.6 %collective-permute-done = bf16[2,256,512]{2,1,0:T(8,128)(2,1)S(1)} collective-permute-done((bf16[2,256,512]{2,1,0:T(8,128)(2,1)S(1)}, bf16[2,256,512]{2,1,0:T(8,128)(2,1)S(1)}, u32[]{:S(2)}, u32[]{:S(2)}) %collective-permute-start) | collective-permute-done | bytes 524320 | tf_op jit(solution)/shard_map/ppermute | solution.py:15
  41.5 0.3 fusion.155
  41.8 0.3 fusion.157
  42.1 0.3 fusion.158
  42.4 0.3 fusion.156
  42.7 0.4 fusion.52
  43.1 0.4 fusion.58
  43.5 0.2 multiply_reduce_fusion.1
  43.7 0.2 fusion.13
  44.0 0.2 fusion.50
  44.2 0.2 convolution_multiply_fusion.13
  44.4 0.2 multiply_reduce_fusion.2
  44.7 0.2 fusion.14
  44.9 0.2 fusion.49
  45.2 0.2 convolution_multiply_fusion.14
  45.4 0.2 multiply_reduce_fusion.3
  45.6 0.2 fusion.15
  45.9 0.2 fusion.48
  46.1 0.2 convolution_multiply_fusion.15
  46.4 0.2 fusion.70
  46.6 0.2 fusion.72
  46.8 0.2 fusion.74
  47.0 0.2 fusion.68
  47.2 0.2 multiply_reduce_fusion
  47.5 0.2 fusion.12
  47.8 1.3 %collective-permute-start.2 = (f32[2,4,256]{2,1,0:T(4,128)S(1)}, f32[2,4,256]{2,1,0:T(4,128)S(1)}, u32[]{:S(2)}, u32[]{:S(2)}) collective-permute-start(f32[2,4,256]{2,1,0:T(4,128)S(1)} %pad_maximum_fusion.6), channel_id=1, source_target_pairs={{4,0},{8,4},{12,8},{5,1},{9,5},{13,9},{6,2},{10,6},{14,10},{7,3},{... | collective-permute-start | bytes 24584 | tf_op jit(solution)/shard_map/ppermute | solution.py:15
  49.1 0.2 convolution_multiply_fusion.12
  49.3 0.2 fusion.51
  49.7 0.8 %copy.58 = bf16[256,512]{1,0:T(8,128)(2,1)} copy(bf16[256,512]{0,1:T(8,128)(2,1)S(1)} %pad_maximum_fusion.2) | data formatting | bytes 524288
  50.5 0.8 %copy.59 = bf16[256,512]{1,0:T(8,128)(2,1)} copy(bf16[256,512]{0,1:T(8,128)(2,1)S(1)} %pad_maximum_fusion.3) | data formatting | bytes 524288
  51.4 2.4 %collective-permute-done.2 = f32[2,4,256]{2,1,0:T(4,128)S(1)} collective-permute-done((f32[2,4,256]{2,1,0:T(4,128)S(1)}, f32[2,4,256]{2,1,0:T(4,128)S(1)}, u32[]{:S(2)}, u32[]{:S(2)}) %collective-permute-start.2) | collective-permute-done | bytes 8224 | tf_op jit(solution)/shard_map/ppermute | solution.py:15
  53.8 0.2 fusion.20
  54.0 0.2 fusion.80
  54.3 0.4 fusion.41
  54.6 0.2 fusion.25
  54.9 0.2 fusion.82
  55.1 0.4 fusion.43
  55.5 0.2 fusion.30
  55.7 0.2 fusion.84
  55.9 0.4 fusion.45
  56.3 0.2 fusion.35
  56.5 0.2 fusion.86
  56.7 0.4 fusion.47
  57.2 0.8 %copy.60 = bf16[256,512]{1,0:T(8,128)(2,1)} copy(bf16[256,512]{0,1:T(8,128)(2,1)S(1)} %fusion.56) | data formatting | bytes 524288
  58.1 0.8 %copy.61 = bf16[256,512]{1,0:T(8,128)(2,1)} copy(bf16[256,512]{0,1:T(8,128)(2,1)S(1)} %fusion.57) | data formatting | bytes 524288
  (29 shorter events, 0.6 us)
Async XLA Ops:
  2.3 4.3 %copy-start = (bf16[256,512]{1,0:T(8,128)(2,1)S(1)}, bf16[256,512]{1,0:T(8,128)(2,1)}, u32[]{:S(2)}) copy-start(bf16[256,512]{1,0:T(8,128)(2,1)} %param.8) | copy-start | bytes 786436
  2.3 10.4 %all-to-all-start.1 = ((bf16[64,4,512]{2,0,1:T(8,128)(2,1)}), bf16[64,4,512]{2,0,1:T(8,128)(2,1)S(1)}, u32[]{:S(2)}, u32[]{:S(2)}) async-start(bf16[64,4,512]{2,0,1:T(8,128)(2,1)} %bitcast.108), calls=%async_computation.1 | async-start | bytes 524288 | tf_op jit(solution)/shard_map/all_to_all | solution.py:129
  6.6 1.0 %copy-start.1 = (bf16[64,2048]{1,0:T(8,128)(2,1)S(1)}, bf16[64,2048]{1,0:T(8,128)(2,1)}, u32[]{:S(2)}) copy-start(bf16[64,2048]{1,0:T(8,128)(2,1)} %param.5) | copy-start | bytes 786436
  7.6 1.0 %copy-start.2 = (bf16[64,2048]{1,0:T(8,128)(2,1)S(1)}, bf16[64,2048]{1,0:T(8,128)(2,1)}, u32[]{:S(2)}) copy-start(bf16[64,2048]{1,0:T(8,128)(2,1)} %param.6) | copy-start | bytes 786436
  9.4 0.7 %copy-start.3 = (s32[4]{0:T(128)S(1)}, s32[4]{0:T(128)}, u32[]{:S(2)}) copy-start(s32[4]{0:T(128)} %param.9) | copy-start | bytes 52
  12.7 9.4 %all-to-all-start = ((bf16[64,4,512]{2,0,1:T(8,128)(2,1)}), bf16[64,4,512]{2,0,1:T(8,128)(2,1)S(1)}, u32[]{:S(2)}, u32[]{:S(2)}) async-start(bf16[64,4,512]{2,0,1:T(8,128)(2,1)} %bitcast.109), calls=%async_computation | async-start | bytes 524288 | tf_op jit(solution)/shard_map/all_to_all | solution.py:128
  22.1 9.4 %all-to-all-start.2 = ((bf16[64,4,512]{2,0,1:T(8,128)(2,1)}), bf16[64,4,512]{2,0,1:T(8,128)(2,1)S(1)}, u32[]{:S(2)}, u32[]{:S(2)}) async-start(bf16[64,4,512]{2,0,1:T(8,128)(2,1)} %bitcast.107), calls=%async_computation.2 | async-start | bytes 524288 | tf_op jit(solution)/shard_map/all_to_all | solution.py:127
  25.6 15.9 %collective-permute-start = (bf16[2,256,512]{2,1,0:T(8,128)(2,1)S(1)}, bf16[2,256,512]{2,1,0:T(8,128)(2,1)S(1)}, u32[]{:S(2)}, u32[]{:S(2)}) collective-permute-start(bf16[2,256,512]{2,1,0:T(8,128)(2,1)S(1)} %pad_maximum_fusion), channel_id=1, source_target_pairs={{0,4},{4,8},{8,12},{1,5},{5,9},{9,13},{2,6},{6,10},{10,14},{3,7},{... | collective-permute-start | bytes 1572872 | tf_op jit(solution)/shard_map/ppermute | solution.py:15
  31.6 18.0 %collective-permute-start.1 = (bf16[2,256,512]{2,1,0:T(8,128)(2,1)S(1)}, bf16[2,256,512]{2,1,0:T(8,128)(2,1)S(1)}, u32[]{:S(2)}, u32[]{:S(2)}) collective-permute-start(bf16[2,256,512]{2,1,0:T(8,128)(2,1)S(1)} %pad_maximum_fusion.1), channel_id=1, source_target_pairs={{4,0},{8,4},{12,8},{5,1},{9,5},{13,9},{6,2},{10,6},{14,10},{7,3},{... | collective-permute-start | bytes 1572872 | tf_op jit(solution)/shard_map/ppermute | solution.py:15
  47.8 6.0 %collective-permute-start.2 = (f32[2,4,256]{2,1,0:T(4,128)S(1)}, f32[2,4,256]{2,1,0:T(4,128)S(1)}, u32[]{:S(2)}, u32[]{:S(2)}) collective-permute-start(f32[2,4,256]{2,1,0:T(4,128)S(1)} %pad_maximum_fusion.6), channel_id=1, source_target_pairs={{4,0},{8,4},{12,8},{5,1},{9,5},{13,9},{6,2},{10,6},{14,10},{7,3},{... | collective-permute-start | bytes 24584 | tf_op jit(solution)/shard_map/ppermute | solution.py:15
where the time goes:
time: 59.5 us; the launch traced here: 58.9 us
  waiting for transfers between devices  20.9 us (35%)
  starting transfers between devices  17.9 us (30%)
  matrix products  8.91 us (15%)
  local copies, waits for them, and re-layouts  8.82 us (15%)
  other arithmetic  1.41 us (2%)
  between operations  1.08 us (2%)
    ppermute x3, waiting for transfers between devices, shifted(): return lax.ppermute(block, axis, route)  11 us
    ppermute x3, starting transfers between devices, shifted(): return lax.ppermute(block, axis, route)  6.72 us
    all_to_all x1, waiting for transfers between devices, on_device(): lax.all_to_all(key_states, 'head', split_axis=1, concat_axis=0, tiled=True)  5.91 us
    unnamed x17, local copies, waits for them, and re-layouts  5.61 us
    all_to_all x1, starting transfers between devices, on_device(): lax.all_to_all(value_states, 'head', split_axis=1, concat_axis=0, tiled=T...  4.34 us
    all_to_all x1, starting transfers between devices, on_device(): lax.all_to_all(queries, 'head', split_axis=1, concat_axis=0, tiled=True)  3.41 us
    all_to_all x1, starting transfers between devices, on_device(): lax.all_to_all(key_states, 'head', split_axis=1, concat_axis=0, tiled=True)  3.41 us
    all_to_all x1, waiting for transfers between devices, on_device(): lax.all_to_all(value_states, 'head', split_axis=1, concat_axis=0, tiled=T...  2.48 us
  transfers between devices with their start and end apart: 6, of which 5 were waited for; matrix products, arithmetic and copies ran while one was open for 18% of the time, Pallas kernels for 0%

commit v1 on v0

v1 whole, which is shorter than its diff:
```python
import math

import jax
import jax.numpy as jnp
from jax import lax
from jax.experimental import pallas as pl
from jax.experimental.pallas import tpu as pltpu
from jax.sharding import PartitionSpec as P

HEAD_DIM = 128

masked_fill = -1e30
score_scale = HEAD_DIM ** (-0.5)
exp2_scale = score_scale * math.log2(math.e)

VMEM = pl.BlockSpec(memory_space=pltpu.VMEM)
SMEM = pl.BlockSpec(memory_space=pltpu.SMEM)
ANY = pl.BlockSpec(memory_space=pl.ANY)


def bf16(*shape):
    return jax.ShapeDtypeStruct(shape, jnp.bfloat16)


def partner_exchange(rows, step):
    route = [(i, i ^ step) for i in range(lax.axis_size("head"))]
    return lax.ppermute(rows, "head", route)


def block_exchange(rows, parity):
    parts, blocks = lax.axis_size("dp"), lax.axis_size("blk")
    route = []
    for part in range(parts):
        for block in range(blocks):
            other = block + 1 if block % 2 == parity else block - 1
            if 0 <= other < blocks:
                route.append((part * blocks + block, part * blocks + other))
            elif part ^ 1 < parts:
                route.append((part * blocks + block, (part ^ 1) * blocks + block))
    return lax.ppermute(rows, ("dp", "blk"), route)


def to_previous(rows):
    blocks = lax.axis_size("blk")
    return lax.ppermute(rows, "blk", [(i, i - 1) for i in range(1, blocks)])


def is_even():
    return lax.rem(lax.axis_index("blk"), 2) == 0


def place(step, size):
    owner = jnp.bitwise_xor(lax.axis_index("head"), step)
    return pl.ds(pl.multiple_of(owner * size, size), size)


def cut_pieces(queries, key_states, value_states, upstream):
    sharers = lax.axis_size("head")
    rows, features = queries.shape
    width = features // sharers
    block_rows = rows * sharers

    def kernel(q, k, v, u, *rest):
        pairs, singles = rest[:sharers], rest[sharers : 2 * sharers]
        first, second, sems = rest[2 * sharers :]
        copies = []

        def copy(source, target):
            copies.append(pltpu.make_async_copy(source, target, sems.at[len(copies)]))

        for step in range(sharers):
            columns = place(step, width)
            copy(k.at[:, columns], pairs[step].at[pl.ds(0, rows)])
            copy(q.at[:, columns], pairs[step].at[pl.ds(rows, rows)])
            copy(v.at[:, columns], singles[step])

        def swap(forward, backward):
            made = []
            for step in range(sharers):
                made.append(
                    pltpu.make_async_copy(
                        v.at[:, pl.ds(step * width, width)],
                        forward.at[pl.ds(step * rows, rows)],
                        sems.at[len(copies) + step],
                    )
                )
            made.append(pltpu.make_async_copy(u, backward, sems.at[len(copies) + sharers]))
            return made

        for c in copies:
            c.start()

        @pl.when(is_even())
        def _():
            for c in swap(first, second):
                c.start()
            for c in swap(first, second):
                c.wait()

        @pl.when(jnp.logical_not(is_even()))
        def _():
            for c in swap(second, first):
                c.start()
            for c in swap(second, first):
                c.wait()

        for c in copies:
            c.wait()

    out = pl.pallas_call(
        kernel,
        out_shape=[bf16(2 * rows, width)] * sharers
        + [bf16(rows, width)] * sharers
        + [bf16(block_rows, width)] * 2,
        in_specs=[ANY] * 4,
        out_specs=[VMEM] * (2 * sharers + 2),
        scratch_shapes=[pltpu.SemaphoreType.DMA((4 * sharers + 1,))],
        name="cut_pieces",
    )(queries, key_states, value_states, upstream)
    return out[:sharers], out[sharers : 2 * sharers], out[2 * sharers], out[2 * sharers + 1]


def join_keys_queries(pairs):
    sharers = len(pairs)
    rows, width = pairs[0].shape[0] // 2, pairs[0].shape[1]
    block_rows = rows * sharers

    def kernel(*refs):
        pairs_in = refs[:sharers]
        keys, queries, first, second = refs[sharers:]
        for step in range(sharers):
            where = place(step, rows)
            keys[where, :] = pairs_in[step][pl.ds(0, rows), :]
            queries[where, :] = pairs_in[step][pl.ds(rows, rows), :]

        @pl.when(is_even())
        def _():
            first[...] = keys[...]
            second[...] = queries[...]

        @pl.when(jnp.logical_not(is_even()))
        def _():
            first[...] = queries[...]
            second[...] = keys[...]

    return pl.pallas_call(
        kernel,
        out_shape=[bf16(block_rows, width)] * 4,
        in_specs=[VMEM] * sharers,
        out_specs=[VMEM] * 4,
        name="join_keys_queries",
    )(*pairs)


def cut_previous_values(first_got, second_got, sharers):
    block_rows, width = first_got.shape
    rows = block_rows // sharers

    def kernel(first, second, *out):
        def split(forward, backward):
            for step in range(sharers):
                out[step][...] = forward[place(step, rows), :]
            out[sharers][...] = backward[...]

        @pl.when(is_even())
        def _():
            split(second, first)

        @pl.when(jnp.logical_not(is_even()))
        def _():
            split(first, second)

    out = pl.pallas_call(
        kernel,
        out_shape=[bf16(rows, width)] * sharers + [bf16(block_rows, width)],
        in_specs=[VMEM] * 2,
        out_specs=[VMEM] * (sharers + 1),
        name="cut_previous_values",
    )(first_got, second_got)
    return out[:sharers], out[sharers]


def clip_ids(lengths, shape, axis, block, blocks):
    position = block * shape[axis] + lax.broadcasted_iota(jnp.int32, shape, axis)
    ids, end = jnp.zeros(shape, jnp.int32), jnp.int32(0)
    for clip in range(lengths.shape[0]):
        end = end + lengths[clip]
        ids = ids + (position >= end).astype(jnp.int32)
    return jnp.where(jnp.logical_and(block >= 0, block < blocks), ids, -1)


def mask_bias(key_ids, query_ids):
    return jnp.where(key_ids == query_ids, 0.0, masked_fill).astype(jnp.float32)


def by_rows(a, b):
    return lax.dot_general(a, b, (((1,), (1,)), ((), ())), preferred_element_type=jnp.float32)


def by_columns(a, b):
    return lax.dot_general(a, b, (((0,), (0,)), ((), ())), preferred_element_type=jnp.float32)


def product(a, b):
    return jnp.dot(a, b, preferred_element_type=jnp.float32)


def own_part(keys, queries, singles, upstream, clip_lengths):
    sharers = len(singles)
    block_rows, width = keys.shape
    rows = block_rows // sharers
    heads = width // HEAD_DIM

    def kernel(k, q, u, lengths, *rest):
        singles_in = rest[:sharers]
        values, stats, bias = rest[sharers:]
        block, blocks = lax.axis_index("blk"), lax.axis_size("blk")
        for step in range(sharers):
            values[place(step, rows), :] = singles_in[step][...]
        bias[...] = mask_bias(
            clip_ids(lengths, (block_rows, 1), 0, block, blocks),
            clip_ids(lengths, (1, block_rows), 1, block, blocks),
        )
        for head in range(heads):
            columns = pl.ds(head * HEAD_DIM, HEAD_DIM)
            scores = by_rows(k[:, columns], q[:, columns]) * exp2_scale + bias[...]
            row_max = jnp.max(scores, axis=0, keepdims=True)
            grown = jnp.exp2(scores - row_max)
            totals = jnp.sum(grown, axis=0, keepdims=True)
            dchances = by_rows(values[:, columns], u[:, columns])
            offset = jnp.sum(grown * dchances, axis=0, keepdims=True) / totals
            stats[pl.ds(head, 1), :] = row_max + jnp.log2(totals)
            stats[pl.ds(heads + head, 1), :] = offset

    return pl.pallas_call(
        kernel,
        out_shape=[bf16(block_rows, width), jax.ShapeDtypeStruct((2 * heads, block_rows), jnp.float32)],
        in_specs=[VMEM] * 3 + [SMEM] + [VMEM] * sharers,
        out_specs=[VMEM] * 2,
        scratch_shapes=[pltpu.VMEM((block_rows, block_rows), jnp.float32)],
        compiler_params=pltpu.CompilerParams(vmem_limit_bytes=24 * 2**20),
        name="own_part",
    )(keys, queries, upstream, clip_lengths, *singles)


def window(keys, queries, values, upstream, first_got, second_got, previous_values, next_upstream, next_stats, clip_lengths):
    sharers = len(previous_values)
    block_rows, width = keys.shape
    rows = block_rows // sharers
    heads = width // HEAD_DIM
    square = (block_rows, block_rows)

    def kernel(k, q, v, u, first, second, nu, stats, lengths, *rest):
        pieces = rest[:sharers]
        attended, query_grads, key_grads, value_grads = rest[sharers : sharers + 4]
        pk, nq, pv, own_bias, previous_bias, next_bias = rest[sharers + 4 :]
        block, blocks = lax.axis_index("blk"), lax.axis_size("blk")

        @pl.when(is_even())
        def _():
            pk[...] = second[...]
            nq[...] = first[...]

        @pl.when(jnp.logical_not(is_even()))
        def _():
            pk[...] = first[...]
            nq[...] = second[...]

        for step in range(sharers):
            pv[place(step, rows), :] = pieces[step][...]

        tall, wide = (block_rows, 1), (1, block_rows)
        key_ids = clip_ids(lengths, tall, 0, block, blocks)
        query_ids = clip_ids(lengths, wide, 1, block, blocks)
        own_bias[...] = mask_bias(key_ids, query_ids)
        previous_bias[...] = mask_bias(clip_ids(lengths, tall, 0, block - 1, blocks), query_ids)
        next_bias[...] = mask_bias(key_ids, clip_ids(lengths, wide, 1, block + 1, blocks))

        for head in range(heads):
            columns = pl.ds(head * HEAD_DIM, HEAD_DIM)
            key, query, value, up = k[:, columns], q[:, columns], v[:, columns], u[:, columns]
            past_key, past_value = pk[:, columns], pv[:, columns]
            later_query, later_up = nq[:, columns], nu[:, columns]

            scores = by_rows(key, query) * exp2_scale + own_bias[...]
            past_scores = by_rows(past_key, query) * exp2_scale + previous_bias[...]
            row_max = jnp.maximum(
                jnp.max(scores, axis=0, keepdims=True), jnp.max(past_scores, axis=0, keepdims=True)
            )
            grown = jnp.exp2(scores - row_max)
            past_grown = jnp.exp2(past_scores - row_max)
            share = 1.0 / (
                jnp.sum(grown, axis=0, keepdims=True) + jnp.sum(past_grown, axis=0, keepdims=True)
            )
            chances = grown * share
            past_chances = past_grown * share
            dchances = by_rows(value, up)
            past_dchances = by_rows(past_value, up)
            offset = jnp.sum(chances * dchances, axis=0, keepdims=True) + jnp.sum(
                past_chances * past_dchances, axis=0, keepdims=True
            )
            dscores = (chances * (dchances - offset)).astype(jnp.bfloat16)
            past_dscores = (past_chances * (past_dchances - offset)).astype(jnp.bfloat16)
            weights = chances.astype(jnp.bfloat16)
            past_weights = past_chances.astype(jnp.bfloat16)
            attended[:, columns] = (
                by_columns(weights, value) + by_columns(past_weights, past_value)
            ).astype(jnp.bfloat16)
            query_grads[:, columns] = (
                score_scale * (by_columns(dscores, key) + by_columns(past_dscores, past_key))
            ).astype(jnp.bfloat16)

            later_scores = by_rows(key, later_query) * exp2_scale + next_bias[...]
            later_max = jnp.max(later_scores, axis=0, keepdims=True)
            later_grown = jnp.exp2(later_scores - later_max)
            later_total = jnp.sum(later_grown, axis=0, keepdims=True)
            later_dchances = by_rows(value, later_up)
            later_offset = jnp.sum(later_grown * later_dchances, axis=0, keepdims=True) / later_total
            far_norm, far_offset = stats[pl.ds(head, 1), :], stats[pl.ds(heads + head, 1), :]
            near_norm = later_max + jnp.log2(later_total)
            top = jnp.maximum(far_norm, near_norm)
            far_part, near_part = jnp.exp2(far_norm - top), jnp.exp2(near_norm - top)
            whole = 1.0 / (far_part + near_part)
            full_offset = (far_part * far_offset + near_part * later_offset) * whole
            later_chances = later_grown * (jnp.exp2(later_max - top) * whole)
            later_dscores = (later_chances * (later_dchances - full_offset)).astype(jnp.bfloat16)
            later_weights = later_chances.astype(jnp.bfloat16)
            key_grads[:, columns] = (
                score_scale * (product(dscores, query) + product(later_dscores, later_query))
            ).astype(jnp.bfloat16)
            value_grads[:, columns] = (
                product(weights, up) + product(later_weights, later_up)
            ).astype(jnp.bfloat16)

    return pl.pallas_call(
        kernel,
        out_shape=[bf16(block_rows, width)] * 4,
        in_specs=[VMEM] * 8 + [SMEM] + [VMEM] * sharers,
        out_specs=[VMEM] * 4,
        scratch_shapes=[pltpu.VMEM((block_rows, width), jnp.bfloat16)] * 3
        + [pltpu.VMEM(square, jnp.float32)] * 3,
        compiler_params=pltpu.CompilerParams(vmem_limit_bytes=40 * 2**20),
        name="window",
    )(keys, queries, values, upstream, first_got, second_got, next_upstream, next_stats, clip_lengths, *previous_values)


def on_device(queries, key_states, value_states, upstream, clip_lengths):
    sharers = lax.axis_size("head")
    steps = range(1, sharers)
    pairs, singles, first, second = cut_pieces(queries, key_states, value_states, upstream)
    pairs = [pairs[0]] + [partner_exchange(pairs[step], step) for step in steps]
    first_got, second_got = block_exchange(first, 0), block_exchange(second, 1)
    keys, query_rows, first, second = join_keys_queries(pairs)
    singles = [singles[0]] + [partner_exchange(singles[step], step) for step in steps]
    later_first, later_second = block_exchange(first, 0), block_exchange(second, 1)
    previous, next_upstream = cut_previous_values(first_got, second_got, sharers)
    previous = [previous[0]] + [partner_exchange(previous[step], step) for step in steps]
    values, stats = own_part(keys, query_rows, singles, upstream, clip_lengths)
    next_stats = to_previous(stats)
    return tuple(
        window(
            keys, query_rows, values, upstream, later_first, later_second,
            previous, next_upstream, next_stats, clip_lengths,
        )
    )


def solution(mesh):
    return jax.shard_map(
        on_device,
        mesh=mesh,
        in_specs=(
            P(("dp", "blk", "head"), None),
            P(("dp", "blk", "head"), None),
            P(("dp", "blk", "head"), None),
            P(("dp", "blk"), "head"),
            P("dp"),
        ),
        out_specs=(
            P(("dp", "blk"), "head"),
            P(("dp", "blk"), "head"),
            P(("dp", "blk"), "head"),
            P(("dp", "blk"), "head"),
        ),
        check_vma=False,
    )
```

time: 59.5 us -> 49.7 us (0.84)
  Pallas kernels: 0 us -> 13.3 us
  matrix products: 8.91 us -> 0 us
  waiting for transfers between devices: 20.9 us -> 14.1 us
  starting transfers between devices: 17.9 us -> 14.6 us
  local copies, waits for them, and re-layouts: 8.82 us -> 6.4 us
  other arithmetic: 1.41 us -> 0 us
    pallas_call x0 -> x5, Pallas kernels: none -> 13.3 us  [the longest x1 5.55 us: window(): pl.pallas_call(kernel, out_shape=[bf16(block_rows, width)] * 4, in_specs=...]
    all_to_all x3 -> x0, starting transfers between devices: 11.2 us -> none  [the longest x1 4.34 us: on_device(): lax.all_to_all(value_states, 'head', split_axis=1, concat_axis=0, tiled=T...]
    all_to_all x3 -> x0, waiting for transfers between devices: 9.82 us -> none  [the longest x1 5.91 us: on_device(): lax.all_to_all(key_states, 'head', split_axis=1, concat_axis=0, tiled=True)]
    dot_general x36 -> x0, matrix products: 8.91 us -> none  [the longest x4 1.46 us: head_neighbour(): jnp.einsum('qk,qe->ke', dscores, query_head, preferred_element_type=jnp.f...]
    ppermute x3 -> x14, starting transfers between devices: 6.72 us -> 14.6 us  [the longest x9 6.68 us: partner_exchange(): return lax.ppermute(rows, 'head', route)]
    all_to_all x3 -> x0, local copies, waits for them, and re-layouts: 3.12 us -> none  [the longest x1 1.67 us: on_device(): lax.all_to_all(value_states, 'head', split_axis=1, concat_axis=0, tiled=T...]
    ppermute x3 -> x14, waiting for transfers between devices: 11 us -> 14.1 us  [the longest x9 14 us: partner_exchange(): return lax.ppermute(rows, 'head', route)]
    unnamed x17 -> x32, local copies, waits for them, and re-layouts: 5.61 us -> 6.4 us
  transfers between devices with their start and end apart: 6 -> 14, of which waited for: 5 -> 7; matrix products, arithmetic and copies ran while one was open for 18% -> 0% of each run, Pallas kernels for 0% -> 10%
where the time goes in v1:
time: 49.7 us; the launch traced here: 49.2 us
  starting transfers between devices  14.6 us (29%)
  waiting for transfers between devices  14.1 us (28%)
  Pallas kernels  13.3 us (27%)
  local copies, waits for them, and re-layouts  6.4 us (13%)
  between operations  0.75 us (2%)
    ppermute x9, waiting for transfers between devices, partner_exchange(): return lax.ppermute(rows, 'head', route)  14 us
    ppermute x9, starting transfers between devices, partner_exchange(): return lax.ppermute(rows, 'head', route)  6.68 us
    ppermute x4, starting transfers between devices, block_exchange(): return lax.ppermute(rows, ('dp', 'blk'), route)  6.5 us
    unnamed x32, local copies, waits for them, and re-layouts  6.4 us
    pallas_call x1, Pallas kernels, window(): pl.pallas_call(kernel, out_shape=[bf16(block_rows, width)] * 4, in_specs=...  5.55 us
    pallas_call x1, Pallas kernels, cut_pieces(): pl.pallas_call(kernel, out_shape=[bf16(2 * rows, width)] * sharers + [bf1...  2.62 us
    pallas_call x1, Pallas kernels, join_keys_queries(): pl.pallas_call(kernel, out_shape=[bf16(block_rows, width)] * 4, in_specs=...  2.19 us
    pallas_call x1, Pallas kernels, cut_previous_values(): pl.pallas_call(kernel, out_shape=[bf16(rows, width)] * sharers + [bf16(bl...  1.87 us
  transfers between devices with their start and end apart: 14, of which 7 were waited for; matrix products, arithmetic and copies ran while one was open for 0% of the time, Pallas kernels for 10%

profile of v1, /device:TPU:0, one launch (start us, length us, event | category | flops | bytes accessed | tf_op | source)
XLA Modules:
  0.0 49.2 jit_solution(10693097396920445998)
XLA Ops:
  0.6 2.6 %cut_pieces.1 = (bf16[128,512]{1,0:T(8,128)(2,1)}, bf16[128,512]{1,0:T(8,128)(2,1)}, bf16[128,512]{1,0:T(8,128)(2,1)}, bf16[128,512]{1,0:T(8,128)(2,1)}, bf16[64...) custom-call(bf16[64,2048]{1,0:T(8,128)(2,1)} %q.1, ...), custom_call_target="tpu_custom_call" | custom-call | tf_op jit(solution)/shard_map/cut_pieces/pallas_call | solution.py:110
  3.3 0.5 %collective-permute-start = (bf16[128,512]{1,0:T(8,128)(2,1)}, bf16[128,512]{1,0:T(8,128)(2,1)S(1)}, u32[]{:S(2)}, u32[]{:S(2)}) collective-permute-start(bf16[128,512]{1,0:T(8,128)(2,1)} %get-tuple-element.26), channel_id=1, source_target_pairs={{0,1},{1,0},{2,3},{3,2},{4,5},{5,4},{6,7},{7,6},{8,9},{9,8},{10,11... | collective-permute-start | bytes 393224 | tf_op jit(solution)/shard_map/ppermute | solution.py:27
  3.8 2.6 %collective-permute-start.1 = (bf16[128,512]{1,0:T(8,128)(2,1)}, bf16[128,512]{1,0:T(8,128)(2,1)S(1)}, u32[]{:S(2)}, u32[]{:S(2)}) collective-permute-start(bf16[128,512]{1,0:T(8,128)(2,1)} %get-tuple-element.27), channel_id=1, source_target_pairs={{0,2},{1,3},{2,0},{3,1},{4,6},{5,7},{6,4},{7,5},{8,10},{9,11},{10,... | collective-permute-start | bytes 393224 | tf_op jit(solution)/shard_map/ppermute | solution.py:27
  6.3 0.1 collective-permute-start.2
  6.4 1.8 %collective-permute-start.8 = (bf16[256,512]{1,0:T(8,128)(2,1)}, bf16[256,512]{1,0:T(8,128)(2,1)S(1)}, u32[]{:S(2)}, u32[]{:S(2)}) collective-permute-start(bf16[256,512]{1,0:T(8,128)(2,1)} %get-tuple-element.38), channel_id=1, source_target_pairs={{0,4},{4,0},{8,12},{12,8},{16,20},{20,16},{24,28},{28,24},{1,5},{5... | collective-permute-start | bytes 786440 | tf_op jit(solution)/shard_map/ppermute | solution.py:40
  8.2 1.5 %collective-permute-start.9 = (bf16[256,512]{1,0:T(8,128)(2,1)}, bf16[256,512]{1,0:T(8,128)(2,1)S(1)}, u32[]{:S(2)}, u32[]{:S(2)}) collective-permute-start(bf16[256,512]{1,0:T(8,128)(2,1)} %get-tuple-element.39), channel_id=1, source_target_pairs={{0,16},{4,8},{8,4},{12,28},{16,0},{20,24},{24,20},{28,12},{1,17},{... | collective-permute-start | bytes 786440 | tf_op jit(solution)/shard_map/ppermute | solution.py:40
  9.7 0.0 collective-permute-done.refs_1_
  9.7 0.0 copy-start.11
  9.7 0.0 collective-permute-start.3
  9.8 1.1 %collective-permute-done.1.refs_2_ = bf16[128,512]{1,0:T(8,128)(2,1)S(1)} collective-permute-done((bf16[128,512]{1,0:T(8,128)(2,1)}, bf16[128,512]{1,0:T(8,128)(2,1)S(1)}, u32[]{:S(2)}, u32[]{:S(2)}) %collective-permute-start.1) | collective-permute-done | bytes 131104 | tf_op jit(solution)/shard_map/ppermute | solution.py:27
  10.9 0.0 copy-start.12
  10.9 2.3 %collective-permute-done.2.refs_3_ = bf16[128,512]{1,0:T(8,128)(2,1)S(1)} collective-permute-done((bf16[128,512]{1,0:T(8,128)(2,1)}, bf16[128,512]{1,0:T(8,128)(2,1)S(1)}, u32[]{:S(2)}, u32[]{:S(2)}) %collective-permute-start.2) | collective-permute-done | bytes 131104 | tf_op jit(solution)/shard_map/ppermute | solution.py:27
  13.2 0.0 copy-start.13
  13.2 0.0 copy-done.11
  13.2 0.0 copy-done.12
  13.2 0.6 %copy-done.13 = bf16[128,512]{1,0:T(8,128)(2,1)} copy-done((bf16[128,512]{1,0:T(8,128)(2,1)}, bf16[128,512]{1,0:T(8,128)(2,1)S(1)}, u32[]{:S(2)}) %copy-start.13) | copy-done | bytes 131096
  13.8 0.0 copy-start.15
  13.8 0.0 copy-start.14
  13.8 0.0 copy-start
  13.8 0.0 copy-start.7
  13.8 2.2 %join_keys_queries.1 = (bf16[256,512]{1,0:T(8,128)(2,1)}, bf16[256,512]{1,0:T(8,128)(2,1)}, bf16[256,512]{1,0:T(8,128)(2,1)}, bf16[256,512]{1,0:T(8,128)(2,1)}) custom-call(bf16[128,512]{1,0:T(8,128)(2,1)} %get-tuple-element.25.refs_0_, bf16[128,512]{1,0:T(8,128)(2,1)} %copy-done.11, bf16[128,512]{1,0:T(8,128)(2,1)} %copy-done.12, bf16[128,512]{1,0:T(8,128)(2,1)} %copy-done.13), custom_call_target="tpu_custom_call" | custom-call | tf_op jit(solution)/shard_map/join_keys_queries/pallas_call | solution.py:146
  16.0 1.7 %collective-permute-start.6 = (bf16[256,512]{1,0:T(8,128)(2,1)}, bf16[256,512]{1,0:T(8,128)(2,1)S(1)}, u32[]{:S(2)}, u32[]{:S(2)}) collective-permute-start(bf16[256,512]{1,0:T(8,128)(2,1)} %get-tuple-element.36), channel_id=1, source_target_pairs={{0,4},{4,0},{8,12},{12,8},{16,20},{20,16},{24,28},{28,24},{1,5},{5... | collective-permute-start | bytes 786440 | tf_op jit(solution)/shard_map/ppermute | solution.py:40
  17.7 1.5 %collective-permute-start.7 = (bf16[256,512]{1,0:T(8,128)(2,1)}, bf16[256,512]{1,0:T(8,128)(2,1)S(1)}, u32[]{:S(2)}, u32[]{:S(2)}) collective-permute-start(bf16[256,512]{1,0:T(8,128)(2,1)} %get-tuple-element.37), channel_id=1, source_target_pairs={{0,16},{4,8},{8,4},{12,28},{16,0},{20,24},{24,20},{28,12},{1,17},{... | collective-permute-start | bytes 786440 | tf_op jit(solution)/shard_map/ppermute | solution.py:40
  19.2 0.0 collective-permute-done.3.rest_1_
  19.2 0.0 copy-done.15
  19.2 1.5 %collective-permute-start.4 = (bf16[64,512]{1,0:T(8,128)(2,1)S(1)}, bf16[64,512]{1,0:T(8,128)(2,1)S(1)}, u32[]{:S(2)}, u32[]{:S(2)}) collective-permute-start(bf16[64,512]{1,0:T(8,128)(2,1)S(1)} %copy-done.15), channel_id=1, source_target_pairs={{0,2},{1,3},{2,0},{3,1},{4,6},{5,7},{6,4},{7,5},{8,10},{9,11},{10,... | collective-permute-start | bytes 196616 | tf_op jit(solution)/shard_map/ppermute | solution.py:27
  20.7 2.8 %collective-permute-done.4.rest_2_ = bf16[64,512]{1,0:T(8,128)(2,1)S(1)} collective-permute-done((bf16[64,512]{1,0:T(8,128)(2,1)S(1)}, bf16[64,512]{1,0:T(8,128)(2,1)S(1)}, u32[]{:S(2)}, u32[]{:S(2)}) %collective-permute-start.4) | collective-permute-done | bytes 65568 | tf_op jit(solution)/shard_map/ppermute | solution.py:27
  23.5 0.0 copy-done.14
  23.5 0.3 collective-permute-start.5
  23.7 4.1 %collective-permute-done.5.rest_3_ = bf16[64,512]{1,0:T(8,128)(2,1)S(1)} collective-permute-done((bf16[64,512]{1,0:T(8,128)(2,1)S(1)}, bf16[64,512]{1,0:T(8,128)(2,1)S(1)}, u32[]{:S(2)}, u32[]{:S(2)}) %collective-permute-start.5) | collective-permute-done | bytes 65568 | tf_op jit(solution)/shard_map/ppermute | solution.py:27
  27.8 0.0 copy-start.8
  27.8 0.0 copy-done
  27.8 0.0 copy-done.7
  27.8 0.6 %copy-done.8 = s32[4]{0:T(128)S(1)} copy-done((s32[4]{0:T(128)S(1)}, s32[4]{0:T(128)}, u32[]{:S(2)}) %copy-start.8) | copy-done | bytes 40
  28.5 0.0 copy-start.1
  28.5 0.9 %copy-done.1 = bf16[256,512]{1,0:T(8,128)(2,1)S(1)} copy-done((bf16[256,512]{1,0:T(8,128)(2,1)S(1)}, bf16[256,512]{1,0:T(8,128)(2,1)}, u32[]{:S(2)}) %copy-start.1) | copy-done | bytes 262168
  29.4 0.0 copy-start.3
  29.4 0.9 %copy-done.3 = bf16[256,512]{1,0:T(8,128)(2,1)S(1)} copy-done((bf16[256,512]{1,0:T(8,128)(2,1)S(1)}, bf16[256,512]{1,0:T(8,128)(2,1)}, u32[]{:S(2)}) %copy-start.3) | copy-done | bytes 262168
  30.4 1.1 %own_part.1 = (bf16[256,512]{1,0:T(8,128)(2,1)S(1)}, f32[8,256]{1,0:T(8,128)S(1)}) custom-call(bf16[256,512]{1,0:T(8,128)(2,1)S(1)} %copy-done.1, bf16[256,512]{1,0:T(8,128)(2,1)S(1)} %copy-done.3, bf16[256,512]{1,0:T(8,128)(2,1)S(1)} %copy-done, s32[4]{0:T(128)S(1)} %copy-done.8, bf16[64,512]{1,0:T(8,128)(2,1)S(1)} %copy-done.7, ...), custom_call_target="tpu_custom_call" | custom-call | tf_op jit(solution)/shard_map/own_part/pallas_call | solution.py:235
  31.5 0.0 copy-start.2
  31.5 0.0 copy-start.4
  31.5 1.4 %collective-permute-start.10 = (f32[8,256]{1,0:T(8,128)S(1)}, f32[8,256]{1,0:T(8,128)S(1)}, u32[]{:S(2)}, u32[]{:S(2)}) collective-permute-start(f32[8,256]{1,0:T(8,128)S(1)} %get-tuple-element.41), channel_id=1, source_target_pairs={{4,0},{8,4},{12,8},{5,1},{9,5},{13,9},{6,2},{10,6},{14,10},{7,3},{... | collective-permute-start | bytes 24584 | tf_op jit(solution)/shard_map/ppermute | solution.py:45
  32.9 0.0 collective-permute-done.8.first
  33.0 0.0 copy-start.9
  33.0 0.0 collective-permute-done.9.second
  33.0 0.7 %copy-done.9 = bf16[256,512]{1,0:T(8,128)(2,1)} copy-done((bf16[256,512]{1,0:T(8,128)(2,1)}, bf16[256,512]{1,0:T(8,128)(2,1)S(1)}, u32[]{:S(2)}) %copy-start.9) | copy-done | bytes 262168
  33.7 0.0 copy-start.10
  33.7 0.7 %copy-done.10 = bf16[256,512]{1,0:T(8,128)(2,1)} copy-done((bf16[256,512]{1,0:T(8,128)(2,1)}, bf16[256,512]{1,0:T(8,128)(2,1)S(1)}, u32[]{:S(2)}) %copy-start.10) | copy-done | bytes 262168
  34.4 1.9 %cut_previous_values.1 = (bf16[64,512]{1,0:T(8,128)(2,1)}, bf16[64,512]{1,0:T(8,128)(2,1)}, bf16[64,512]{1,0:T(8,128)(2,1)}, bf16[64,512]{1,0:T(8,128)(2,1)}, bf16[256,512]{1,0:T(8,128)(2,1)}) custom-call(bf16[256,512]{1,0:T(8,128)(2,1)} %copy-done.9, bf16[256,512]{1,0:T(8,128)(2,1)} %copy-done.10), custom_call_target="tpu_custom_call" | custom-call | tf_op jit(solution)/shard_map/cut_previous_values/pallas_call | solution.py:173
  36.2 0.1 collective-permute-start.11
  36.3 0.8 %collective-permute-start.12 = (bf16[64,512]{1,0:T(8,128)(2,1)}, bf16[64,512]{1,0:T(8,128)(2,1)S(1)}, u32[]{:S(2)}, u32[]{:S(2)}) collective-permute-start(bf16[64,512]{1,0:T(8,128)(2,1)} %get-tuple-element.44), channel_id=1, source_target_pairs={{0,2},{1,3},{2,0},{3,1},{4,6},{5,7},{6,4},{7,5},{8,10},{9,11},{10,... | collective-permute-start | bytes 196616 | tf_op jit(solution)/shard_map/ppermute | solution.py:27
  37.1 0.1 collective-permute-done.10.stats
  37.2 0.9 %collective-permute-start.13 = (bf16[64,512]{1,0:T(8,128)(2,1)}, bf16[64,512]{1,0:T(8,128)(2,1)S(1)}, u32[]{:S(2)}, u32[]{:S(2)}) collective-permute-start(bf16[64,512]{1,0:T(8,128)(2,1)} %get-tuple-element.45), channel_id=1, source_target_pairs={{0,3},{1,2},{2,1},{3,0},{4,7},{5,6},{6,5},{7,4},{8,11},{9,10},{10,... | collective-permute-start | bytes 196616 | tf_op jit(solution)/shard_map/ppermute | solution.py:27
  38.1 0.0 collective-permute-done.11.rest_1_
  38.1 3.4 %collective-permute-done.12.rest_2_ = bf16[64,512]{1,0:T(8,128)(2,1)S(1)} collective-permute-done((bf16[64,512]{1,0:T(8,128)(2,1)}, bf16[64,512]{1,0:T(8,128)(2,1)S(1)}, u32[]{:S(2)}, u32[]{:S(2)}) %collective-permute-start.12) | collective-permute-done | bytes 65568 | tf_op jit(solution)/shard_map/ppermute | solution.py:27
  41.5 0.3 collective-permute-done.13.rest_3_
  41.8 0.0 collective-permute-done.6.first
  41.8 0.0 collective-permute-done.7.second
  41.8 0.0 copy-done.2
  41.8 0.0 copy-done.4
  41.8 0.0 copy-start.5
  41.8 0.9 %copy-done.5 = bf16[256,512]{1,0:T(8,128)(2,1)S(1)} copy-done((bf16[256,512]{1,0:T(8,128)(2,1)S(1)}, bf16[256,512]{1,0:T(8,128)(2,1)}, u32[]{:S(2)}) %copy-start.5) | copy-done | bytes 262168
  42.8 0.8 %copy-done.6 = bf16[64,512]{1,0:T(8,128)(2,1)S(1)} copy-done((bf16[64,512]{1,0:T(8,128)(2,1)S(1)}, bf16[64,512]{1,0:T(8,128)(2,1)}, u32[]{:S(2)}) %copy-start.6) | copy-done | bytes 65560
  43.6 5.6 %window.1 = (bf16[256,512]{1,0:T(8,128)(2,1)}, bf16[256,512]{1,0:T(8,128)(2,1)}, bf16[256,512]{1,0:T(8,128)(2,1)}, bf16[256,512]{1,0:T(8,128)(2,1)}) custom-call(bf16[256,512]{1,0:T(8,128)(2,1)S(1)} %copy-done.2, bf16[256,512]{1,0:T(8,128)(2,1)S(1)} %copy-done.4, bf16[256,512]{1,0:T(8,128)(2,1)S(1)} %get-tuple-element.35.v, bf16[256,512]{1,0:T(8,128)(2,1)S(1)} %copy-done, ...), custom_call_target="tpu_custom_call" | custom-call | tf_op jit(solution)/shard_map/window/pallas_call | solution.py:335
  (1 shorter events, 0.0 us)
Async XLA Ops:
  3.3 6.5 %collective-permute-start = (bf16[128,512]{1,0:T(8,128)(2,1)}, bf16[128,512]{1,0:T(8,128)(2,1)S(1)}, u32[]{:S(2)}, u32[]{:S(2)}) collective-permute-start(bf16[128,512]{1,0:T(8,128)(2,1)} %get-tuple-element.26), channel_id=1, source_target_pairs={{0,1},{1,0},{2,3},{3,2},{4,5},{5,4},{6,7},{7,6},{8,9},{9,8},{10,11... | collective-permute-start | bytes 393224 | tf_op jit(solution)/shard_map/ppermute | solution.py:27
  3.8 7.1 %collective-permute-start.1 = (bf16[128,512]{1,0:T(8,128)(2,1)}, bf16[128,512]{1,0:T(8,128)(2,1)S(1)}, u32[]{:S(2)}, u32[]{:S(2)}) collective-permute-start(bf16[128,512]{1,0:T(8,128)(2,1)} %get-tuple-element.27), channel_id=1, source_target_pairs={{0,2},{1,3},{2,0},{3,1},{4,6},{5,7},{6,4},{7,5},{8,10},{9,11},{10,... | collective-permute-start | bytes 393224 | tf_op jit(solution)/shard_map/ppermute | solution.py:27
  6.3 6.8 %collective-permute-start.2 = (bf16[128,512]{1,0:T(8,128)(2,1)}, bf16[128,512]{1,0:T(8,128)(2,1)S(1)}, u32[]{:S(2)}, u32[]{:S(2)}) collective-permute-start(bf16[128,512]{1,0:T(8,128)(2,1)} %get-tuple-element.28), channel_id=1, source_target_pairs={{0,3},{1,2},{2,1},{3,0},{4,7},{5,6},{6,5},{7,4},{8,11},{9,10},{10,... | collective-permute-start | bytes 393224 | tf_op jit(solution)/shard_map/ppermute | solution.py:27
  6.4 26.5 %collective-permute-start.8 = (bf16[256,512]{1,0:T(8,128)(2,1)}, bf16[256,512]{1,0:T(8,128)(2,1)S(1)}, u32[]{:S(2)}, u32[]{:S(2)}) collective-permute-start(bf16[256,512]{1,0:T(8,128)(2,1)} %get-tuple-element.38), channel_id=1, source_target_pairs={{0,4},{4,0},{8,12},{12,8},{16,20},{20,16},{24,28},{28,24},{1,5},{5... | collective-permute-start | bytes 786440 | tf_op jit(solution)/shard_map/ppermute | solution.py:40
  8.2 24.7 %collective-permute-start.9 = (bf16[256,512]{1,0:T(8,128)(2,1)}, bf16[256,512]{1,0:T(8,128)(2,1)S(1)}, u32[]{:S(2)}, u32[]{:S(2)}) collective-permute-start(bf16[256,512]{1,0:T(8,128)(2,1)} %get-tuple-element.39), channel_id=1, source_target_pairs={{0,16},{4,8},{8,4},{12,28},{16,0},{20,24},{24,20},{28,12},{1,17},{... | collective-permute-start | bytes 786440 | tf_op jit(solution)/shard_map/ppermute | solution.py:40
  9.7 3.4 %copy-start.11 = (bf16[128,512]{1,0:T(8,128)(2,1)}, bf16[128,512]{1,0:T(8,128)(2,1)S(1)}, u32[]{:S(2)}) copy-start(bf16[128,512]{1,0:T(8,128)(2,1)S(1)} %collective-permute-done.refs_1_) | copy-start | bytes 393220
  9.7 9.5 %collective-permute-start.3 = (bf16[64,512]{1,0:T(8,128)(2,1)}, bf16[64,512]{1,0:T(8,128)(2,1)S(1)}, u32[]{:S(2)}, u32[]{:S(2)}) collective-permute-start(bf16[64,512]{1,0:T(8,128)(2,1)} %get-tuple-element.32), channel_id=1, source_target_pairs={{0,1},{1,0},{2,3},{3,2},{4,5},{5,4},{6,7},{7,6},{8,9},{9,8},{10,11... | collective-permute-start | bytes 196616 | tf_op jit(solution)/shard_map/ppermute | solution.py:27
  10.9 2.3 %copy-start.12 = (bf16[128,512]{1,0:T(8,128)(2,1)}, bf16[128,512]{1,0:T(8,128)(2,1)S(1)}, u32[]{:S(2)}) copy-start(bf16[128,512]{1,0:T(8,128)(2,1)S(1)} %collective-permute-done.1.refs_2_) | copy-start | bytes 393220
  13.2 0.6 %copy-start.13 = (bf16[128,512]{1,0:T(8,128)(2,1)}, bf16[128,512]{1,0:T(8,128)(2,1)S(1)}, u32[]{:S(2)}) copy-start(bf16[128,512]{1,0:T(8,128)(2,1)S(1)} %collective-permute-done.2.refs_3_) | copy-start | bytes 393220
  13.8 5.4 %copy-start.15 = (bf16[64,512]{1,0:T(8,128)(2,1)S(1)}, bf16[64,512]{1,0:T(8,128)(2,1)}, u32[]{:S(2)}) copy-start(bf16[64,512]{1,0:T(8,128)(2,1)} %get-tuple-element.33) | copy-start | bytes 196612
  13.8 9.6 %copy-start.14 = (bf16[64,512]{1,0:T(8,128)(2,1)S(1)}, bf16[64,512]{1,0:T(8,128)(2,1)}, u32[]{:S(2)}) copy-start(bf16[64,512]{1,0:T(8,128)(2,1)} %get-tuple-element.34) | copy-start | bytes 196612
  13.8 14.0 %copy-start = (bf16[256,512]{1,0:T(8,128)(2,1)S(1)}, bf16[256,512]{1,0:T(8,128)(2,1)}, u32[]{:S(2)}) copy-start(bf16[256,512]{1,0:T(8,128)(2,1)} %u.5) | copy-start | bytes 786436
  13.8 14.0 %copy-start.7 = (bf16[64,512]{1,0:T(8,128)(2,1)S(1)}, bf16[64,512]{1,0:T(8,128)(2,1)}, u32[]{:S(2)}) copy-start(bf16[64,512]{1,0:T(8,128)(2,1)} %get-tuple-element.31.rest_0_) | copy-start | bytes 196612
  16.0 25.8 %collective-permute-start.6 = (bf16[256,512]{1,0:T(8,128)(2,1)}, bf16[256,512]{1,0:T(8,128)(2,1)S(1)}, u32[]{:S(2)}, u32[]{:S(2)}) collective-permute-start(bf16[256,512]{1,0:T(8,128)(2,1)} %get-tuple-element.36), channel_id=1, source_target_pairs={{0,4},{4,0},{8,12},{12,8},{16,20},{20,16},{24,28},{28,24},{1,5},{5... | collective-permute-start | bytes 786440 | tf_op jit(solution)/shard_map/ppermute | solution.py:40
  17.7 24.1 %collective-permute-start.7 = (bf16[256,512]{1,0:T(8,128)(2,1)}, bf16[256,512]{1,0:T(8,128)(2,1)S(1)}, u32[]{:S(2)}, u32[]{:S(2)}) collective-permute-start(bf16[256,512]{1,0:T(8,128)(2,1)} %get-tuple-element.37), channel_id=1, source_target_pairs={{0,16},{4,8},{8,4},{12,28},{16,0},{20,24},{24,20},{28,12},{1,17},{... | collective-permute-start | bytes 786440 | tf_op jit(solution)/shard_map/ppermute | solution.py:40
  19.2 4.3 %collective-permute-start.4 = (bf16[64,512]{1,0:T(8,128)(2,1)S(1)}, bf16[64,512]{1,0:T(8,128)(2,1)S(1)}, u32[]{:S(2)}, u32[]{:S(2)}) collective-permute-start(bf16[64,512]{1,0:T(8,128)(2,1)S(1)} %copy-done.15), channel_id=1, source_target_pairs={{0,2},{1,3},{2,0},{3,1},{4,6},{5,7},{6,4},{7,5},{8,10},{9,11},{10,... | collective-permute-start | bytes 196616 | tf_op jit(solution)/shard_map/ppermute | solution.py:27
  23.5 4.3 %collective-permute-start.5 = (bf16[64,512]{1,0:T(8,128)(2,1)S(1)}, bf16[64,512]{1,0:T(8,128)(2,1)S(1)}, u32[]{:S(2)}, u32[]{:S(2)}) collective-permute-start(bf16[64,512]{1,0:T(8,128)(2,1)S(1)} %copy-done.14), channel_id=1, source_target_pairs={{0,3},{1,2},{2,1},{3,0},{4,7},{5,6},{6,5},{7,4},{8,11},{9,10},{10,... | collective-permute-start | bytes 196616 | tf_op jit(solution)/shard_map/ppermute | solution.py:27
  27.8 0.7 %copy-start.8 = (s32[4]{0:T(128)S(1)}, s32[4]{0:T(128)}, u32[]{:S(2)}) copy-start(s32[4]{0:T(128)} %lengths.3) | copy-start | bytes 52
  28.5 0.9 %copy-start.1 = (bf16[256,512]{1,0:T(8,128)(2,1)S(1)}, bf16[256,512]{1,0:T(8,128)(2,1)}, u32[]{:S(2)}) copy-start(bf16[256,512]{1,0:T(8,128)(2,1)} %get-tuple-element.29.k) | copy-start | bytes 786436
  29.4 0.9 %copy-start.3 = (bf16[256,512]{1,0:T(8,128)(2,1)S(1)}, bf16[256,512]{1,0:T(8,128)(2,1)}, u32[]{:S(2)}) copy-start(bf16[256,512]{1,0:T(8,128)(2,1)} %get-tuple-element.30.q) | copy-start | bytes 786436
  31.5 10.3 %copy-start.2 = (bf16[256,512]{1,0:T(8,128)(2,1)S(1)}, bf16[256,512]{1,0:T(8,128)(2,1)}, u32[]{:S(2)}) copy-start(bf16[256,512]{1,0:T(8,128)(2,1)} %get-tuple-element.29.k) | copy-start | bytes 786436
  31.5 10.3 %copy-start.4 = (bf16[256,512]{1,0:T(8,128)(2,1)S(1)}, bf16[256,512]{1,0:T(8,128)(2,1)}, u32[]{:S(2)}) copy-start(bf16[256,512]{1,0:T(8,128)(2,1)} %get-tuple-element.30.q) | copy-start | bytes 786436
  31.5 5.7 %collective-permute-start.10 = (f32[8,256]{1,0:T(8,128)S(1)}, f32[8,256]{1,0:T(8,128)S(1)}, u32[]{:S(2)}, u32[]{:S(2)}) collective-permute-start(f32[8,256]{1,0:T(8,128)S(1)} %get-tuple-element.41), channel_id=1, source_target_pairs={{4,0},{8,4},{12,8},{5,1},{9,5},{13,9},{6,2},{10,6},{14,10},{7,3},{... | collective-permute-start | bytes 24584 | tf_op jit(solution)/shard_map/ppermute | solution.py:45
  33.0 0.7 %copy-start.9 = (bf16[256,512]{1,0:T(8,128)(2,1)}, bf16[256,512]{1,0:T(8,128)(2,1)S(1)}, u32[]{:S(2)}) copy-start(bf16[256,512]{1,0:T(8,128)(2,1)S(1)} %collective-permute-done.8.first) | copy-start | bytes 786436
  33.7 0.7 %copy-start.10 = (bf16[256,512]{1,0:T(8,128)(2,1)}, bf16[256,512]{1,0:T(8,128)(2,1)S(1)}, u32[]{:S(2)}) copy-start(bf16[256,512]{1,0:T(8,128)(2,1)S(1)} %collective-permute-done.9.second) | copy-start | bytes 786436
  36.2 1.9 %collective-permute-start.11 = (bf16[64,512]{1,0:T(8,128)(2,1)}, bf16[64,512]{1,0:T(8,128)(2,1)S(1)}, u32[]{:S(2)}, u32[]{:S(2)}) collective-permute-start(bf16[64,512]{1,0:T(8,128)(2,1)} %get-tuple-element.43), channel_id=1, source_target_pairs={{0,1},{1,0},{2,3},{3,2},{4,5},{5,4},{6,7},{7,6},{8,9},{9,8},{10,11... | collective-permute-start | bytes 196616 | tf_op jit(solution)/shard_map/ppermute | solution.py:27
  36.3 5.1 %collective-permute-start.12 = (bf16[64,512]{1,0:T(8,128)(2,1)}, bf16[64,512]{1,0:T(8,128)(2,1)S(1)}, u32[]{:S(2)}, u32[]{:S(2)}) collective-permute-start(bf16[64,512]{1,0:T(8,128)(2,1)} %get-tuple-element.44), channel_id=1, source_target_pairs={{0,2},{1,3},{2,0},{3,1},{4,6},{5,7},{6,4},{7,5},{8,10},{9,11},{10,... | collective-permute-start | bytes 196616 | tf_op jit(solution)/shard_map/ppermute | solution.py:27
  37.2 4.6 %collective-permute-start.13 = (bf16[64,512]{1,0:T(8,128)(2,1)}, bf16[64,512]{1,0:T(8,128)(2,1)S(1)}, u32[]{:S(2)}, u32[]{:S(2)}) collective-permute-start(bf16[64,512]{1,0:T(8,128)(2,1)} %get-tuple-element.45), channel_id=1, source_target_pairs={{0,3},{1,2},{2,1},{3,0},{4,7},{5,6},{6,5},{7,4},{8,11},{9,10},{10,... | collective-permute-start | bytes 196616 | tf_op jit(solution)/shard_map/ppermute | solution.py:27
  41.8 1.0 %copy-start.5 = (bf16[256,512]{1,0:T(8,128)(2,1)S(1)}, bf16[256,512]{1,0:T(8,128)(2,1)}, u32[]{:S(2)}) copy-start(bf16[256,512]{1,0:T(8,128)(2,1)} %get-tuple-element.40.nu) | copy-start | bytes 786436
  42.8 0.8 %copy-start.6 = (bf16[64,512]{1,0:T(8,128)(2,1)S(1)}, bf16[64,512]{1,0:T(8,128)(2,1)}, u32[]{:S(2)}) copy-start(bf16[64,512]{1,0:T(8,128)(2,1)} %get-tuple-element.42.rest_0_) | copy-start | bytes 196612

commit v2 on v1

--- a/solution.py
+++ b/solution.py
@@ -54,15 +54,24 @@
     return pl.ds(pl.multiple_of(owner * size, size), size)
 
 
+def small_kernel():
+    return pltpu.CompilerParams(vmem_limit_bytes=4 * 2**20)
+
+
+def weighed(flops):
+    return pl.CostEstimate(flops=int(flops), bytes_accessed=0, transcendentals=0)
+
+
 def cut_pieces(queries, key_states, value_states, upstream):
     sharers = lax.axis_size("head")
     rows, features = queries.shape
     width = features // sharers
     block_rows = rows * sharers
+    heights = [(2 + sharers // 2) * rows if step < 2 else 2 * rows for step in range(sharers)]
 
     def kernel(q, k, v, u, *rest):
-        pairs, singles = rest[:sharers], rest[sharers : 2 * sharers]
-        first, second, sems = rest[2 * sharers :]
+        pieces = rest[:sharers]
+        first, second, sems = rest[sharers:]
         copies = []
 
         def copy(source, target):
@@ -70,9 +79,9 @@
 
         for step in range(sharers):
             columns = place(step, width)
-            copy(k.at[:, columns], pairs[step].at[pl.ds(0, rows)])
-            copy(q.at[:, columns], pairs[step].at[pl.ds(rows, rows)])
-            copy(v.at[:, columns], singles[step])
+            copy(k.at[:, columns], pieces[step].at[pl.ds(0, rows)])
+            copy(q.at[:, columns], pieces[step].at[pl.ds(rows, rows)])
+            copy(v.at[:, columns], pieces[step % 2].at[pl.ds((2 + step // 2) * rows, rows)])
 
         def swap(forward, backward):
             made = []
@@ -109,29 +118,49 @@
 
     out = pl.pallas_call(
         kernel,
-        out_shape=[bf16(2 * rows, width)] * sharers
-        + [bf16(rows, width)] * sharers
-        + [bf16(block_rows, width)] * 2,
+        out_shape=[bf16(height, width) for height in heights] + [bf16(block_rows, width)] * 2,
         in_specs=[ANY] * 4,
-        out_specs=[VMEM] * (2 * sharers + 2),
+        out_specs=[VMEM] * (sharers + 2),
         scratch_shapes=[pltpu.SemaphoreType.DMA((4 * sharers + 1,))],
+        compiler_params=pltpu.CompilerParams(vmem_limit_bytes=53 * 2**20),
         name="cut_pieces",
     )(queries, key_states, value_states, upstream)
-    return out[:sharers], out[sharers : 2 * sharers], out[2 * sharers], out[2 * sharers + 1]
-
-
-def join_keys_queries(pairs):
-    sharers = len(pairs)
-    rows, width = pairs[0].shape[0] // 2, pairs[0].shape[1]
+    return out[:sharers], out[sharers], out[sharers + 1]
+
+
+def stack_values(own, got, rows):
+    pairs = own.shape[0] // rows - 2
+    width = own.shape[1]
+
+    def kernel(mine, theirs, *out):
+        for pair in range(1, pairs):
+            where = pl.ds((2 + pair) * rows, rows)
+            out[pair - 1][pl.ds(0, rows), :] = mine[where, :]
+            out[pair - 1][pl.ds(rows, rows), :] = theirs[where, :]
+
+    return pl.pallas_call(
+        kernel,
+        out_shape=[bf16(2 * rows, width)] * (pairs - 1),
+        in_specs=[VMEM] * 2,
+        out_specs=[VMEM] * (pairs - 1),
+        compiler_params=small_kernel(),
+        cost_estimate=weighed(5e9),
+        name="stack_values",
+    )(own, got)
+
+
+def join_keys_queries(pieces, rows):
+    sharers = len(pieces)
+    width = pieces[0].shape[1]
     block_rows = rows * sharers
 
     def kernel(*refs):
-        pairs_in = refs[:sharers]
+        pieces_in = refs[:sharers]
         keys, queries, first, second = refs[sharers:]
         for step in range(sharers):
             where = place(step, rows)
-            keys[where, :] = pairs_in[step][pl.ds(0, rows), :]
-            queries[where, :] = pairs_in[step][pl.ds(rows, rows), :]
+            keys[where, :] = pieces_in[step][pl.ds(0, rows), :]
+            queries[where, :] = pieces_in[step][pl.ds(rows, rows), :]
 
         @pl.when(is_even())
         def _():
@@ -148,15 +177,18 @@
         out_shape=[bf16(block_rows, width)] * 4,
         in_specs=[VMEM] * sharers,
         out_specs=[VMEM] * 4,
+        compiler_params=small_kernel(),
+        cost_estimate=weighed(5e9),
         name="join_keys_queries",
-    )(*pairs)
-
-
-def cut_previous_values(first_got, second_got, sharers):
+    )(*pieces)
+
+
+def cut_previous_values(first_got, second_got, sharers, far):
     block_rows, width = first_got.shape
     rows = block_rows // sharers
 
     def kernel(first, second, *out):
+        out = out[len(far) :]
         def split(forward, backward):
             for step in range(sharers):
                 out[step][...] = forward[place(step, rows), :]
@@ -173,10 +205,12 @@
     out = pl.pallas_call(
         kernel,
         out_shape=[bf16(rows, width)] * sharers + [bf16(block_rows, width)],
-        in_specs=[VMEM] * 2,
+        in_specs=[VMEM] * (2 + len(far)),
         out_specs=[VMEM] * (sharers + 1),
+        compiler_params=small_kernel(),
+        cost_estimate=weighed(0),
         name="cut_previous_values",
-    )(first_got, second_got)
+    )(first_got, second_got, *far)
     return out[:sharers], out[sharers]
 
 
@@ -205,18 +239,20 @@
     return jnp.dot(a, b, preferred_element_type=jnp.float32)
 
 
-def own_part(keys, queries, singles, upstream, clip_lengths):
-    sharers = len(singles)
+def own_part(keys, queries, chip_values, far_values, upstream, clip_lengths):
+    sharers = 2 + 2 * len(far_values)
     block_rows, width = keys.shape
     rows = block_rows // sharers
     heads = width // HEAD_DIM
 
     def kernel(k, q, u, lengths, *rest):
-        singles_in = rest[:sharers]
-        values, stats, bias = rest[sharers:]
+        values_in = [ref.at[pl.ds(2 * rows, rows)] for ref in rest[:2]]
+        for ref in rest[2 : 1 + sharers // 2]:
+            values_in += [ref.at[pl.ds(0, rows)], ref.at[pl.ds(rows, rows)]]
+        values, stats, bias = rest[1 + sharers // 2 :]
         block, blocks = lax.axis_index("blk"), lax.axis_size("blk")
         for step in range(sharers):
-            values[place(step, rows), :] = singles_in[step][...]
+            values[place(step, rows), :] = values_in[step][...]
         bias[...] = mask_bias(
             clip_ids(lengths, (block_rows, 1), 0, block, blocks),
             clip_ids(lengths, (1, block_rows), 1, block, blocks),
@@ -235,53 +271,48 @@
     return pl.pallas_call(
         kernel,
         out_shape=[bf16(block_rows, width), jax.ShapeDtypeStruct((2 * heads, block_rows), jnp.float32)],
-        in_specs=[VMEM] * 3 + [SMEM] + [VMEM] * sharers,
+        in_specs=[VMEM] * 3 + [SMEM] + [VMEM] * (1 + sharers // 2),
         out_specs=[VMEM] * 2,
         scratch_shapes=[pltpu.VMEM((block_rows, block_rows), jnp.float32)],
-        compiler_params=pltpu.CompilerParams(vmem_limit_bytes=24 * 2**20),
+        compiler_params=pltpu.CompilerParams(vmem_limit_bytes=8 * 2**20),
+        cost_estimate=weighed(2e10),
         name="own_part",
-    )(keys, queries, upstream, clip_lengths, *singles)
-
-
-def window(keys, queries, values, upstream, first_got, second_got, previous_values, next_upstream, next_stats, clip_lengths):
+    )(keys, queries, upstream, clip_lengths, *chip_values, *far_values)
+
+
+def own_rows(keys, queries, values, upstream, first_got, second_got, previous_values, clip_lengths):
     sharers = len(previous_values)
     block_rows, width = keys.shape
     rows = block_rows // sharers
     heads = width // HEAD_DIM
     square = (block_rows, block_rows)
 
-    def kernel(k, q, v, u, first, second, nu, stats, lengths, *rest):
+    def kernel(k, q, v, u, first, second, lengths, *rest):
         pieces = rest[:sharers]
-        attended, query_grads, key_grads, value_grads = rest[sharers : sharers + 4]
-        pk, nq, pv, own_bias, previous_bias, next_bias = rest[sharers + 4 :]
+        attended, query_grads, key_part, value_part = rest[sharers : sharers + 4]
+        pk, pv, own_bias, previous_bias = rest[sharers + 4 :]
         block, blocks = lax.axis_index("blk"), lax.axis_size("blk")
 
         @pl.when(is_even())
         def _():
             pk[...] = second[...]
-            nq[...] = first[...]
 
         @pl.when(jnp.logical_not(is_even()))
         def _():
             pk[...] = first[...]
-            nq[...] = second[...]
 
         for step in range(sharers):
             pv[place(step, rows), :] = pieces[step][...]
 
         tall, wide = (block_rows, 1), (1, block_rows)
-        key_ids = clip_ids(lengths, tall, 0, block, blocks)
         query_ids = clip_ids(lengths, wide, 1, block, blocks)
-        own_bias[...] = mask_bias(key_ids, query_ids)
+        own_bias[...] = mask_bias(clip_ids(lengths, tall, 0, block, blocks), query_ids)
         previous_bias[...] = mask_bias(clip_ids(lengths, tall, 0, block - 1, blocks), query_ids)
-        next_bias[...] = mask_bias(key_ids, clip_ids(lengths, wide, 1, block + 1, blocks))
 
         for head in range(heads):
             columns = pl.ds(head * HEAD_DIM, HEAD_DIM)
             key, query, value, up = k[:, columns], q[:, columns], v[:, columns], u[:, columns]
             past_key, past_value = pk[:, columns], pv[:, columns]
-            later_query, later_up = nq[:, columns], nu[:, columns]
-
             scores = by_rows(key, query) * exp2_scale + own_bias[...]
             past_scores = by_rows(past_key, query) * exp2_scale + previous_bias[...]
             row_max = jnp.maximum(
@@ -309,60 +340,98 @@
             query_grads[:, columns] = (
                 score_scale * (by_columns(dscores, key) + by_columns(past_dscores, past_key))
             ).astype(jnp.bfloat16)
-
-            later_scores = by_rows(key, later_query) * exp2_scale + next_bias[...]
-            later_max = jnp.max(later_scores, axis=0, keepdims=True)
-            later_grown = jnp.exp2(later_scores - later_max)
-            later_total = jnp.sum(later_grown, axis=0, keepdims=True)
-            later_dchances = by_rows(value, later_up)
-            later_offset = jnp.sum(later_grown * later_dchances, axis=0, keepdims=True) / later_total
+            key_part[:, columns] = product(dscores, query)
+            value_part[:, columns] = product(weights, up)
+
+    return pl.pallas_call(
+        kernel,
+        out_shape=[bf16(block_rows, width)] * 2
+        + [jax.ShapeDtypeStruct((block_rows, width), jnp.float32)] * 2,
+        in_specs=[VMEM] * 6 + [SMEM] + [VMEM] * sharers,
+        out_specs=[VMEM] * 4,
+        scratch_shapes=[pltpu.VMEM((block_rows, width), jnp.bfloat16)] * 2
+        + [pltpu.VMEM(square, jnp.float32)] * 2,
+        compiler_params=pltpu.CompilerParams(vmem_limit_bytes=16 * 2**20),
+        name="own_rows",
+    )(keys, queries, values, upstream, first_got, second_got, clip_lengths, *previous_values)
+
+
+def next_rows(keys, values, first_got, second_got, next_upstream, next_stats, key_part, value_part, clip_lengths):
+    block_rows, width = keys.shape
+    heads = width // HEAD_DIM
+    square = (block_rows, block_rows)
+
+    def kernel(k, v, first, second, nu, stats, key_part, value_part, lengths, key_grads, value_grads, nq, bias):
+        block, blocks = lax.axis_index("blk"), lax.axis_size("blk")
+
+        @pl.when(is_even())
+        def _():
+            nq[...] = first[...]
+
+        @pl.when(jnp.logical_not(is_even()))
+        def _():
+            nq[...] = second[...]
+
+        bias[...] = mask_bias(
+            clip_ids(lengths, (block_rows, 1), 0, block, blocks),
+            clip_ids(lengths, (1, block_rows), 1, block + 1, blocks),
+        )
+        for head in range(heads):
+            columns = pl.ds(head * HEAD_DIM, HEAD_DIM)
+            key, value, query, up = k[:, columns], v[:, columns], nq[:, columns], nu[:, columns]
+            scores = by_rows(key, query) * exp2_scale + bias[...]
+            row_max = jnp.max(scores, axis=0, keepdims=True)
+            grown = jnp.exp2(scores - row_max)
+            total = jnp.sum(grown, axis=0, keepdims=True)
+            dchances = by_rows(value, up)
+            offset = jnp.sum(grown * dchances, axis=0, keepdims=True) / total
             far_norm, far_offset = stats[pl.ds(head, 1), :], stats[pl.ds(heads + head, 1), :]
-            near_norm = later_max + jnp.log2(later_total)
+            near_norm = row_max + jnp.log2(total)
             top = jnp.maximum(far_norm, near_norm)
             far_part, near_part = jnp.exp2(far_norm - top), jnp.exp2(near_norm - top)
             whole = 1.0 / (far_part + near_part)
-            full_offset = (far_part * far_offset + near_part * later_offset) * whole
-            later_chances = later_grown * (jnp.exp2(later_max - top) * whole)
-            later_dscores = (later_chances * (later_dchances - full_offset)).astype(jnp.bfloat16)
-            later_weights = later_chances.astype(jnp.bfloat16)
+            full_offset = (far_part * far_offset + near_part * offset) * whole
+            chances = grown * (jnp.exp2(row_max - top) * whole)
+            dscores = (chances * (dchances - full_offset)).astype(jnp.bfloat16)
+            weights = chances.astype(jnp.bfloat16)
             key_grads[:, columns] = (
-                score_scale * (product(dscores, query) + product(later_dscores, later_query))
+                score_scale * (key_part[:, columns] + product(dscores, query))
             ).astype(jnp.bfloat16)
-            value_grads[:, columns] = (
-                product(weights, up) + product(later_weights, later_up)
-            ).astype(jnp.bfloat16)
+            value_grads[:, columns] = (value_part[:, columns] + product(weights, up)).astype(jnp.bfloat16)
 
     return pl.pallas_call(
         kernel,
-        out_shape=[bf16(block_rows, width)] * 4,
-        in_specs=[VMEM] * 8 + [SMEM] + [VMEM] * sharers,
-        out_specs=[VMEM] * 4,
-        scratch_shapes=[pltpu.VMEM((block_rows, width), jnp.bfloat16)] * 3
-        + [pltpu.VMEM(square, jnp.float32)] * 3,
-        compiler_params=pltpu.CompilerParams(vmem_limit_bytes=40 * 2**20),
-        name="window",
-    )(keys, queries, values, upstream, first_got, second_got, next_upstream, next_stats, clip_lengths, *previous_values)
+        out_shape=[bf16(block_rows, width)] * 2,
+        in_specs=[VMEM] * 8 + [SMEM],
+        out_specs=[VMEM] * 2,
+        scratch_shapes=[pltpu.VMEM((block_rows, width), jnp.bfloat16), pltpu.VMEM(square, jnp.float32)],
+        compiler_params=pltpu.CompilerParams(vmem_limit_bytes=16 * 2**20),
+        name="next_rows",
+    )(keys, values, first_got, second_got, next_upstream, next_stats, key_part, value_part, clip_lengths)
 
 
 def on_device(queries, key_states, value_states, upstream, clip_lengths):
     sharers = lax.axis_size("head")
     steps = range(1, sharers)
-    pairs, singles, first, second = cut_pieces(queries, key_states, value_states, upstream)
-    pairs = [pairs[0]] + [partner_exchange(pairs[step], step) for step in steps]
+    rows = queries.shape[0]
+    pieces, first, second = cut_pieces(queries, key_states, value_states, upstream)
+    pieces = [pieces[0]] + [partner_exchange(pieces[step], step) for step in steps]
     first_got, second_got = block_exchange(first, 0), block_exchange(second, 1)
-    keys, query_rows, first, second = join_keys_queries(pairs)
-    singles = [singles[0]] + [partner_exchange(singles[step], step) for step in steps]
-    later_first, later_second = block_exchange(first, 0), block_exchange(second, 1)
-    previous, next_upstream = cut_previous_values(first_got, second_got, sharers)
+    stacked = stack_values(pieces[0], pieces[1], rows)
+    far_values = [partner_exchange(stack, 2 * pair + 2) for pair, stack in enumerate(stacked)]
+    keys, query_rows, first, second = join_keys_queries(pieces, rows)
+    previous, next_upstream = cut_previous_values(first_got, second_got, sharers, far_values)
+    first_got, second_got = block_exchange(first, 0), block_exchange(second, 1)
     previous = [previous[0]] + [partner_exchange(previous[step], step) for step in steps]
-    values, stats = own_part(keys, query_rows, singles, upstream, clip_lengths)
+    values, stats = own_part(keys, query_rows, pieces[:2], far_values, upstream, clip_lengths)
     next_stats = to_previous(stats)
-    return tuple(
-        window(
-            keys, query_rows, values, upstream, later_first, later_second,
-            previous, next_upstream, next_stats, clip_lengths,
-        )
+    attended, query_grads, key_part, value_part = own_rows(
+        keys, query_rows, values, upstream, first_got, second_got, previous, clip_lengths
     )
+    key_grads, value_grads = next_rows(
+        keys, values, first_got, second_got, next_upstream, next_stats, key_part, value_part, clip_lengths
+    )
+    return attended, query_grads, key_grads, value_grads
 
 
 def solution(mesh):

time: 49.7 us -> 30.8 us (0.62)
  waiting for transfers between devices: 14.1 us -> 4.01 us
  local copies, waits for them, and re-layouts: 6.4 us -> 0.66 us
  Pallas kernels: 13.3 us -> 10.8 us
    ppermute x9 -> x7, waiting for transfers between devices: 14 us -> 2.31 us  [partner_exchange(): return lax.ppermute(rows, 'head', route)]
    unnamed x32 -> x4, local copies, waits for them, and re-layouts: 6.4 us -> 0.66 us
    pallas_call x1, Pallas kernels: 2.19 us -> 0.08 us  [join_keys_queries(): pl.pallas_call(kernel, out_shape=[bf16(block_rows, width)] * 4, in_specs=...]
    pallas_call x1, Pallas kernels: 1.87 us -> 0.04 us  [cut_previous_values(): pl.pallas_call(kernel, out_shape=[bf16(rows, width)] * sharers + [bf16(bl...]
    ppermute x4, waiting for transfers between devices: 0.01 us -> 1.7 us  [block_exchange(): return lax.ppermute(rows, ('dp', 'blk'), route)]
    pallas_call x2 -> x4, Pallas kernels: 8.17 us -> 9.53 us  [the longest x1 4.05 us: own_rows(): pl.pallas_call(kernel, out_shape=[bf16(block_rows, width)] * 2 + [jax.Sha...]
    ppermute x9 -> x7, starting transfers between devices: 6.68 us -> 6.65 us  [partner_exchange(): return lax.ppermute(rows, 'head', route)]
  transfers between devices with their start and end apart: 14 -> 12, of which waited for: 7 -> 4; matrix products, arithmetic and copies ran while one was open for 0% -> 0% of each run, Pallas kernels for 10% -> 17%
where the time goes in v2:
time: 30.8 us; the launch traced here: 30.6 us
  starting transfers between devices  14.5 us (47%)
  Pallas kernels  10.8 us (35%)
  waiting for transfers between devices  4.01 us (13%)
  between operations  0.7 us (2%)
  local copies, waits for them, and re-layouts  0.66 us (2%)
    ppermute x7, starting transfers between devices, partner_exchange(): return lax.ppermute(rows, 'head', route)  6.65 us
    ppermute x4, starting transfers between devices, block_exchange(): return lax.ppermute(rows, ('dp', 'blk'), route)  6.57 us
    pallas_call x1, Pallas kernels, own_rows(): pl.pallas_call(kernel, out_shape=[bf16(block_rows, width)] * 2 + [jax.Sha...  4.05 us
    pallas_call x1, Pallas kernels, next_rows(): pl.pallas_call(kernel, out_shape=[bf16(block_rows, width)] * 2, in_specs=...  3.12 us
    pallas_call x1, Pallas kernels, cut_pieces(): pl.pallas_call(kernel, out_shape=[bf16(height, width) for height in heigh...  2.35 us
    ppermute x7, waiting for transfers between devices, partner_exchange(): return lax.ppermute(rows, 'head', route)  2.31 us
    ppermute x4, waiting for transfers between devices, block_exchange(): return lax.ppermute(rows, ('dp', 'blk'), route)  1.7 us
    ppermute x1, starting transfers between devices, to_previous(): return lax.ppermute(rows, 'blk', [(i, i - 1) for i in range(1, blocks)])  1.29 us
  transfers between devices with their start and end apart: 12, of which 4 were waited for; matrix products, arithmetic and copies ran while one was open for 0% of the time, Pallas kernels for 17%

profile of v2, /device:TPU:0, one launch (start us, length us, event | category | flops | bytes accessed | tf_op | source)
XLA Modules:
  0.0 30.6 jit_solution(5840139382717289789)
XLA Ops:
  0.6 2.4 %cut_pieces.1 = (bf16[256,512]{1,0:T(8,128)(2,1)S(1)}, bf16[256,512]{1,0:T(8,128)(2,1)S(1)}, bf16[128,512]{1,0:T(8,128)(2,1)S(1)}, bf16[128,512]{1,0:T(8,128)(2,...) custom-call(bf16[64,2048]{1,0:T(8,128)(2,1)} %q.1, bf16[64,2048]{1,0:T(8,128)(2,1)} %k.1, bf16[64,2048]{1,0:T(8,128)(2,1)} %v.1, ...), custom_call_target="tpu_custom_call" | custom-call | tf_op jit(solution)/shard_map/cut_pieces/pallas_call | solution.py:119
  3.0 0.5 %collective-permute-start = (bf16[256,512]{1,0:T(8,128)(2,1)S(1)}, bf16[256,512]{1,0:T(8,128)(2,1)S(1)}, u32[]{:S(2)}, u32[]{:S(2)}) collective-permute-start(bf16[256,512]{1,0:T(8,128)(2,1)S(1)} %get-tuple-element.28), channel_id=1, source_target_pairs={{0,1},{1,0},{2,3},{3,2},{4,5},{5,4},{6,7},{7,6},{8,9},{9,8},{10,11... | collective-permute-start | bytes 786440 | tf_op jit(solution)/shard_map/ppermute | solution.py:27
  3.5 2.6 %collective-permute-start.1 = (bf16[128,512]{1,0:T(8,128)(2,1)S(1)}, bf16[128,512]{1,0:T(8,128)(2,1)S(1)}, u32[]{:S(2)}, u32[]{:S(2)}) collective-permute-start(bf16[128,512]{1,0:T(8,128)(2,1)S(1)} %get-tuple-element.29), channel_id=1, source_target_pairs={{0,2},{1,3},{2,0},{3,1},{4,6},{5,7},{6,4},{7,5},{8,10},{9,11},{10,... | collective-permute-start | bytes 393224 | tf_op jit(solution)/shard_map/ppermute | solution.py:27
  6.1 0.1 collective-permute-start.2
  6.1 1.8 %collective-permute-start.6 = (bf16[256,512]{1,0:T(8,128)(2,1)}, bf16[256,512]{1,0:T(8,128)(2,1)S(1)}, u32[]{:S(2)}, u32[]{:S(2)}) collective-permute-start(bf16[256,512]{1,0:T(8,128)(2,1)} %get-tuple-element.36), channel_id=1, source_target_pairs={{0,4},{4,0},{8,12},{12,8},{16,20},{20,16},{24,28},{28,24},{1,5},{5... | collective-permute-start | bytes 786440 | tf_op jit(solution)/shard_map/ppermute | solution.py:40
  8.0 1.5 %collective-permute-start.7 = (bf16[256,512]{1,0:T(8,128)(2,1)}, bf16[256,512]{1,0:T(8,128)(2,1)S(1)}, u32[]{:S(2)}, u32[]{:S(2)}) collective-permute-start(bf16[256,512]{1,0:T(8,128)(2,1)} %get-tuple-element.37), channel_id=1, source_target_pairs={{0,16},{4,8},{8,4},{12,28},{16,0},{20,24},{24,20},{28,12},{1,17},{... | collective-permute-start | bytes 786440 | tf_op jit(solution)/shard_map/ppermute | solution.py:40
  9.5 0.0 collective-permute-done.refs_1_.theirs.rest_1_
  9.5 1.6 %collective-permute-start.3 = (bf16[128,512]{1,0:T(8,128)(2,1)S(1)}, bf16[128,512]{1,0:T(8,128)(2,1)S(1)}, u32[]{:S(2)}, u32[]{:S(2)}) collective-permute-start(bf16[128,512]{1,0:T(8,128)(2,1)S(1)} %stack_values.1), channel_id=1, source_target_pairs={{0,2},{1,3},{2,0},{3,1},{4,6},{5,7},{6,4},{7,5},{8,10},{9,11},{10,... | collective-permute-start | bytes 393224 | tf_op jit(solution)/shard_map/ppermute | solution.py:27
  11.1 0.0 collective-permute-done.1.refs_2_
  11.1 1.7 %collective-permute-done.2.refs_3_ = bf16[128,512]{1,0:T(8,128)(2,1)S(1)} collective-permute-done((bf16[128,512]{1,0:T(8,128)(2,1)S(1)}, bf16[128,512]{1,0:T(8,128)(2,1)S(1)}, u32[]{:S(2)}, u32[]{:S(2)}) %collective-permute-start.2) | collective-permute-done | bytes 131104 | tf_op jit(solution)/shard_map/ppermute | solution.py:27
  12.7 0.1 join_keys_queries.1
  12.8 1.7 %collective-permute-start.4 = (bf16[256,512]{1,0:T(8,128)(2,1)S(1)}, bf16[256,512]{1,0:T(8,128)(2,1)S(1)}, u32[]{:S(2)}, u32[]{:S(2)}) collective-permute-start(bf16[256,512]{1,0:T(8,128)(2,1)S(1)} %get-tuple-element.34), channel_id=1, source_target_pairs={{0,4},{4,0},{8,12},{12,8},{16,20},{20,16},{24,28},{28,24},{1,5},{5... | collective-permute-start | bytes 786440 | tf_op jit(solution)/shard_map/ppermute | solution.py:40
  14.5 0.0 copy-start
  14.5 1.5 %collective-permute-start.5 = (bf16[256,512]{1,0:T(8,128)(2,1)S(1)}, bf16[256,512]{1,0:T(8,128)(2,1)S(1)}, u32[]{:S(2)}, u32[]{:S(2)}) collective-permute-start(bf16[256,512]{1,0:T(8,128)(2,1)S(1)} %get-tuple-element.35), channel_id=1, source_target_pairs={{0,16},{4,8},{8,4},{12,28},{16,0},{20,24},{24,20},{28,12},{1,17},{... | collective-permute-start | bytes 786440 | tf_op jit(solution)/shard_map/ppermute | solution.py:40
  16.0 0.0 collective-permute-done.6.first
  16.0 0.4 %collective-permute-done.7.second = bf16[256,512]{1,0:T(8,128)(2,1)S(1)} collective-permute-done((bf16[256,512]{1,0:T(8,128)(2,1)}, bf16[256,512]{1,0:T(8,128)(2,1)S(1)}, u32[]{:S(2)}, u32[]{:S(2)}) %collective-permute-start.7) | collective-permute-done | bytes 262176 | tf_op jit(solution)/shard_map/ppermute | solution.py:40
  16.4 0.0 collective-permute-done.3.rest_2_.out_0_
  16.5 0.1 collective-permute-start.8
  16.6 1.5 %collective-permute-start.9 = (bf16[64,512]{1,0:T(8,128)(2,1)S(1)}, bf16[64,512]{1,0:T(8,128)(2,1)S(1)}, u32[]{:S(2)}, u32[]{:S(2)}) collective-permute-start(bf16[64,512]{1,0:T(8,128)(2,1)S(1)} %get-tuple-element.40), channel_id=1, source_target_pairs={{0,2},{1,3},{2,0},{3,1},{4,6},{5,7},{6,4},{7,5},{8,10},{9,11},{10,... | collective-permute-start | bytes 196616 | tf_op jit(solution)/shard_map/ppermute | solution.py:27
  18.1 0.3 collective-permute-start.10
  18.4 0.0 copy-start.1
  18.4 0.0 copy-done
  18.4 0.7 %copy-done.1 = s32[4]{0:T(128)S(1)} copy-done((s32[4]{0:T(128)S(1)}, s32[4]{0:T(128)}, u32[]{:S(2)}) %copy-start.1) | copy-done | bytes 40
  19.1 1.1 %own_part.1 = (bf16[256,512]{1,0:T(8,128)(2,1)S(1)}, f32[8,256]{1,0:T(8,128)S(1)}) custom-call(bf16[256,512]{1,0:T(8,128)(2,1)S(1)} %get-tuple-element.31.k, bf16[256,512]{1,0:T(8,128)(2,1)S(1)} %get-tuple-element.32.q, bf16[256,512]{1,0:T(8,128)(2,1)S(1)} %copy-done, s32[4]{0:T(128)S(1)} %copy-done.1, ...), custom_call_target="tpu_custom_call" | custom-call | flops 20000000000 | tf_op jit(solution)/shard_map/own_part/pallas_call | solution.py:271
  20.2 0.0 collective-permute-done.8.rest_1_
  20.2 1.3 %collective-permute-start.11 = (f32[8,256]{1,0:T(8,128)S(1)}, f32[8,256]{1,0:T(8,128)S(1)}, u32[]{:S(2)}, u32[]{:S(2)}) collective-permute-start(f32[8,256]{1,0:T(8,128)S(1)} %get-tuple-element.45), channel_id=1, source_target_pairs={{4,0},{8,4},{12,8},{5,1},{9,5},{13,9},{6,2},{10,6},{14,10},{7,3},{... | collective-permute-start | bytes 24584 | tf_op jit(solution)/shard_map/ppermute | solution.py:45
  21.5 0.0 collective-permute-done.9.rest_2_
  21.5 0.6 %collective-permute-done.10.rest_3_ = bf16[64,512]{1,0:T(8,128)(2,1)S(1)} collective-permute-done((bf16[64,512]{1,0:T(8,128)(2,1)S(1)}, bf16[64,512]{1,0:T(8,128)(2,1)S(1)}, u32[]{:S(2)}, u32[]{:S(2)}) %collective-permute-start.10) | collective-permute-done | bytes 65568 | tf_op jit(solution)/shard_map/ppermute | solution.py:27
  22.2 0.0 collective-permute-done.4.first
  22.2 1.3 %collective-permute-done.5.second = bf16[256,512]{1,0:T(8,128)(2,1)S(1)} collective-permute-done((bf16[256,512]{1,0:T(8,128)(2,1)S(1)}, bf16[256,512]{1,0:T(8,128)(2,1)S(1)}, u32[]{:S(2)}, u32[]{:S(2)}) %collective-permute-start.5) | collective-permute-done | bytes 262176 | tf_op jit(solution)/shard_map/ppermute | solution.py:40
  23.5 4.0 %own_rows.1 = (bf16[256,512]{1,0:T(8,128)(2,1)}, bf16[256,512]{1,0:T(8,128)(2,1)}, f32[256,512]{1,0:T(8,128)S(1)}, f32[256,512]{1,0:T(8,128)S(1)}) custom-call(bf16[256,512]{1,0:T(8,128)(2,1)S(1)} %get-tuple-element.31.k, bf16[256,512]{1,0:T(8,128)(2,1)S(1)} %get-tuple-element.32.q, bf16[256,512]{1,0:T(8,128)(2,1)S(1)} %get-tuple-element.33.v, ...), custom_call_target="tpu_custom_call" | custom-call | tf_op jit(solution)/shard_map/own_rows/pallas_call | solution.py:346
  27.5 0.0 collective-permute-done.11.stats
  27.5 3.1 %next_rows.1 = (bf16[256,512]{1,0:T(8,128)(2,1)}, bf16[256,512]{1,0:T(8,128)(2,1)}) custom-call(bf16[256,512]{1,0:T(8,128)(2,1)S(1)} %get-tuple-element.31.k, bf16[256,512]{1,0:T(8,128)(2,1)S(1)} %get-tuple-element.33.v, bf16[256,512]{1,0:T(8,128)(2,1)S(1)} %collective-permute-done.4.first, bf16[256,512]{1,0:T(8,128)(2,1)S(1)} %collective-permute-done.5.second, ...), custom_call_target="tpu_custom_call" | custom-call | tf_op jit(solution)/shard_map/next_rows/pallas_call | solution.py:402
  (2 shorter events, 0.0 us)
Async XLA Ops:
  3.0 6.5 %collective-permute-start = (bf16[256,512]{1,0:T(8,128)(2,1)S(1)}, bf16[256,512]{1,0:T(8,128)(2,1)S(1)}, u32[]{:S(2)}, u32[]{:S(2)}) collective-permute-start(bf16[256,512]{1,0:T(8,128)(2,1)S(1)} %get-tuple-element.28), channel_id=1, source_target_pairs={{0,1},{1,0},{2,3},{3,2},{4,5},{5,4},{6,7},{7,6},{8,9},{9,8},{10,11... | collective-permute-start | bytes 786440 | tf_op jit(solution)/shard_map/ppermute | solution.py:27
  3.5 7.5 %collective-permute-start.1 = (bf16[128,512]{1,0:T(8,128)(2,1)S(1)}, bf16[128,512]{1,0:T(8,128)(2,1)S(1)}, u32[]{:S(2)}, u32[]{:S(2)}) collective-permute-start(bf16[128,512]{1,0:T(8,128)(2,1)S(1)} %get-tuple-element.29), channel_id=1, source_target_pairs={{0,2},{1,3},{2,0},{3,1},{4,6},{5,7},{6,4},{7,5},{8,10},{9,11},{10,... | collective-permute-start | bytes 393224 | tf_op jit(solution)/shard_map/ppermute | solution.py:27
  6.1 6.6 %collective-permute-start.2 = (bf16[128,512]{1,0:T(8,128)(2,1)S(1)}, bf16[128,512]{1,0:T(8,128)(2,1)S(1)}, u32[]{:S(2)}, u32[]{:S(2)}) collective-permute-start(bf16[128,512]{1,0:T(8,128)(2,1)S(1)} %get-tuple-element.30), channel_id=1, source_target_pairs={{0,3},{1,2},{2,1},{3,0},{4,7},{5,6},{6,5},{7,4},{8,11},{9,10},{10,... | collective-permute-start | bytes 393224 | tf_op jit(solution)/shard_map/ppermute | solution.py:27
  6.1 9.9 %collective-permute-start.6 = (bf16[256,512]{1,0:T(8,128)(2,1)}, bf16[256,512]{1,0:T(8,128)(2,1)S(1)}, u32[]{:S(2)}, u32[]{:S(2)}) collective-permute-start(bf16[256,512]{1,0:T(8,128)(2,1)} %get-tuple-element.36), channel_id=1, source_target_pairs={{0,4},{4,0},{8,12},{12,8},{16,20},{20,16},{24,28},{28,24},{1,5},{5... | collective-permute-start | bytes 786440 | tf_op jit(solution)/shard_map/ppermute | solution.py:40
  8.0 8.5 %collective-permute-start.7 = (bf16[256,512]{1,0:T(8,128)(2,1)}, bf16[256,512]{1,0:T(8,128)(2,1)S(1)}, u32[]{:S(2)}, u32[]{:S(2)}) collective-permute-start(bf16[256,512]{1,0:T(8,128)(2,1)} %get-tuple-element.37), channel_id=1, source_target_pairs={{0,16},{4,8},{8,4},{12,28},{16,0},{20,24},{24,20},{28,12},{1,17},{... | collective-permute-start | bytes 786440 | tf_op jit(solution)/shard_map/ppermute | solution.py:40
  9.5 7.0 %collective-permute-start.3 = (bf16[128,512]{1,0:T(8,128)(2,1)S(1)}, bf16[128,512]{1,0:T(8,128)(2,1)S(1)}, u32[]{:S(2)}, u32[]{:S(2)}) collective-permute-start(bf16[128,512]{1,0:T(8,128)(2,1)S(1)} %stack_values.1), channel_id=1, source_target_pairs={{0,2},{1,3},{2,0},{3,1},{4,6},{5,7},{6,4},{7,5},{8,10},{9,11},{10,... | collective-permute-start | bytes 393224 | tf_op jit(solution)/shard_map/ppermute | solution.py:27
  12.8 9.4 %collective-permute-start.4 = (bf16[256,512]{1,0:T(8,128)(2,1)S(1)}, bf16[256,512]{1,0:T(8,128)(2,1)S(1)}, u32[]{:S(2)}, u32[]{:S(2)}) collective-permute-start(bf16[256,512]{1,0:T(8,128)(2,1)S(1)} %get-tuple-element.34), channel_id=1, source_target_pairs={{0,4},{4,0},{8,12},{12,8},{16,20},{20,16},{24,28},{28,24},{1,5},{5... | collective-permute-start | bytes 786440 | tf_op jit(solution)/shard_map/ppermute | solution.py:40
  14.5 3.9 %copy-start = (bf16[256,512]{1,0:T(8,128)(2,1)S(1)}, bf16[256,512]{1,0:T(8,128)(2,1)}, u32[]{:S(2)}) copy-start(bf16[256,512]{1,0:T(8,128)(2,1)} %u.5) | copy-start | bytes 786436
  14.5 9.0 %collective-permute-start.5 = (bf16[256,512]{1,0:T(8,128)(2,1)S(1)}, bf16[256,512]{1,0:T(8,128)(2,1)S(1)}, u32[]{:S(2)}, u32[]{:S(2)}) collective-permute-start(bf16[256,512]{1,0:T(8,128)(2,1)S(1)} %get-tuple-element.35), channel_id=1, source_target_pairs={{0,16},{4,8},{8,4},{12,28},{16,0},{20,24},{24,20},{28,12},{1,17},{... | collective-permute-start | bytes 786440 | tf_op jit(solution)/shard_map/ppermute | solution.py:40
  16.5 3.7 %collective-permute-start.8 = (bf16[64,512]{1,0:T(8,128)(2,1)S(1)}, bf16[64,512]{1,0:T(8,128)(2,1)S(1)}, u32[]{:S(2)}, u32[]{:S(2)}) collective-permute-start(bf16[64,512]{1,0:T(8,128)(2,1)S(1)} %get-tuple-element.39), channel_id=1, source_target_pairs={{0,1},{1,0},{2,3},{3,2},{4,5},{5,4},{6,7},{7,6},{8,9},{9,8},{10,11... | collective-permute-start | bytes 196616 | tf_op jit(solution)/shard_map/ppermute | solution.py:27
  16.6 4.9 %collective-permute-start.9 = (bf16[64,512]{1,0:T(8,128)(2,1)S(1)}, bf16[64,512]{1,0:T(8,128)(2,1)S(1)}, u32[]{:S(2)}, u32[]{:S(2)}) collective-permute-start(bf16[64,512]{1,0:T(8,128)(2,1)S(1)} %get-tuple-element.40), channel_id=1, source_target_pairs={{0,2},{1,3},{2,0},{3,1},{4,6},{5,7},{6,4},{7,5},{8,10},{9,11},{10,... | collective-permute-start | bytes 196616 | tf_op jit(solution)/shard_map/ppermute | solution.py:27
  18.1 4.0 %collective-permute-start.10 = (bf16[64,512]{1,0:T(8,128)(2,1)S(1)}, bf16[64,512]{1,0:T(8,128)(2,1)S(1)}, u32[]{:S(2)}, u32[]{:S(2)}) collective-permute-start(bf16[64,512]{1,0:T(8,128)(2,1)S(1)} %get-tuple-element.41), channel_id=1, source_target_pairs={{0,3},{1,2},{2,1},{3,0},{4,7},{5,6},{6,5},{7,4},{8,11},{9,10},{10,... | collective-permute-start | bytes 196616 | tf_op jit(solution)/shard_map/ppermute | solution.py:27
  18.4 0.7 %copy-start.1 = (s32[4]{0:T(128)S(1)}, s32[4]{0:T(128)}, u32[]{:S(2)}) copy-start(s32[4]{0:T(128)} %lengths.5) | copy-start | bytes 52
  20.2 7.3 %collective-permute-start.11 = (f32[8,256]{1,0:T(8,128)S(1)}, f32[8,256]{1,0:T(8,128)S(1)}, u32[]{:S(2)}, u32[]{:S(2)}) collective-permute-start(f32[8,256]{1,0:T(8,128)S(1)} %get-tuple-element.45), channel_id=1, source_target_pairs={{4,0},{8,4},{12,8},{5,1},{9,5},{13,9},{6,2},{10,6},{14,10},{7,3},{... | collective-permute-start | bytes 24584 | tf_op jit(solution)/shard_map/ppermute | solution.py:45

commit v3 on v2

v3 whole, which is shorter than its diff:
```python
import math

import jax
import jax.numpy as jnp
from jax import lax
from jax.experimental import pallas as pl
from jax.experimental.pallas import tpu as pltpu
from jax.sharding import PartitionSpec as P

HEAD_DIM = 128

masked_fill = -1e30
score_scale = HEAD_DIM ** (-0.5)
exp2_scale = score_scale * math.log2(math.e)

VMEM = pl.BlockSpec(memory_space=pltpu.VMEM)
SMEM = pl.BlockSpec(memory_space=pltpu.SMEM)
ANY = pl.BlockSpec(memory_space=pl.ANY)


def bf16(*shape):
    return jax.ShapeDtypeStruct(shape, jnp.bfloat16)


def partner_exchange(rows, step):
    route = [(i, i ^ step) for i in range(lax.axis_size("head"))]
    return lax.ppermute(rows, "head", route)


def block_exchange(rows, parity):
    parts, blocks = lax.axis_size("dp"), lax.axis_size("blk")
    route = []
    for part in range(parts):
        for block in range(blocks):
            other = block + 1 if block % 2 == parity else block - 1
            if 0 <= other < blocks:
                route.append((part * blocks + block, part * blocks + other))
            elif part ^ 1 < parts:
                route.append((part * blocks + block, (part ^ 1) * blocks + block))
    return lax.ppermute(rows, ("dp", "blk"), route)


def to_previous(rows):
    blocks = lax.axis_size("blk")
    return lax.ppermute(rows, "blk", [(i, i - 1) for i in range(1, blocks)])


def is_even():
    return lax.rem(lax.axis_index("blk"), 2) == 0


def place(step, size):
    owner = jnp.bitwise_xor(lax.axis_index("head"), step)
    return pl.ds(pl.multiple_of(owner * size, size), size)


def small_kernel():
    return pltpu.CompilerParams(vmem_limit_bytes=4 * 2**20)


def weighed(flops):
    return pl.CostEstimate(flops=int(flops), bytes_accessed=0, transcendentals=0)


def cut_pieces(queries, key_states, value_states):
    sharers = lax.axis_size("head")
    rows, features = queries.shape
    width = features // sharers
    heights = [(2 + sharers // 2) * rows if step < 2 else 2 * rows for step in range(sharers)]

    def kernel(q, k, v, *rest):
        pieces, sems = rest[:sharers], rest[sharers]
        copies = []

        def copy(source, target):
            copies.append(pltpu.make_async_copy(source, target, sems.at[len(copies)]))

        for step in range(sharers):
            columns = place(step, width)
            copy(k.at[:, columns], pieces[step].at[pl.ds(0, rows)])
            copy(q.at[:, columns], pieces[step].at[pl.ds(rows, rows)])
            copy(v.at[:, columns], pieces[step % 2].at[pl.ds((2 + step // 2) * rows, rows)])
        for c in copies:
            c.start()
        for c in copies:
            c.wait()

    return pl.pallas_call(
        kernel,
        out_shape=[bf16(height, width) for height in heights],
        in_specs=[ANY] * 3,
        out_specs=[VMEM] * sharers,
        scratch_shapes=[pltpu.SemaphoreType.DMA((3 * sharers,))],
        compiler_params=pltpu.CompilerParams(vmem_limit_bytes=53 * 2**20),
        name="cut_pieces",
    )(queries, key_states, value_states)


def stack_values(own, got, upstream, rows):
    pairs = own.shape[0] // rows - 2
    width = own.shape[1]
    block_rows = upstream.shape[0]

    def kernel(mine, theirs, u, *out):
        first, second = out[pairs - 1 :]

        def stack(target, pair, start):
            where = pl.ds((2 + pair) * rows, rows)
            target[pl.ds(start, rows), :] = mine[where, :]
            target[pl.ds(start + rows, rows), :] = theirs[where, :]

        for pair in range(1, pairs):
            stack(out[pair - 1], pair, 0)

        def spread(forward, backward):
            for pair in range(pairs):
                stack(forward, pair, 2 * rows * pair)
            backward[...] = u[...]

        @pl.when(is_even())
        def _():
            spread(first, second)

        @pl.when(jnp.logical_not(is_even()))
        def _():
            spread(second, first)

    out = pl.pallas_call(
        kernel,
        out_shape=[bf16(2 * rows, width)] * (pairs - 1) + [bf16(block_rows, width)] * 2,
        in_specs=[VMEM] * 3,
        out_specs=[VMEM] * (pairs + 1),
        compiler_params=small_kernel(),
        cost_estimate=weighed(5e9),
        name="stack_values",
    )(own, got, upstream)
    return out[: pairs - 1], out[-2], out[-1]


def join_keys_queries(pieces, rows):
    sharers = len(pieces)
    width = pieces[0].shape[1]
    block_rows = rows * sharers

    def kernel(*refs):
        pieces_in = refs[:sharers]
        keys, queries, first, second = refs[sharers:]
        for step in range(sharers):
            where = place(step, rows)
            keys[where, :] = pieces_in[step][pl.ds(0, rows), :]
            queries[where, :] = pieces_in[step][pl.ds(rows, rows), :]

        @pl.when(is_even())
        def _():
            first[...] = keys[...]
            second[...] = queries[...]

        @pl.when(jnp.logical_not(is_even()))
        def _():
            first[...] = queries[...]
            second[...] = keys[...]

    return pl.pallas_call(
        kernel,
        out_shape=[bf16(block_rows, width)] * 4,
        in_specs=[VMEM] * sharers,
        out_specs=[VMEM] * 4,
        compiler_params=small_kernel(),
        cost_estimate=weighed(5e9),
        name="join_keys_queries",
    )(*pieces)


def cut_previous_values(first_got, second_got, pairs, far):
    block_rows, width = first_got.shape
    rows = block_rows // pairs

    def kernel(first, second, *out):
        out = out[len(far) :]

        def split(forward, backward):
            for pair in range(pairs):
                out[pair][...] = forward[pl.ds(pair * rows, rows), :]
            out[pairs][...] = backward[...]

        @pl.when(is_even())
        def _():
            split(second, first)

        @pl.when(jnp.logical_not(is_even()))
        def _():
            split(first, second)

    out = pl.pallas_call(
        kernel,
        out_shape=[bf16(rows, width)] * pairs + [bf16(block_rows, width)],
        in_specs=[VMEM] * (2 + len(far)),
        out_specs=[VMEM] * (pairs + 1),
        compiler_params=small_kernel(),
        cost_estimate=weighed(0),
        name="cut_previous_values",
    )(first_got, second_got, *far)
    return out[:pairs], out[pairs]


def clip_ids(lengths, shape, axis, block, blocks):
    position = block * shape[axis] + lax.broadcasted_iota(jnp.int32, shape, axis)
    ids, end = jnp.zeros(shape, jnp.int32), jnp.int32(0)
    for clip in range(lengths.shape[0]):
        end = end + lengths[clip]
        ids = ids + (position >= end).astype(jnp.int32)
    return jnp.where(jnp.logical_and(block >= 0, block < blocks), ids, -1)


def mask_bias(key_ids, query_ids):
    return jnp.where(key_ids == query_ids, 0.0, masked_fill).astype(jnp.float32)


def by_rows(a, b):
    return lax.dot_general(a, b, (((1,), (1,)), ((), ())), preferred_element_type=jnp.float32)


def by_columns(a, b):
    return lax.dot_general(a, b, (((0,), (0,)), ((), ())), preferred_element_type=jnp.float32)


def product(a, b):
    return jnp.dot(a, b, preferred_element_type=jnp.float32)


def masks(clip_lengths, block_rows):
    square = jax.ShapeDtypeStruct((block_rows, block_rows), jnp.float32)

    def kernel(lengths, own, past, ahead):
        block, blocks = lax.axis_index("blk"), lax.axis_size("blk")
        tall, wide = (block_rows, 1), (1, block_rows)
        key_ids, row_ids = clip_ids(lengths, tall, 0, block, blocks), clip_ids(lengths, wide, 1, block, blocks)
        own[...] = mask_bias(key_ids, row_ids)
        past[...] = mask_bias(clip_ids(lengths, tall, 0, block - 1, blocks), row_ids)
        ahead[...] = mask_bias(key_ids, clip_ids(lengths, wide, 1, block + 1, blocks))

    return pl.pallas_call(
        kernel,
        out_shape=[square] * 3,
        in_specs=[SMEM],
        out_specs=[VMEM] * 3,
        compiler_params=small_kernel(),
        cost_estimate=weighed(0),
        name="masks",
    )(clip_lengths)


def own_scores(keys, queries, chip_values, far_values, upstream, bias):
    sharers = 2 + 2 * len(far_values)
    block_rows, width = keys.shape
    rows = block_rows // sharers
    heads = width // HEAD_DIM

    def kernel(k, q, u, bias, *rest):
        values_in = [ref.at[pl.ds(2 * rows, rows)] for ref in rest[:2]]
        for ref in rest[2 : 1 + sharers // 2]:
            values_in += [ref.at[pl.ds(0, rows)], ref.at[pl.ds(rows, rows)]]
        values, stats, tops, grown_t, slopes_t = rest[1 + sharers // 2 :]
        for step in range(sharers):
            values[place(step, rows), :] = values_in[step][...]
        for head in range(heads):
            columns = pl.ds(head * HEAD_DIM, HEAD_DIM)
            scores = by_rows(k[:, columns], q[:, columns]) * exp2_scale + bias[...]
            row_max = jnp.max(scores, axis=0, keepdims=True)
            grown = jnp.exp2(scores - row_max)
            total = jnp.sum(grown, axis=0, keepdims=True)
            dchances = by_rows(values[:, columns], u[:, columns])
            offset = jnp.sum(grown * dchances, axis=0, keepdims=True) / total
            stats[pl.ds(head, 1), :] = row_max + jnp.log2(total)
            stats[pl.ds(heads + head, 1), :] = offset
            tops[pl.ds(head, 1), :] = row_max
            grown_t[head] = grown.astype(jnp.bfloat16)
            slopes_t[head] = (grown * (dchances - offset)).astype(jnp.bfloat16)

    square = bf16(heads, block_rows, block_rows)
    return pl.pallas_call(
        kernel,
        out_shape=[
            bf16(block_rows, width),
            jax.ShapeDtypeStruct((2 * heads, block_rows), jnp.float32),
            jax.ShapeDtypeStruct((heads, block_rows), jnp.float32),
            square,
            square,
        ],
        in_specs=[VMEM] * (5 + sharers // 2),
        out_specs=[VMEM] * 5,
        compiler_params=pltpu.CompilerParams(vmem_limit_bytes=12 * 2**20),
        cost_estimate=weighed(2e10),
        name="own_scores",
    )(keys, queries, upstream, bias, *chip_values, *far_values)


def own_products(keys, values, grown_t, slopes_t, next_upstream):
    block_rows, width = keys.shape
    heads = width // HEAD_DIM

    def kernel(k, v, grown_t, slopes_t, nu, summed, grown_keys, slope_keys, later):
        for head in range(heads):
            columns = pl.ds(head * HEAD_DIM, HEAD_DIM)
            key, value = k[:, columns], v[:, columns]
            both = by_columns(grown_t[head], jnp.concatenate([value, key], axis=1))
            summed[:, columns] = both[:, :HEAD_DIM]
            grown_keys[:, columns] = both[:, HEAD_DIM:]
            slope_keys[:, columns] = by_columns(slopes_t[head], key)
            later[head] = by_rows(value, nu[:, columns])

    wide = jax.ShapeDtypeStruct((block_rows, width), jnp.float32)
    return pl.pallas_call(
        kernel,
        out_shape=[wide, wide, wide, jax.ShapeDtypeStruct((heads, block_rows, block_rows), jnp.float32)],
        in_specs=[VMEM] * 5,
        out_specs=[VMEM] * 4,
        compiler_params=pltpu.CompilerParams(vmem_limit_bytes=16 * 2**20),
        cost_estimate=weighed(2e10),
        name="own_products",
    )(keys, values, grown_t, slopes_t, next_upstream)


def finish(keys, queries, upstream, first_got, second_got, next_upstream, stats, next_stats, own, previous_values):
    pairs = len(previous_values)
    block_rows, width = keys.shape
    rows = block_rows // pairs // 2
    heads = width // HEAD_DIM

    def kernel(
        k, q, u, first, second, nu, own_stats, stats,
        tops, grown_t, slopes_t, summed, grown_keys, slope_keys, later, past_bias, next_bias, *rest
    ):
        pieces = rest[:pairs]
        attended, query_grads, key_grads, value_grads = rest[pairs : pairs + 4]
        pv, factors = rest[pairs + 4 :]
        even = is_even()
        for step in range(2 * pairs):
            pv[place(step, rows), :] = pieces[step // 2][pl.ds(step % 2 * rows, rows), :]
        factors[...] = jnp.zeros(factors.shape, jnp.float32)

        past, ahead = [], []
        for head in range(heads):
            columns = pl.ds(head * HEAD_DIM, HEAD_DIM)
            query, up, past_value = q[:, columns], u[:, columns], pv[:, columns]
            past_key = jnp.where(even, second[:, columns], first[:, columns])
            own_norm, own_offset = own_stats[pl.ds(head, 1), :], own_stats[pl.ds(heads + head, 1), :]
            own_max = tops[pl.ds(head, 1), :]
            scores = by_rows(past_key, query) * exp2_scale + past_bias[...]
            row_max = jnp.maximum(own_max, jnp.max(scores, axis=0, keepdims=True))
            grown = jnp.exp2(scores - row_max)
            own_total = jnp.exp2(own_norm - row_max)
            share = 1.0 / (own_total + jnp.sum(grown, axis=0, keepdims=True))
            dchances = by_rows(past_value, up)
            offset = share * (own_offset * own_total + jnp.sum(grown * dchances, axis=0, keepdims=True))
            chances = grown * share
            dscores = (chances * (dchances - offset)).astype(jnp.bfloat16)
            factor = jnp.exp2(own_max - row_max) * share
            factors[pl.ds(head, 1), :] = factor
            factors[pl.ds(heads + head, 1), :] = factor * (offset - own_offset)
            past.append((past_key, past_value, chances.astype(jnp.bfloat16), dscores))

        for head in range(heads):
            columns = pl.ds(head * HEAD_DIM, HEAD_DIM)
            key = k[:, columns]
            query = jnp.where(even, first[:, columns], second[:, columns])
            scores = by_rows(key, query) * exp2_scale + next_bias[...]
            row_max = jnp.max(scores, axis=0, keepdims=True)
            grown = jnp.exp2(scores - row_max)
            total = jnp.sum(grown, axis=0, keepdims=True)
            dchances = later[head]
            offset = jnp.sum(grown * dchances, axis=0, keepdims=True) / total
            far_norm, far_offset = stats[pl.ds(head, 1), :], stats[pl.ds(heads + head, 1), :]
            near_norm = row_max + jnp.log2(total)
            top = jnp.maximum(far_norm, near_norm)
            far_part, near_part = jnp.exp2(far_norm - top), jnp.exp2(near_norm - top)
            whole = 1.0 / (far_part + near_part)
            offset = (far_part * far_offset + near_part * offset) * whole
            chances = grown * (jnp.exp2(row_max - top) * whole)
            dscores = (chances * (dchances - offset)).astype(jnp.bfloat16)
            weights = chances.astype(jnp.bfloat16)
            ahead.append((product(dscores, query), product(weights, nu[:, columns])))

        turned = jnp.transpose(factors[...])
        for head in range(heads):
            columns = pl.ds(head * HEAD_DIM, HEAD_DIM)
            past_key, past_value, weights, dscores = past[head]
            factor, shift = turned[:, head : head + 1], turned[:, heads + head : heads + head + 1]
            attended[:, columns] = (
                factor * summed[:, columns] + by_columns(weights, past_value)
            ).astype(jnp.bfloat16)
            query_grads[:, columns] = (
                score_scale
                * (factor * slope_keys[:, columns] - shift * grown_keys[:, columns] + by_columns(dscores, past_key))
            ).astype(jnp.bfloat16)
            wide_query = q[:, columns].astype(jnp.float32)
            scaled_query = (wide_query * factor).astype(jnp.bfloat16)
            shifted_query = (wide_query * shift).astype(jnp.bfloat16)
            scaled_up = (u[:, columns].astype(jnp.float32) * factor).astype(jnp.bfloat16)
            key_grads[:, columns] = (
                score_scale
                * (
                    product(slopes_t[head], scaled_query)
                    - product(grown_t[head], shifted_query)
                    + ahead[head][0]
                )
            ).astype(jnp.bfloat16)
            value_grads[:, columns] = (product(grown_t[head], scaled_up) + ahead[head][1]).astype(jnp.bfloat16)

    return pl.pallas_call(
        kernel,
        out_shape=[bf16(block_rows, width)] * 4,
        in_specs=[VMEM] * (17 + pairs),
        out_specs=[VMEM] * 4,
        scratch_shapes=[
            pltpu.VMEM((block_rows, width), jnp.bfloat16),
            pltpu.VMEM((HEAD_DIM, block_rows), jnp.float32),
        ],
        compiler_params=pltpu.CompilerParams(vmem_limit_bytes=20 * 2**20),
        name="finish",
    )(
        keys, queries, upstream, first_got, second_got, next_upstream, stats, next_stats, *own, *previous_values,
    )


def on_device(queries, key_states, value_states, upstream, clip_lengths):
    sharers = lax.axis_size("head")
    rows = queries.shape[0]
    pieces = cut_pieces(queries, key_states, value_states)
    pieces = [pieces[0]] + [partner_exchange(pieces[step], step) for step in range(1, sharers)]
    far_values, first, second = stack_values(pieces[0], pieces[1], upstream, rows)
    first_got, second_got = block_exchange(first, 0), block_exchange(second, 1)
    far_values = [partner_exchange(stack, 2 * pair + 2) for pair, stack in enumerate(far_values)]
    keys, query_rows, first, second = join_keys_queries(pieces, rows)
    previous, next_upstream = cut_previous_values(first_got, second_got, sharers // 2, far_values)
    first_got, second_got = block_exchange(first, 0), block_exchange(second, 1)
    previous = [partner_exchange(stack, 2 * pair) if pair else stack for pair, stack in enumerate(previous)]
    own_bias, past_bias, next_bias = masks(clip_lengths, upstream.shape[0])
    values, stats, tops, grown_t, slopes_t = own_scores(
        keys, query_rows, pieces[:2], far_values, upstream, own_bias
    )
    next_stats = to_previous(stats)
    own = own_products(keys, values, grown_t, slopes_t, next_upstream)
    own = (tops, grown_t, slopes_t, *own, past_bias, next_bias)
    return tuple(
        finish(
            keys, query_rows, upstream, first_got, second_got, next_upstream, stats, next_stats, own, previous
        )
    )


def solution(mesh):
    return jax.shard_map(
        on_device,
        mesh=mesh,
        in_specs=(
            P(("dp", "blk", "head"), None),
            P(("dp", "blk", "head"), None),
            P(("dp", "blk", "head"), None),
            P(("dp", "blk"), "head"),
            P("dp"),
        ),
        out_specs=(
            P(("dp", "blk"), "head"),
            P(("dp", "blk"), "head"),
            P(("dp", "blk"), "head"),
            P(("dp", "blk"), "head"),
        ),
        check_vma=False,
    )
```

time: 30.8 us -> 27.1 us (0.88)
  Pallas kernels: 10.8 us -> 7.42 us
  waiting for transfers between devices: 4.01 us -> 5.34 us
  starting transfers between devices: 14.5 us -> 13.5 us
  local copies, waits for them, and re-layouts: 0.66 us -> 0.01 us
    ppermute x1, waiting for transfers between devices: 0.01 us -> 2.52 us  [to_previous(): return lax.ppermute(rows, 'blk', [(i, i - 1) for i in range(1, blocks)])]
    pallas_call x5 -> x6, Pallas kernels: 8.33 us -> 6.04 us  [the longest x1 3.91 us: finish(): pl.pallas_call(kernel, out_shape=[bf16(block_rows, width)] * 4, in_specs=...]
    ppermute x7 -> x5, waiting for transfers between devices: 2.31 us -> 0.98 us  [partner_exchange(): return lax.ppermute(rows, 'head', route)]
    pallas_call x1, Pallas kernels: 2.35 us -> 1.31 us  [cut_pieces(): pl.pallas_call(kernel, out_shape=[bf16(height, width) for height in heigh...]
    ppermute x7 -> x5, starting transfers between devices: 6.65 us -> 5.85 us  [partner_exchange(): return lax.ppermute(rows, 'head', route)]
    unnamed x4, local copies, waits for them, and re-layouts: 0.66 us -> 0.01 us
  transfers between devices with their start and end apart: 12 -> 10, of which waited for: 4 -> 5; matrix products, arithmetic and copies ran while one was open for 0% -> 0% of each run, Pallas kernels for 17% -> 8%
where the time goes in v3:
time: 27.1 us; the launch traced here: 27 us
  starting transfers between devices  13.5 us (50%)
  Pallas kernels  7.42 us (27%)
  waiting for transfers between devices  5.34 us (20%)
  between operations  0.73 us (3%)
    ppermute x4, starting transfers between devices, block_exchange(): return lax.ppermute(rows, ('dp', 'blk'), route)  6.31 us
    ppermute x5, starting transfers between devices, partner_exchange(): return lax.ppermute(rows, 'head', route)  5.85 us
    pallas_call x1, Pallas kernels, finish(): pl.pallas_call(kernel, out_shape=[bf16(block_rows, width)] * 4, in_specs=...  3.91 us
    ppermute x1, waiting for transfers between devices, to_previous(): return lax.ppermute(rows, 'blk', [(i, i - 1) for i in range(1, blocks)])  2.52 us
    ppermute x4, waiting for transfers between devices, block_exchange(): return lax.ppermute(rows, ('dp', 'blk'), route)  1.83 us
    pallas_call x1, Pallas kernels, cut_pieces(): pl.pallas_call(kernel, out_shape=[bf16(height, width) for height in heigh...  1.31 us
    ppermute x1, starting transfers between devices, to_previous(): return lax.ppermute(rows, 'blk', [(i, i - 1) for i in range(1, blocks)])  1.29 us
    ppermute x5, waiting for transfers between devices, partner_exchange(): return lax.ppermute(rows, 'head', route)  0.98 us
  transfers between devices with their start and end apart: 10, of which 5 were waited for; matrix products, arithmetic and copies ran while one was open for 0% of the time, Pallas kernels for 8%

profile of v3, /device:TPU:0, one launch (start us, length us, event | category | flops | bytes accessed | tf_op | source)
XLA Modules:
  0.0 27.0 jit_solution(13150870593102522674)
XLA Ops:
  0.6 0.0 copy-start
  0.6 1.3 %cut_pieces.1 = (bf16[256,512]{1,0:T(8,128)(2,1)S(1)}, bf16[256,512]{1,0:T(8,128)(2,1)S(1)}, bf16[128,512]{1,0:T(8,128)(2,1)S(1)}, bf16[128,512]{1,0:T(8,128)(2,1)S(1)}) custom-call(bf16[64,2048]{1,0:T(8,128)(2,1)} %q.1, bf16[64,2048]{1,0:T(8,128)(2,1)} %k.1, bf16[64,2048]{1,0:T(8,128)(2,1)} %v.1), custom_call_target="tpu_custom_call" | custom-call | tf_op jit(solution)/shard_map/cut_pieces/pallas_call | solution.py:88
  2.0 0.5 %collective-permute-start = (bf16[256,512]{1,0:T(8,128)(2,1)S(1)}, bf16[256,512]{1,0:T(8,128)(2,1)S(1)}, u32[]{:S(2)}, u32[]{:S(2)}) collective-permute-start(bf16[256,512]{1,0:T(8,128)(2,1)S(1)} %get-tuple-element.31), channel_id=1, source_target_pairs={{0,1},{1,0},{2,3},{3,2},{4,5},{5,4},{6,7},{7,6},{8,9},{9,8},{10,11... | collective-permute-start | bytes 786440 | tf_op jit(solution)/shard_map/ppermute | solution.py:27
  2.5 0.0 copy-start.1
  2.5 2.6 %collective-permute-start.1 = (bf16[128,512]{1,0:T(8,128)(2,1)S(1)}, bf16[128,512]{1,0:T(8,128)(2,1)S(1)}, u32[]{:S(2)}, u32[]{:S(2)}) collective-permute-start(bf16[128,512]{1,0:T(8,128)(2,1)S(1)} %get-tuple-element.32), channel_id=1, source_target_pairs={{0,2},{1,3},{2,0},{3,1},{4,6},{5,7},{6,4},{7,5},{8,10},{9,11},{10,... | collective-permute-start | bytes 393224 | tf_op jit(solution)/shard_map/ppermute | solution.py:27
  5.1 0.1 collective-permute-start.2
  5.1 0.0 copy-done.1
  5.1 0.7 %masks.1 = (f32[256,256]{1,0:T(8,128)S(1)}, f32[256,256]{1,0:T(8,128)S(1)}, f32[256,256]{1,0:T(8,128)S(1)}) custom-call(s32[4]{0:T(128)S(1)} %copy-done.1), custom_call_target="tpu_custom_call" | custom-call | tf_op jit(solution)/shard_map/masks/pallas_call | solution.py:242
  5.9 0.0 collective-permute-done.refs_1_.theirs.rest_1_
  5.9 0.0 copy-done
  5.9 0.1 stack_values.1
  5.9 1.8 %collective-permute-start.7 = (bf16[128,512]{1,0:T(8,128)(2,1)S(1)}, bf16[128,512]{1,0:T(8,128)(2,1)S(1)}, u32[]{:S(2)}, u32[]{:S(2)}) collective-permute-start(bf16[128,512]{1,0:T(8,128)(2,1)S(1)} %get-tuple-element.40), channel_id=1, source_target_pairs={{0,2},{1,3},{2,0},{3,1},{4,6},{5,7},{6,4},{7,5},{8,10},{9,11},{10,... | collective-permute-start | bytes 393224 | tf_op jit(solution)/shard_map/ppermute | solution.py:27
  7.7 1.6 %collective-permute-start.5 = (bf16[256,512]{1,0:T(8,128)(2,1)S(1)}, bf16[256,512]{1,0:T(8,128)(2,1)S(1)}, u32[]{:S(2)}, u32[]{:S(2)}) collective-permute-start(bf16[256,512]{1,0:T(8,128)(2,1)S(1)} %get-tuple-element.38), channel_id=1, source_target_pairs={{0,4},{4,0},{8,12},{12,8},{16,20},{20,16},{24,28},{28,24},{1,5},{5... | collective-permute-start | bytes 786440 | tf_op jit(solution)/shard_map/ppermute | solution.py:40
  9.3 1.5 %collective-permute-start.6 = (bf16[256,512]{1,0:T(8,128)(2,1)S(1)}, bf16[256,512]{1,0:T(8,128)(2,1)S(1)}, u32[]{:S(2)}, u32[]{:S(2)}) collective-permute-start(bf16[256,512]{1,0:T(8,128)(2,1)S(1)} %get-tuple-element.39), channel_id=1, source_target_pairs={{0,16},{4,8},{8,4},{12,28},{16,0},{20,24},{24,20},{28,12},{1,17},{... | collective-permute-start | bytes 786440 | tf_op jit(solution)/shard_map/ppermute | solution.py:40
  10.8 0.0 collective-permute-done.1.refs_2_
  10.8 0.9 %collective-permute-done.2.refs_3_ = bf16[128,512]{1,0:T(8,128)(2,1)S(1)} collective-permute-done((bf16[128,512]{1,0:T(8,128)(2,1)S(1)}, bf16[128,512]{1,0:T(8,128)(2,1)S(1)}, u32[]{:S(2)}, u32[]{:S(2)}) %collective-permute-start.2) | collective-permute-done | bytes 131104 | tf_op jit(solution)/shard_map/ppermute | solution.py:27
  11.7 0.1 join_keys_queries.1
  11.8 1.7 %collective-permute-start.3 = (bf16[256,512]{1,0:T(8,128)(2,1)S(1)}, bf16[256,512]{1,0:T(8,128)(2,1)S(1)}, u32[]{:S(2)}, u32[]{:S(2)}) collective-permute-start(bf16[256,512]{1,0:T(8,128)(2,1)S(1)} %get-tuple-element.36), channel_id=1, source_target_pairs={{0,4},{4,0},{8,12},{12,8},{16,20},{20,16},{24,28},{28,24},{1,5},{5... | collective-permute-start | bytes 786440 | tf_op jit(solution)/shard_map/ppermute | solution.py:40
  13.5 1.5 %collective-permute-start.4 = (bf16[256,512]{1,0:T(8,128)(2,1)S(1)}, bf16[256,512]{1,0:T(8,128)(2,1)S(1)}, u32[]{:S(2)}, u32[]{:S(2)}) collective-permute-start(bf16[256,512]{1,0:T(8,128)(2,1)S(1)} %get-tuple-element.37), channel_id=1, source_target_pairs={{0,16},{4,8},{8,4},{12,28},{16,0},{20,24},{24,20},{28,12},{1,17},{... | collective-permute-start | bytes 786440 | tf_op jit(solution)/shard_map/ppermute | solution.py:40
  15.0 0.0 collective-permute-done.7.out_0_.rest_2_
  15.0 0.7 %own_scores.1 = (bf16[256,512]{1,0:T(8,128)(2,1)S(1)}, f32[8,256]{1,0:T(8,128)S(1)}, f32[4,256]{1,0:T(4,128)S(1)}, bf16[4,256,256]{2,1,0:T(8,128)(2,1)S(1)}, bf16[4,256,256]{2,1,0:T(8,128)(2,1)S(1)}) custom-call(bf16[256,512]{1,0:T(8,128)(2,1)S(1)} %get-tuple-element.34.k, bf16[256,512]{1,0:T(8,128)(2,1)S(1)} %get-tuple-element.35.q, ...), custom_call_target="tpu_custom_call" | custom-call | flops 20000000000 | tf_op jit(solution)/shard_map/own_scores/pallas_call | solution.py:281
  15.7 1.3 %collective-permute-start.8 = (f32[8,256]{1,0:T(8,128)S(1)}, f32[8,256]{1,0:T(8,128)S(1)}, u32[]{:S(2)}, u32[]{:S(2)}) collective-permute-start(f32[8,256]{1,0:T(8,128)S(1)} %get-tuple-element.43.own_stats), channel_id=1, source_target_pairs={{4,0},{8,4},{12,8},{5,1},{9,5},{13,9},{6,2},{10,6},{14,10},{7,3},{... | collective-permute-start | bytes 24584 | tf_op jit(solution)/shard_map/ppermute | solution.py:45
  17.0 0.0 collective-permute-done.5.first
  17.0 0.7 %collective-permute-done.6.second = bf16[256,512]{1,0:T(8,128)(2,1)S(1)} collective-permute-done((bf16[256,512]{1,0:T(8,128)(2,1)S(1)}, bf16[256,512]{1,0:T(8,128)(2,1)S(1)}, u32[]{:S(2)}, u32[]{:S(2)}) %collective-permute-start.6) | collective-permute-done | bytes 262176 | tf_op jit(solution)/shard_map/ppermute | solution.py:40
  17.8 0.9 %collective-permute-start.9 = (bf16[128,512]{1,0:T(8,128)(2,1)S(1)}, bf16[128,512]{1,0:T(8,128)(2,1)S(1)}, u32[]{:S(2)}, u32[]{:S(2)}) collective-permute-start(bf16[128,512]{1,0:T(8,128)(2,1)S(1)} %get-tuple-element.55), channel_id=1, source_target_pairs={{0,2},{1,3},{2,0},{3,1},{4,6},{5,7},{6,4},{7,5},{8,10},{9,11},{10,... | collective-permute-start | bytes 393224 | tf_op jit(solution)/shard_map/ppermute | solution.py:27
  18.7 0.6 %own_products.1 = (f32[256,512]{1,0:T(8,128)S(1)}, f32[256,512]{1,0:T(8,128)S(1)}, f32[256,512]{1,0:T(8,128)S(1)}, f32[4,256,256]{2,1,0:T(8,128)S(1)}) custom-call(bf16[256,512]{1,0:T(8,128)(2,1)S(1)} %get-tuple-element.34.k, bf16[256,512]{1,0:T(8,128)(2,1)S(1)} %get-tuple-element.47.v, bf16[4,256,256]{2,1,0:T(8,128)(2,1)S(1)} %get-tuple-element.45.grown_t, ...), custom_call_target="tpu_custom_call" | custom-call | flops 20000000000 | tf_op jit(solution)/shard_map/own_products/pallas_call | solution.py:313
  19.3 2.5 %collective-permute-done.8.stats = f32[8,256]{1,0:T(8,128)S(1)} collective-permute-done((f32[8,256]{1,0:T(8,128)S(1)}, f32[8,256]{1,0:T(8,128)S(1)}, u32[]{:S(2)}, u32[]{:S(2)}) %collective-permute-start.8) | collective-permute-done | bytes 8224 | tf_op jit(solution)/shard_map/ppermute | solution.py:45
  21.8 0.0 collective-permute-done.3.first
  21.8 1.1 %collective-permute-done.4.second = bf16[256,512]{1,0:T(8,128)(2,1)S(1)} collective-permute-done((bf16[256,512]{1,0:T(8,128)(2,1)S(1)}, bf16[256,512]{1,0:T(8,128)(2,1)S(1)}, u32[]{:S(2)}, u32[]{:S(2)}) %collective-permute-start.4) | collective-permute-done | bytes 262176 | tf_op jit(solution)/shard_map/ppermute | solution.py:40
  22.9 0.1 collective-permute-done.9.rest_1_
  23.0 3.9 %finish.1 = (bf16[256,512]{1,0:T(8,128)(2,1)}, bf16[256,512]{1,0:T(8,128)(2,1)}, bf16[256,512]{1,0:T(8,128)(2,1)}, bf16[256,512]{1,0:T(8,128)(2,1)}) custom-call(bf16[256,512]{1,0:T(8,128)(2,1)S(1)} %get-tuple-element.34.k, bf16[256,512]{1,0:T(8,128)(2,1)S(1)} %get-tuple-element.35.q, bf16[256,512]{1,0:T(8,128)(2,1)S(1)} %copy-done, ...), custom_call_target="tpu_custom_call" | custom-call | tf_op jit(solution)/shard_map/finish/pallas_call | solution.py:410
  (1 shorter events, 0.0 us)
Async XLA Ops:
  0.6 5.2 %copy-start = (bf16[256,512]{1,0:T(8,128)(2,1)S(1)}, bf16[256,512]{1,0:T(8,128)(2,1)}, u32[]{:S(2)}) copy-start(bf16[256,512]{1,0:T(8,128)(2,1)} %u.5) | copy-start | bytes 786436
  2.0 3.9 %collective-permute-start = (bf16[256,512]{1,0:T(8,128)(2,1)S(1)}, bf16[256,512]{1,0:T(8,128)(2,1)S(1)}, u32[]{:S(2)}, u32[]{:S(2)}) collective-permute-start(bf16[256,512]{1,0:T(8,128)(2,1)S(1)} %get-tuple-element.31), channel_id=1, source_target_pairs={{0,1},{1,0},{2,3},{3,2},{4,5},{5,4},{6,7},{7,6},{8,9},{9,8},{10,11... | collective-permute-start | bytes 786440 | tf_op jit(solution)/shard_map/ppermute | solution.py:27
  2.5 2.6 %copy-start.1 = (s32[4]{0:T(128)S(1)}, s32[4]{0:T(128)}, u32[]{:S(2)}) copy-start(s32[4]{0:T(128)} %lengths.1) | copy-start | bytes 52
  2.5 8.3 %collective-permute-start.1 = (bf16[128,512]{1,0:T(8,128)(2,1)S(1)}, bf16[128,512]{1,0:T(8,128)(2,1)S(1)}, u32[]{:S(2)}, u32[]{:S(2)}) collective-permute-start(bf16[128,512]{1,0:T(8,128)(2,1)S(1)} %get-tuple-element.32), channel_id=1, source_target_pairs={{0,2},{1,3},{2,0},{3,1},{4,6},{5,7},{6,4},{7,5},{8,10},{9,11},{10,... | collective-permute-start | bytes 393224 | tf_op jit(solution)/shard_map/ppermute | solution.py:27
  5.1 6.6 %collective-permute-start.2 = (bf16[128,512]{1,0:T(8,128)(2,1)S(1)}, bf16[128,512]{1,0:T(8,128)(2,1)S(1)}, u32[]{:S(2)}, u32[]{:S(2)}) collective-permute-start(bf16[128,512]{1,0:T(8,128)(2,1)S(1)} %get-tuple-element.33), channel_id=1, source_target_pairs={{0,3},{1,2},{2,1},{3,0},{4,7},{5,6},{6,5},{7,4},{8,11},{9,10},{10,... | collective-permute-start | bytes 393224 | tf_op jit(solution)/shard_map/ppermute | solution.py:27
  5.9 9.1 %collective-permute-start.7 = (bf16[128,512]{1,0:T(8,128)(2,1)S(1)}, bf16[128,512]{1,0:T(8,128)(2,1)S(1)}, u32[]{:S(2)}, u32[]{:S(2)}) collective-permute-start(bf16[128,512]{1,0:T(8,128)(2,1)S(1)} %get-tuple-element.40), channel_id=1, source_target_pairs={{0,2},{1,3},{2,0},{3,1},{4,6},{5,7},{6,4},{7,5},{8,10},{9,11},{10,... | collective-permute-start | bytes 393224 | tf_op jit(solution)/shard_map/ppermute | solution.py:27
  7.7 9.3 %collective-permute-start.5 = (bf16[256,512]{1,0:T(8,128)(2,1)S(1)}, bf16[256,512]{1,0:T(8,128)(2,1)S(1)}, u32[]{:S(2)}, u32[]{:S(2)}) collective-permute-start(bf16[256,512]{1,0:T(8,128)(2,1)S(1)} %get-tuple-element.38), channel_id=1, source_target_pairs={{0,4},{4,0},{8,12},{12,8},{16,20},{20,16},{24,28},{28,24},{1,5},{5... | collective-permute-start | bytes 786440 | tf_op jit(solution)/shard_map/ppermute | solution.py:40
  9.3 8.4 %collective-permute-start.6 = (bf16[256,512]{1,0:T(8,128)(2,1)S(1)}, bf16[256,512]{1,0:T(8,128)(2,1)S(1)}, u32[]{:S(2)}, u32[]{:S(2)}) collective-permute-start(bf16[256,512]{1,0:T(8,128)(2,1)S(1)} %get-tuple-element.39), channel_id=1, source_target_pairs={{0,16},{4,8},{8,4},{12,28},{16,0},{20,24},{24,20},{28,12},{1,17},{... | collective-permute-start | bytes 786440 | tf_op jit(solution)/shard_map/ppermute | solution.py:40
  11.8 10.0 %collective-permute-start.3 = (bf16[256,512]{1,0:T(8,128)(2,1)S(1)}, bf16[256,512]{1,0:T(8,128)(2,1)S(1)}, u32[]{:S(2)}, u32[]{:S(2)}) collective-permute-start(bf16[256,512]{1,0:T(8,128)(2,1)S(1)} %get-tuple-element.36), channel_id=1, source_target_pairs={{0,4},{4,0},{8,12},{12,8},{16,20},{20,16},{24,28},{28,24},{1,5},{5... | collective-permute-start | bytes 786440 | tf_op jit(solution)/shard_map/ppermute | solution.py:40
  13.5 9.5 %collective-permute-start.4 = (bf16[256,512]{1,0:T(8,128)(2,1)S(1)}, bf16[256,512]{1,0:T(8,128)(2,1)S(1)}, u32[]{:S(2)}, u32[]{:S(2)}) collective-permute-start(bf16[256,512]{1,0:T(8,128)(2,1)S(1)} %get-tuple-element.37), channel_id=1, source_target_pairs={{0,16},{4,8},{8,4},{12,28},{16,0},{20,24},{24,20},{28,12},{1,17},{... | collective-permute-start | bytes 786440 | tf_op jit(solution)/shard_map/ppermute | solution.py:40
  15.7 6.1 %collective-permute-start.8 = (f32[8,256]{1,0:T(8,128)S(1)}, f32[8,256]{1,0:T(8,128)S(1)}, u32[]{:S(2)}, u32[]{:S(2)}) collective-permute-start(f32[8,256]{1,0:T(8,128)S(1)} %get-tuple-element.43.own_stats), channel_id=1, source_target_pairs={{4,0},{8,4},{12,8},{5,1},{9,5},{13,9},{6,2},{10,6},{14,10},{7,3},{... | collective-permute-start | bytes 24584 | tf_op jit(solution)/shard_map/ppermute | solution.py:45
  17.8 5.3 %collective-permute-start.9 = (bf16[128,512]{1,0:T(8,128)(2,1)S(1)}, bf16[128,512]{1,0:T(8,128)(2,1)S(1)}, u32[]{:S(2)}, u32[]{:S(2)}) collective-permute-start(bf16[128,512]{1,0:T(8,128)(2,1)S(1)} %get-tuple-element.55), channel_id=1, source_target_pairs={{0,2},{1,3},{2,0},{3,1},{4,6},{5,7},{6,4},{7,5},{8,10},{9,11},{10,... | collective-permute-start | bytes 393224 | tf_op jit(solution)/shard_map/ppermute | solution.py:27

commit v4 on v3

v4 whole, which is shorter than its diff:
```python
import math

import jax
import jax.numpy as jnp
from jax import lax
from jax.experimental import pallas as pl
from jax.experimental.pallas import tpu as pltpu
from jax.sharding import PartitionSpec as P

HEAD_DIM = 128
GROUP = 4

masked_fill = -1e30
score_scale = HEAD_DIM ** (-0.5)
exp2_scale = score_scale * math.log2(math.e)

VMEM = pl.BlockSpec(memory_space=pltpu.VMEM)
SMEM = pl.BlockSpec(memory_space=pltpu.SMEM)
ANY = pl.BlockSpec(memory_space=pl.ANY)


def bf16(*shape):
    return jax.ShapeDtypeStruct(shape, jnp.bfloat16)


def partner_exchange(rows, step):
    route = [(i, i ^ step) for i in range(lax.axis_size("head"))]
    return lax.ppermute(rows, "head", route)


def block_exchange(rows, parity):
    parts, blocks, sharers = lax.axis_size("dp"), lax.axis_size("blk"), lax.axis_size("head")
    route = []
    for part in range(parts):
        for block in range(blocks):
            other = block + 1 if block % 2 == parity else block - 1
            for sharer in range(sharers):
                here = (part * blocks + block) * sharers + sharer
                if 0 <= other < blocks:
                    route.append((here, (part * blocks + other) * sharers + sharer))
                else:
                    route.append((here, here ^ 1))
    return lax.ppermute(rows, ("dp", "blk", "head"), route)


def to_previous(rows):
    blocks = lax.axis_size("blk")
    return lax.ppermute(rows, "blk", [(i, i - 1) for i in range(1, blocks)])


def is_even():
    return lax.rem(lax.axis_index("blk"), 2) == 0


def place(step, size):
    owner = jnp.bitwise_xor(lax.axis_index("head"), step)
    return pl.ds(pl.multiple_of(owner * size, size), size)


def small_kernel():
    return pltpu.CompilerParams(vmem_limit_bytes=4 * 2**20)


def weighed(flops):
    return pl.CostEstimate(flops=int(flops), bytes_accessed=0, transcendentals=0)


def cut_pieces(queries, key_states, value_states):
    sharers = lax.axis_size("head")
    rows, features = queries.shape
    width = features // sharers
    heights = [(2 + sharers // 2) * rows if step < 2 else 2 * rows for step in range(sharers)]

    def kernel(q, k, v, *rest):
        pieces, sems = rest[:sharers], rest[sharers]
        copies = []

        def copy(source, target):
            copies.append(pltpu.make_async_copy(source, target, sems.at[len(copies)]))

        for step in range(sharers):
            columns = place(step, width)
            copy(k.at[:, columns], pieces[step].at[pl.ds(0, rows)])
            copy(q.at[:, columns], pieces[step].at[pl.ds(rows, rows)])
            copy(v.at[:, columns], pieces[step % 2].at[pl.ds((2 + step // 2) * rows, rows)])
        for c in copies:
            c.start()
        for c in copies:
            c.wait()

    return pl.pallas_call(
        kernel,
        out_shape=[bf16(height, width) for height in heights],
        in_specs=[ANY] * 3,
        out_specs=[VMEM] * sharers,
        scratch_shapes=[pltpu.SemaphoreType.DMA((3 * sharers,))],
        compiler_params=pltpu.CompilerParams(vmem_limit_bytes=53 * 2**20),
        name="cut_pieces",
    )(queries, key_states, value_states)


def stack_far_values(own, got, clip_lengths, rows):
    pairs = own.shape[0] // rows - 2
    width = own.shape[1]
    block_rows = 2 * pairs * rows

    def kernel(mine, theirs, lengths, own, past, ahead, *out):
        for pair in range(1, pairs):
            where = pl.ds((2 + pair) * rows, rows)
            out[pair - 1][pl.ds(0, rows), :] = mine[where, :]
            out[pair - 1][pl.ds(rows, rows), :] = theirs[where, :]
        block, blocks = lax.axis_index("blk"), lax.axis_size("blk")
        tall, wide = (block_rows, 1), (1, block_rows)
        key_ids, row_ids = clip_ids(lengths, tall, 0, block, blocks), clip_ids(lengths, wide, 1, block, blocks)
        own[...] = mask_bias(key_ids, row_ids)
        past[...] = mask_bias(clip_ids(lengths, tall, 0, block - 1, blocks), row_ids)
        ahead[...] = mask_bias(key_ids, clip_ids(lengths, wide, 1, block + 1, blocks))

    out = pl.pallas_call(
        kernel,
        out_shape=[jax.ShapeDtypeStruct((block_rows, block_rows), jnp.float32)] * 3
        + [bf16(2 * rows, width)] * (pairs - 1),
        in_specs=[VMEM] * 2 + [SMEM],
        out_specs=[VMEM] * (pairs + 2),
        compiler_params=small_kernel(),
        cost_estimate=weighed(5e9),
        name="stack_far_values",
    )(own, got, clip_lengths)
    return out[3:], out[:3]


def stack_values(own, got, upstream, rows):
    pairs = own.shape[0] // rows - 2
    width = own.shape[1]
    block_rows = upstream.shape[0]

    def kernel(mine, theirs, u, first, second):
        def spread(forward, backward):
            for pair in range(pairs):
                where = pl.ds((2 + pair) * rows, rows)
                forward[pl.ds(2 * pair * rows, rows), :] = mine[where, :]
                forward[pl.ds((2 * pair + 1) * rows, rows), :] = theirs[where, :]
            backward[...] = u[...]

        @pl.when(is_even())
        def _():
            spread(first, second)

        @pl.when(jnp.logical_not(is_even()))
        def _():
            spread(second, first)

    return pl.pallas_call(
        kernel,
        out_shape=[bf16(block_rows, width)] * 2,
        in_specs=[VMEM] * 3,
        out_specs=[VMEM] * 2,
        compiler_params=small_kernel(),
        cost_estimate=weighed(0),
        name="stack_values",
    )(own, got, upstream)


def join_keys_queries(pieces, rows):
    sharers = len(pieces)
    width = pieces[0].shape[1]
    block_rows = rows * sharers

    def kernel(*refs):
        pieces_in = refs[:sharers]
        keys, queries, first, second = refs[sharers:]
        for step in range(sharers):
            where = place(step, rows)
            keys[where, :] = pieces_in[step][pl.ds(0, rows), :]
            queries[where, :] = pieces_in[step][pl.ds(rows, rows), :]

        @pl.when(is_even())
        def _():
            first[...] = keys[...]
            second[...] = queries[...]

        @pl.when(jnp.logical_not(is_even()))
        def _():
            first[...] = queries[...]
            second[...] = keys[...]

    return pl.pallas_call(
        kernel,
        out_shape=[bf16(block_rows, width)] * 4,
        in_specs=[VMEM] * sharers,
        out_specs=[VMEM] * 4,
        compiler_params=small_kernel(),
        cost_estimate=weighed(0),
        name="join_keys_queries",
    )(*pieces)


def cut_previous_values(first_got, second_got, pairs):
    block_rows, width = first_got.shape
    rows = block_rows // pairs

    def kernel(first, second, *out):
        def split(forward, backward):
            for pair in range(pairs):
                out[pair][...] = forward[pl.ds(pair * rows, rows), :]
            out[pairs][...] = backward[...]

        @pl.when(is_even())
        def _():
            split(second, first)

        @pl.when(jnp.logical_not(is_even()))
        def _():
            split(first, second)

    out = pl.pallas_call(
        kernel,
        out_shape=[bf16(rows, width)] * pairs + [bf16(block_rows, width)],
        in_specs=[VMEM] * 2,
        out_specs=[VMEM] * (pairs + 1),
        compiler_params=small_kernel(),
        cost_estimate=weighed(0),
        name="cut_previous_values",
    )(first_got, second_got)
    return out[:pairs], out[pairs]


def clip_ids(lengths, shape, axis, block, blocks):
    position = block * shape[axis] + lax.broadcasted_iota(jnp.int32, shape, axis)
    ids, end = jnp.zeros(shape, jnp.int32), jnp.int32(0)
    for clip in range(lengths.shape[0]):
        end = end + lengths[clip]
        ids = ids + (position >= end).astype(jnp.int32)
    return jnp.where(jnp.logical_and(block >= 0, block < blocks), ids, -1)


def mask_bias(key_ids, query_ids):
    return jnp.where(key_ids == query_ids, 0.0, masked_fill).astype(jnp.float32)


def by_rows(a, b):
    return lax.dot_general(a, b, (((1,), (1,)), ((), ())), preferred_element_type=jnp.float32)


def by_columns(a, b):
    return lax.dot_general(a, b, (((0,), (0,)), ((), ())), preferred_element_type=jnp.float32)


def product(a, b):
    return jnp.dot(a, b, preferred_element_type=jnp.float32)


def own_scores(keys, queries, chip_values, far_values, upstream, bias, after):
    sharers = 2 + 2 * len(far_values)
    block_rows, width = keys.shape
    rows = block_rows // sharers
    heads = width // HEAD_DIM

    def kernel(k, q, u, bias, _, *rest):
        values_in = [ref.at[pl.ds(2 * rows, rows)] for ref in rest[:2]]
        for ref in rest[2 : 1 + sharers // 2]:
            values_in += [ref.at[pl.ds(0, rows)], ref.at[pl.ds(rows, rows)]]
        values, stats, tops, grown_t, slopes_t = rest[1 + sharers // 2 :]
        for step in range(sharers):
            values[place(step, rows), :] = values_in[step][...]
        for head in range(heads):
            columns = pl.ds(head * HEAD_DIM, HEAD_DIM)
            scores = by_rows(k[:, columns], q[:, columns]) * exp2_scale + bias[...]
            row_max = jnp.max(scores, axis=0, keepdims=True)
            grown = jnp.exp2(scores - row_max)
            total = jnp.sum(grown, axis=0, keepdims=True)
            dchances = by_rows(values[:, columns], u[:, columns])
            offset = jnp.sum(grown * dchances, axis=0, keepdims=True) / total
            stats[pl.ds(head, 1), :] = row_max + jnp.log2(total)
            stats[pl.ds(heads + head, 1), :] = offset
            tops[pl.ds(head, 1), :] = row_max
            grown_t[head] = grown.astype(jnp.bfloat16)
            slopes_t[head] = (grown * (dchances - offset)).astype(jnp.bfloat16)

    square = bf16(heads, block_rows, block_rows)
    return pl.pallas_call(
        kernel,
        out_shape=[
            bf16(block_rows, width),
            jax.ShapeDtypeStruct((2 * heads, block_rows), jnp.float32),
            jax.ShapeDtypeStruct((heads, block_rows), jnp.float32),
            square,
            square,
        ],
        in_specs=[VMEM] * (6 + sharers // 2),
        out_specs=[VMEM] * 5,
        compiler_params=pltpu.CompilerParams(vmem_limit_bytes=12 * 2**20),
        cost_estimate=weighed(0),
        name="own_scores",
    )(keys, queries, upstream, bias, after, *chip_values, *far_values)


def own_products(keys, values, grown_t, slopes_t, next_upstream):
    block_rows, width = keys.shape
    heads = width // HEAD_DIM

    def kernel(k, v, grown_t, slopes_t, nu, summed, grown_keys, slope_keys, later):
        for head in range(heads):
            columns = pl.ds(head * HEAD_DIM, HEAD_DIM)
            key, value = k[:, columns], v[:, columns]
            both = by_columns(grown_t[head], jnp.concatenate([value, key], axis=1))
            summed[:, columns] = both[:, :HEAD_DIM]
            grown_keys[:, columns] = both[:, HEAD_DIM:]
            slope_keys[:, columns] = by_columns(slopes_t[head], key)
            later[head] = by_rows(value, nu[:, columns])

    wide = jax.ShapeDtypeStruct((block_rows, width), jnp.float32)
    return pl.pallas_call(
        kernel,
        out_shape=[wide, wide, wide, jax.ShapeDtypeStruct((heads, block_rows, block_rows), jnp.float32)],
        in_specs=[VMEM] * 5,
        out_specs=[VMEM] * 4,
        compiler_params=pltpu.CompilerParams(vmem_limit_bytes=16 * 2**20),
        cost_estimate=weighed(2e10),
        name="own_products",
    )(keys, values, grown_t, slopes_t, next_upstream)


def past_keys(queries, upstream, first_got, second_got, stats, own, previous_values, past_bias):
    pairs = len(previous_values)
    block_rows, width = queries.shape
    rows = block_rows // pairs // 2
    heads = width // HEAD_DIM

    def kernel(
        q, u, first, second, own_stats, tops, grown_t, slopes_t, summed, grown_keys, slope_keys, past_bias, *rest
    ):
        pieces = rest[:pairs]
        attended, query_grads, key_part, value_part, pv, factors = rest[pairs:]
        even = is_even()
        for step in range(2 * pairs):
            pv[place(step, rows), :] = pieces[step // 2][pl.ds(step % 2 * rows, rows), :]
        factors[...] = jnp.zeros(factors.shape, jnp.float32)

        for start in range(0, heads, GROUP):
            group = range(start, min(start + GROUP, heads))
            cols = [pl.ds(head * HEAD_DIM, HEAD_DIM) for head in group]
            keys = [jnp.where(even, second[:, c], first[:, c]) for c in cols]
            scores = [by_rows(key, q[:, c]) * exp2_scale + past_bias[...] for key, c in zip(keys, cols)]
            maxes = [
                jnp.maximum(tops[pl.ds(head, 1), :], jnp.max(x, axis=0, keepdims=True)) for head, x in zip(group, scores)
            ]
            grown = [jnp.exp2(x - m) for x, m in zip(scores, maxes)]
            own = [jnp.exp2(own_stats[pl.ds(head, 1), :] - m) for head, m in zip(group, maxes)]
            shares = [1.0 / (o + jnp.sum(x, axis=0, keepdims=True)) for o, x in zip(own, grown)]
            dchances = [by_rows(pv[:, c], u[:, c]) for c in cols]
            offsets = [
                y * (own_stats[pl.ds(heads + head, 1), :] * o + jnp.sum(x * d, axis=0, keepdims=True))
                for head, o, x, y, d in zip(group, own, grown, shares, dchances)
            ]
            for n, head in enumerate(group):
                factor = jnp.exp2(tops[pl.ds(head, 1), :] - maxes[n]) * shares[n]
                factors[pl.ds(head, 1), :] = factor
                factors[pl.ds(heads + head, 1), :] = factor * (offsets[n] - own_stats[pl.ds(heads + head, 1), :])
            chances = [x * y for x, y in zip(grown, shares)]
            weights = [x.astype(jnp.bfloat16) for x in chances]
            dscores = [(x * (d - o)).astype(jnp.bfloat16) for x, d, o in zip(chances, dchances, offsets)]
            turned = jnp.transpose(factors[...])
            for n, (head, c) in enumerate(zip(group, cols)):
                factor, shift = turned[:, head : head + 1], turned[:, heads + head : heads + head + 1]
                attended[:, c] = (factor * summed[:, c] + by_columns(weights[n], pv[:, c])).astype(jnp.bfloat16)
                query_grads[:, c] = (
                    score_scale * (factor * slope_keys[:, c] - shift * grown_keys[:, c] + by_columns(dscores[n], keys[n]))
                ).astype(jnp.bfloat16)
                wide_query = q[:, c].astype(jnp.float32)
                scaled_query = (wide_query * factor).astype(jnp.bfloat16)
                shifted_query = (wide_query * shift).astype(jnp.bfloat16)
                scaled_up = (u[:, c].astype(jnp.float32) * factor).astype(jnp.bfloat16)
                key_part[:, c] = product(slopes_t[head], scaled_query) - product(grown_t[head], shifted_query)
                value_part[:, c] = product(grown_t[head], scaled_up)

    wide = jax.ShapeDtypeStruct((block_rows, width), jnp.float32)
    return pl.pallas_call(
        kernel,
        out_shape=[bf16(block_rows, width)] * 2 + [wide] * 2,
        in_specs=[VMEM] * (12 + pairs),
        out_specs=[VMEM] * 4,
        scratch_shapes=[
            pltpu.VMEM((block_rows, width), jnp.bfloat16),
            pltpu.VMEM((HEAD_DIM, block_rows), jnp.float32),
        ],
        compiler_params=pltpu.CompilerParams(vmem_limit_bytes=20 * 2**20),
        cost_estimate=weighed(0),
        name="past_keys",
    )(queries, upstream, first_got, second_got, stats, *own, past_bias, *previous_values)


def next_rows(keys, first_got, second_got, next_upstream, next_stats, later, next_bias, done, parts):
    block_rows, width = keys.shape
    heads = width // HEAD_DIM

    def kernel(k, first, second, nu, stats, later, next_bias, attended, query_grads, key_part, value_part, *rest):
        outs, (key_grads, value_grads, sems) = rest[:4], rest[4:]
        copies = [pltpu.make_async_copy(source, outs[i], sems.at[i]) for i, source in enumerate((attended, query_grads))]
        for c in copies:
            c.start()
        even = is_even()
        for start in range(0, heads, GROUP):
            group = range(start, min(start + GROUP, heads))
            cols = [pl.ds(head * HEAD_DIM, HEAD_DIM) for head in group]
            queries = [jnp.where(even, first[:, c], second[:, c]) for c in cols]
            scores = [by_rows(k[:, c], query) * exp2_scale + next_bias[...] for c, query in zip(cols, queries)]
            maxes = [jnp.max(x, axis=0, keepdims=True) for x in scores]
            grown = [jnp.exp2(x - m) for x, m in zip(scores, maxes)]
            totals = [jnp.sum(x, axis=0, keepdims=True) for x in grown]
            offsets = [
                jnp.sum(x * later[head], axis=0, keepdims=True) / total
                for x, head, total in zip(grown, group, totals)
            ]
            scales = []
            for n, head in enumerate(group):
                far_norm, far_offset = stats[pl.ds(head, 1), :], stats[pl.ds(heads + head, 1), :]
                near_norm = maxes[n] + jnp.log2(totals[n])
                top = jnp.maximum(far_norm, near_norm)
                far_part, near_part = jnp.exp2(far_norm - top), jnp.exp2(near_norm - top)
                whole = 1.0 / (far_part + near_part)
                offsets[n] = (far_part * far_offset + near_part * offsets[n]) * whole
                scales.append(jnp.exp2(maxes[n] - top) * whole)
            chances = [x * y for x, y in zip(grown, scales)]
            weights = [x.astype(jnp.bfloat16) for x in chances]
            dscores = [
                (x * (later[head] - offset)).astype(jnp.bfloat16)
                for x, head, offset in zip(chances, group, offsets)
            ]
            for n, c in enumerate(cols):
                key_grads[:, c] = (score_scale * (key_part[:, c] + product(dscores[n], queries[n]))).astype(jnp.bfloat16)
                value_grads[:, c] = (value_part[:, c] + product(weights[n], nu[:, c])).astype(jnp.bfloat16)
            wide = pl.ds(start * HEAD_DIM, len(group) * HEAD_DIM)
            for i, source in ((2, key_grads), (3, value_grads)):
                copies.append(pltpu.make_async_copy(source.at[:, wide], outs[i].at[:, wide], sems.at[len(copies)]))
                copies[-1].start()
        for c in copies:
            c.wait()

    return pl.pallas_call(
        kernel,
        out_shape=[bf16(block_rows, width)] * 4,
        in_specs=[VMEM] * 11,
        out_specs=[ANY] * 4,
        scratch_shapes=[pltpu.VMEM((block_rows, width), jnp.bfloat16)] * 2
        + [pltpu.SemaphoreType.DMA((2 + 2 * heads,))],
        compiler_params=pltpu.CompilerParams(vmem_limit_bytes=16 * 2**20),
        name="next_rows",
    )(keys, first_got, second_got, next_upstream, next_stats, later, next_bias, *done, *parts)


def on_device(queries, key_states, value_states, upstream, clip_lengths):
    sharers = lax.axis_size("head")
    rows = queries.shape[0]
    pieces = cut_pieces(queries, key_states, value_states)
    pieces = [pieces[0]] + [partner_exchange(pieces[step], step) for step in range(1, sharers)]
    first, second = stack_values(pieces[0], pieces[1], upstream, rows)
    first_got, second_got = block_exchange(first, 0), block_exchange(second, 1)
    far_values, (own_bias, past_bias, next_bias) = stack_far_values(pieces[0], pieces[1], clip_lengths, rows)
    far_values = [partner_exchange(stack, 2 * pair + 2) for pair, stack in enumerate(far_values)]
    keys, query_rows, first, second = join_keys_queries(pieces, rows)
    previous, next_upstream = cut_previous_values(first_got, second_got, sharers // 2)
    first_got, second_got = block_exchange(first, 0), block_exchange(second, 1)
    previous = [partner_exchange(stack, 2 * pair) if pair else stack for pair, stack in enumerate(previous)]
    values, stats, tops, grown_t, slopes_t = own_scores(
        keys, query_rows, pieces[:2], far_values, upstream, own_bias, next_upstream
    )
    next_stats = to_previous(stats)
    summed, grown_keys, slope_keys, later = own_products(keys, values, grown_t, slopes_t, next_upstream)
    own = (tops, grown_t, slopes_t, summed, grown_keys, slope_keys)
    attended, query_grads, key_part, value_part = past_keys(
        query_rows, upstream, first_got, second_got, stats, own, previous, past_bias
    )
    return tuple(
        next_rows(
            keys, first_got, second_got, next_upstream, next_stats, later, next_bias,
            (attended, query_grads), (key_part, value_part),
        )
    )


def solution(mesh):
    return jax.shard_map(
        on_device,
        mesh=mesh,
        in_specs=(
            P(("dp", "blk", "head"), None),
            P(("dp", "blk", "head"), None),
            P(("dp", "blk", "head"), None),
            P(("dp", "blk"), "head"),
            P("dp"),
        ),
        out_specs=(
            P(("dp", "blk"), "head"),
            P(("dp", "blk"), "head"),
            P(("dp", "blk"), "head"),
            P(("dp", "blk"), "head"),
        ),
        check_vma=False,
    )
```

time: 27.1 us -> 25 us (0.923); the launches traced: 27 us -> 24.6 us
  starting transfers between devices: 13.5 us -> 11.8 us
  waiting for transfers between devices: 5.34 us -> 4.78 us
    ppermute x1, waiting for transfers between devices: 2.52 us -> 0.01 us  [to_previous(): return lax.ppermute(rows, 'blk', [(i, i - 1) for i in range(1, blocks)])]
    ppermute x4, starting transfers between devices: 6.31 us -> 4.27 us  [block_exchange(): return lax.ppermute(rows, ('dp', 'blk', 'head'), route)]
    ppermute x5, waiting for transfers between devices: 0.98 us -> 2.28 us  [partner_exchange(): return lax.ppermute(rows, 'head', route)]
    ppermute x4, waiting for transfers between devices: 1.83 us -> 2.5 us  [block_exchange(): return lax.ppermute(rows, ('dp', 'blk', 'head'), route)]
    ppermute x5, starting transfers between devices: 5.85 us -> 6.26 us  [partner_exchange(): return lax.ppermute(rows, 'head', route)]
    pallas_call x3 -> x4, Pallas kernels: 4.69 us -> 4.48 us  [the longest x1 1.92 us: next_rows(): pl.pallas_call(kernel, out_shape=[bf16(block_rows, width)] * 4, in_specs=...]
  transfers between devices with their start and end apart: 10 -> 10, of which waited for: 5 -> 2; matrix products, arithmetic and copies ran while one was open for 0% -> 0% of each run, Pallas kernels for 8% -> 16%
where the time goes in v4:
time: 25 us; the launch traced here: 24.6 us
  starting transfers between devices  11.8 us (47%)
  Pallas kernels  7.23 us (29%)
  waiting for transfers between devices  4.78 us (19%)
  between operations  0.73 us (3%)
    ppermute x5, starting transfers between devices, partner_exchange(): return lax.ppermute(rows, 'head', route)  6.26 us
    ppermute x4, starting transfers between devices, block_exchange(): return lax.ppermute(rows, ('dp', 'blk', 'head'), route)  4.27 us
    ppermute x4, waiting for transfers between devices, block_exchange(): return lax.ppermute(rows, ('dp', 'blk', 'head'), route)  2.5 us
    ppermute x5, waiting for transfers between devices, partner_exchange(): return lax.ppermute(rows, 'head', route)  2.28 us
    pallas_call x1, Pallas kernels, next_rows(): pl.pallas_call(kernel, out_shape=[bf16(block_rows, width)] * 4, in_specs=...  1.92 us
    pallas_call x1, Pallas kernels, past_keys(): pl.pallas_call(kernel, out_shape=[bf16(block_rows, width)] * 2 + [wide] *...  1.79 us
    pallas_call x1, Pallas kernels, cut_pieces(): pl.pallas_call(kernel, out_shape=[bf16(height, width) for height in heigh...  1.31 us
    ppermute x1, starting transfers between devices, to_previous(): return lax.ppermute(rows, 'blk', [(i, i - 1) for i in range(1, blocks)])  1.29 us
  transfers between devices with their start and end apart: 10, of which 2 were waited for; matrix products, arithmetic and copies ran while one was open for 0% of the time, Pallas kernels for 16%

profile of v4, /device:TPU:0, one launch (start us, length us, event | category | flops | bytes accessed | tf_op | source)
XLA Modules:
  0.0 24.6 jit_solution(30019147480920858)
XLA Ops:
  0.6 0.0 copy-start
  0.6 1.3 %cut_pieces.1 = (bf16[256,512]{1,0:T(8,128)(2,1)S(1)}, bf16[256,512]{1,0:T(8,128)(2,1)S(1)}, bf16[128,512]{1,0:T(8,128)(2,1)S(1)}, bf16[128,512]{1,0:T(8,128)(2,1)S(1)}) custom-call(bf16[64,2048]{1,0:T(8,128)(2,1)} %q.1, bf16[64,2048]{1,0:T(8,128)(2,1)} %k.1, bf16[64,2048]{1,0:T(8,128)(2,1)} %v.1), custom_call_target="tpu_custom_call" | custom-call | tf_op jit(solution)/shard_map/cut_pieces/pallas_call | solution.py:91
  2.0 0.5 %collective-permute-start = (bf16[256,512]{1,0:T(8,128)(2,1)S(1)}, bf16[256,512]{1,0:T(8,128)(2,1)S(1)}, u32[]{:S(2)}, u32[]{:S(2)}) collective-permute-start(bf16[256,512]{1,0:T(8,128)(2,1)S(1)} %get-tuple-element.35), channel_id=1, source_target_pairs={{0,1},{1,0},{2,3},{3,2},{4,5},{5,4},{6,7},{7,6},{8,9},{9,8},{10,11... | collective-permute-start | bytes 786440 | tf_op jit(solution)/shard_map/ppermute | solution.py:28
  2.5 2.6 %collective-permute-start.1 = (bf16[128,512]{1,0:T(8,128)(2,1)S(1)}, bf16[128,512]{1,0:T(8,128)(2,1)S(1)}, u32[]{:S(2)}, u32[]{:S(2)}) collective-permute-start(bf16[128,512]{1,0:T(8,128)(2,1)S(1)} %get-tuple-element.36), channel_id=1, source_target_pairs={{0,2},{1,3},{2,0},{3,1},{4,6},{5,7},{6,4},{7,5},{8,10},{9,11},{10,... | collective-permute-start | bytes 393224 | tf_op jit(solution)/shard_map/ppermute | solution.py:28
  5.0 0.1 collective-permute-start.2
  5.1 0.0 collective-permute-done.refs_1_.theirs.rest_1_
  5.1 0.0 copy-done
  5.2 0.0 copy-start.1
  5.2 1.9 %collective-permute-start.5 = (bf16[256,512]{1,0:T(8,128)(2,1)S(1)}, bf16[256,512]{1,0:T(8,128)(2,1)S(1)}, u32[]{:S(2)}, u32[]{:S(2)}) collective-permute-start(bf16[256,512]{1,0:T(8,128)(2,1)S(1)} %get-tuple-element.41), channel_id=1, source_target_pairs={{0,4},{1,5},{2,6},{3,7},{4,0},{5,1},{6,2},{7,3},{8,12},{9,13},{10,... | collective-permute-start | bytes 786440 | tf_op jit(solution)/shard_map/ppermute | solution.py:43
  7.0 0.1 collective-permute-start.6
  7.1 0.0 copy-done.1
  7.1 0.7 %stack_far_values.1 = (f32[256,256]{1,0:T(8,128)S(1)}, f32[256,256]{1,0:T(8,128)S(1)}, f32[256,256]{1,0:T(8,128)S(1)}, bf16[128,512]{1,0:T(8,128)(2,1)S(1)}) custom-call(bf16[256,512]{1,0:T(8,128)(2,1)S(1)} %get-tuple-element.34.refs_0_.mine.rest_0_, bf16[256,512]{1,0:T(8,128)(2,1)S(1)} %collective-permute-done.refs_1_.theirs.rest_1_, s32[4]{0:T(128)S(1)} %copy-done.1), custom_call_target="tpu_custom_call" | custom-call | flops 5000000000 | tf_op jit(solution)/shard_map/stack_far_values/pallas_call | solution.py:119
  7.9 1.6 %collective-permute-start.7 = (bf16[128,512]{1,0:T(8,128)(2,1)S(1)}, bf16[128,512]{1,0:T(8,128)(2,1)S(1)}, u32[]{:S(2)}, u32[]{:S(2)}) collective-permute-start(bf16[128,512]{1,0:T(8,128)(2,1)S(1)} %get-tuple-element.46), channel_id=1, source_target_pairs={{0,2},{1,3},{2,0},{3,1},{4,6},{5,7},{6,4},{7,5},{8,10},{9,11},{10,... | collective-permute-start | bytes 393224 | tf_op jit(solution)/shard_map/ppermute | solution.py:28
  9.4 0.0 collective-permute-done.1.refs_2_
  9.4 2.3 %collective-permute-done.2.refs_3_ = bf16[128,512]{1,0:T(8,128)(2,1)S(1)} collective-permute-done((bf16[128,512]{1,0:T(8,128)(2,1)S(1)}, bf16[128,512]{1,0:T(8,128)(2,1)S(1)}, u32[]{:S(2)}, u32[]{:S(2)}) %collective-permute-start.2) | collective-permute-done | bytes 131104 | tf_op jit(solution)/shard_map/ppermute | solution.py:28
  11.7 0.1 join_keys_queries.1
  11.8 1.7 %collective-permute-start.3 = (bf16[256,512]{1,0:T(8,128)(2,1)S(1)}, bf16[256,512]{1,0:T(8,128)(2,1)S(1)}, u32[]{:S(2)}, u32[]{:S(2)}) collective-permute-start(bf16[256,512]{1,0:T(8,128)(2,1)S(1)} %get-tuple-element.39), channel_id=1, source_target_pairs={{0,4},{1,5},{2,6},{3,7},{4,0},{5,1},{6,2},{7,3},{8,12},{9,13},{10,... | collective-permute-start | bytes 786440 | tf_op jit(solution)/shard_map/ppermute | solution.py:43
  13.5 0.6 %collective-permute-start.4 = (bf16[256,512]{1,0:T(8,128)(2,1)S(1)}, bf16[256,512]{1,0:T(8,128)(2,1)S(1)}, u32[]{:S(2)}, u32[]{:S(2)}) collective-permute-start(bf16[256,512]{1,0:T(8,128)(2,1)S(1)} %get-tuple-element.40), channel_id=1, source_target_pairs={{0,1},{1,0},{2,3},{3,2},{4,8},{5,9},{6,10},{7,11},{8,4},{9,5},{10,... | collective-permute-start | bytes 786440 | tf_op jit(solution)/shard_map/ppermute | solution.py:43
  14.1 0.0 collective-permute-done.5.first
  14.1 0.0 collective-permute-done.6.second
  14.1 1.6 %collective-permute-start.9 = (bf16[128,512]{1,0:T(8,128)(2,1)S(1)}, bf16[128,512]{1,0:T(8,128)(2,1)S(1)}, u32[]{:S(2)}, u32[]{:S(2)}) collective-permute-start(bf16[128,512]{1,0:T(8,128)(2,1)S(1)} %get-tuple-element.59), channel_id=1, source_target_pairs={{0,2},{1,3},{2,0},{3,1},{4,6},{5,7},{6,4},{7,5},{8,10},{9,11},{10,... | collective-permute-start | bytes 393224 | tf_op jit(solution)/shard_map/ppermute | solution.py:28
  15.7 0.0 collective-permute-done.7.rest_2_
  15.7 0.7 %own_scores.1 = (bf16[256,512]{1,0:T(8,128)(2,1)S(1)}, f32[8,256]{1,0:T(8,128)S(1)}, f32[4,256]{1,0:T(4,128)S(1)}, bf16[4,256,256]{2,1,0:T(8,128)(2,1)S(1)}, bf16[4,256,256]{2,1,0:T(8,128)(2,1)S(1)}) custom-call(bf16[256,512]{1,0:T(8,128)(2,1)S(1)} %get-tuple-element.38.k, bf16[256,512]{1,0:T(8,128)(2,1)S(1)} %get-tuple-element.44.q, ...), custom_call_target="tpu_custom_call" | custom-call | tf_op jit(solution)/shard_map/own_scores/pallas_call | solution.py:281
  16.4 1.3 %collective-permute-start.8 = (f32[8,256]{1,0:T(8,128)S(1)}, f32[8,256]{1,0:T(8,128)S(1)}, u32[]{:S(2)}, u32[]{:S(2)}) collective-permute-start(f32[8,256]{1,0:T(8,128)S(1)} %get-tuple-element.47.own_stats), channel_id=1, source_target_pairs={{4,0},{8,4},{12,8},{5,1},{9,5},{13,9},{6,2},{10,6},{14,10},{7,3},{... | collective-permute-start | bytes 24584 | tf_op jit(solution)/shard_map/ppermute | solution.py:48
  17.7 0.6 %own_products.1 = (f32[256,512]{1,0:T(8,128)S(1)}, f32[256,512]{1,0:T(8,128)S(1)}, f32[256,512]{1,0:T(8,128)S(1)}, f32[4,256,256]{2,1,0:T(8,128)S(1)}) custom-call(bf16[256,512]{1,0:T(8,128)(2,1)S(1)} %get-tuple-element.38.k, bf16[256,512]{1,0:T(8,128)(2,1)S(1)} %get-tuple-element.48.v, bf16[4,256,256]{2,1,0:T(8,128)(2,1)S(1)} %get-tuple-element.49.grown_t, ...), custom_call_target="tpu_custom_call" | custom-call | flops 20000000000 | tf_op jit(solution)/shard_map/own_products/pallas_call | solution.py:313
  18.4 2.5 %collective-permute-done.3.first = bf16[256,512]{1,0:T(8,128)(2,1)S(1)} collective-permute-done((bf16[256,512]{1,0:T(8,128)(2,1)S(1)}, bf16[256,512]{1,0:T(8,128)(2,1)S(1)}, u32[]{:S(2)}, u32[]{:S(2)}) %collective-permute-start.3) | collective-permute-done | bytes 262176 | tf_op jit(solution)/shard_map/ppermute | solution.py:43
  20.8 0.0 collective-permute-done.4.second
  20.9 0.0 collective-permute-done.9.rest_1_
  20.9 1.8 %past_keys.1 = (bf16[256,512]{1,0:T(8,128)(2,1)S(1)}, bf16[256,512]{1,0:T(8,128)(2,1)S(1)}, f32[256,512]{1,0:T(8,128)S(1)}, f32[256,512]{1,0:T(8,128)S(1)}) custom-call(bf16[256,512]{1,0:T(8,128)(2,1)S(1)} %get-tuple-element.44.q, bf16[256,512]{1,0:T(8,128)(2,1)S(1)} %copy-done, bf16[256,512]{1,0:T(8,128)(2,1)S(1)} %collective-permute-done.3.first, ...), custom_call_target="tpu_custom_call" | custom-call | tf_op jit(solution)/shard_map/past_keys/pallas_call | solution.py:378
  22.6 0.0 collective-permute-done.8.stats
  22.7 1.9 %next_rows.1 = (bf16[256,512]{1,0:T(8,128)(2,1)}, bf16[256,512]{1,0:T(8,128)(2,1)}, bf16[256,512]{1,0:T(8,128)(2,1)}, bf16[256,512]{1,0:T(8,128)(2,1)}) custom-call(bf16[256,512]{1,0:T(8,128)(2,1)S(1)} %get-tuple-element.38.k, bf16[256,512]{1,0:T(8,128)(2,1)S(1)} %collective-permute-done.3.first, bf16[256,512]{1,0:T(8,128)(2,1)S(1)} %collective-permute-done.4.second, ...), custom_call_target="tpu_custom_call" | custom-call | tf_op jit(solution)/shard_map/next_rows/pallas_call | solution.py:440
  (2 shorter events, 0.1 us)
Async XLA Ops:
  0.6 4.5 %copy-start = (bf16[256,512]{1,0:T(8,128)(2,1)S(1)}, bf16[256,512]{1,0:T(8,128)(2,1)}, u32[]{:S(2)}) copy-start(bf16[256,512]{1,0:T(8,128)(2,1)} %u.5) | copy-start | bytes 786436
  2.0 3.2 %collective-permute-start = (bf16[256,512]{1,0:T(8,128)(2,1)S(1)}, bf16[256,512]{1,0:T(8,128)(2,1)S(1)}, u32[]{:S(2)}, u32[]{:S(2)}) collective-permute-start(bf16[256,512]{1,0:T(8,128)(2,1)S(1)} %get-tuple-element.35), channel_id=1, source_target_pairs={{0,1},{1,0},{2,3},{3,2},{4,5},{5,4},{6,7},{7,6},{8,9},{9,8},{10,11... | collective-permute-start | bytes 786440 | tf_op jit(solution)/shard_map/ppermute | solution.py:28
  2.5 6.9 %collective-permute-start.1 = (bf16[128,512]{1,0:T(8,128)(2,1)S(1)}, bf16[128,512]{1,0:T(8,128)(2,1)S(1)}, u32[]{:S(2)}, u32[]{:S(2)}) collective-permute-start(bf16[128,512]{1,0:T(8,128)(2,1)S(1)} %get-tuple-element.36), channel_id=1, source_target_pairs={{0,2},{1,3},{2,0},{3,1},{4,6},{5,7},{6,4},{7,5},{8,10},{9,11},{10,... | collective-permute-start | bytes 393224 | tf_op jit(solution)/shard_map/ppermute | solution.py:28
  5.0 6.6 %collective-permute-start.2 = (bf16[128,512]{1,0:T(8,128)(2,1)S(1)}, bf16[128,512]{1,0:T(8,128)(2,1)S(1)}, u32[]{:S(2)}, u32[]{:S(2)}) collective-permute-start(bf16[128,512]{1,0:T(8,128)(2,1)S(1)} %get-tuple-element.37), channel_id=1, source_target_pairs={{0,3},{1,2},{2,1},{3,0},{4,7},{5,6},{6,5},{7,4},{8,11},{9,10},{10,... | collective-permute-start | bytes 393224 | tf_op jit(solution)/shard_map/ppermute | solution.py:28
  5.2 2.0 %copy-start.1 = (s32[4]{0:T(128)S(1)}, s32[4]{0:T(128)}, u32[]{:S(2)}) copy-start(s32[4]{0:T(128)} %lengths.1) | copy-start | bytes 52
  5.2 8.9 %collective-permute-start.5 = (bf16[256,512]{1,0:T(8,128)(2,1)S(1)}, bf16[256,512]{1,0:T(8,128)(2,1)S(1)}, u32[]{:S(2)}, u32[]{:S(2)}) collective-permute-start(bf16[256,512]{1,0:T(8,128)(2,1)S(1)} %get-tuple-element.41), channel_id=1, source_target_pairs={{0,4},{1,5},{2,6},{3,7},{4,0},{5,1},{6,2},{7,3},{8,12},{9,13},{10,... | collective-permute-start | bytes 786440 | tf_op jit(solution)/shard_map/ppermute | solution.py:43
  7.0 7.1 %collective-permute-start.6 = (bf16[256,512]{1,0:T(8,128)(2,1)S(1)}, bf16[256,512]{1,0:T(8,128)(2,1)S(1)}, u32[]{:S(2)}, u32[]{:S(2)}) collective-permute-start(bf16[256,512]{1,0:T(8,128)(2,1)S(1)} %get-tuple-element.42), channel_id=1, source_target_pairs={{0,1},{1,0},{2,3},{3,2},{4,8},{5,9},{6,10},{7,11},{8,4},{9,5},{10,... | collective-permute-start | bytes 786440 | tf_op jit(solution)/shard_map/ppermute | solution.py:43
  7.9 7.9 %collective-permute-start.7 = (bf16[128,512]{1,0:T(8,128)(2,1)S(1)}, bf16[128,512]{1,0:T(8,128)(2,1)S(1)}, u32[]{:S(2)}, u32[]{:S(2)}) collective-permute-start(bf16[128,512]{1,0:T(8,128)(2,1)S(1)} %get-tuple-element.46), channel_id=1, source_target_pairs={{0,2},{1,3},{2,0},{3,1},{4,6},{5,7},{6,4},{7,5},{8,10},{9,11},{10,... | collective-permute-start | bytes 393224 | tf_op jit(solution)/shard_map/ppermute | solution.py:28
  11.8 9.1 %collective-permute-start.3 = (bf16[256,512]{1,0:T(8,128)(2,1)S(1)}, bf16[256,512]{1,0:T(8,128)(2,1)S(1)}, u32[]{:S(2)}, u32[]{:S(2)}) collective-permute-start(bf16[256,512]{1,0:T(8,128)(2,1)S(1)} %get-tuple-element.39), channel_id=1, source_target_pairs={{0,4},{1,5},{2,6},{3,7},{4,0},{5,1},{6,2},{7,3},{8,12},{9,13},{10,... | collective-permute-start | bytes 786440 | tf_op jit(solution)/shard_map/ppermute | solution.py:43
  13.5 7.4 %collective-permute-start.4 = (bf16[256,512]{1,0:T(8,128)(2,1)S(1)}, bf16[256,512]{1,0:T(8,128)(2,1)S(1)}, u32[]{:S(2)}, u32[]{:S(2)}) collective-permute-start(bf16[256,512]{1,0:T(8,128)(2,1)S(1)} %get-tuple-element.40), channel_id=1, source_target_pairs={{0,1},{1,0},{2,3},{3,2},{4,8},{5,9},{6,10},{7,11},{8,4},{9,5},{10,... | collective-permute-start | bytes 786440 | tf_op jit(solution)/shard_map/ppermute | solution.py:43
  14.1 6.7 %collective-permute-start.9 = (bf16[128,512]{1,0:T(8,128)(2,1)S(1)}, bf16[128,512]{1,0:T(8,128)(2,1)S(1)}, u32[]{:S(2)}, u32[]{:S(2)}) collective-permute-start(bf16[128,512]{1,0:T(8,128)(2,1)S(1)} %get-tuple-element.59), channel_id=1, source_target_pairs={{0,2},{1,3},{2,0},{3,1},{4,6},{5,7},{6,4},{7,5},{8,10},{9,11},{10,... | collective-permute-start | bytes 393224 | tf_op jit(solution)/shard_map/ppermute | solution.py:28
  16.4 6.2 %collective-permute-start.8 = (f32[8,256]{1,0:T(8,128)S(1)}, f32[8,256]{1,0:T(8,128)S(1)}, u32[]{:S(2)}, u32[]{:S(2)}) collective-permute-start(f32[8,256]{1,0:T(8,128)S(1)} %get-tuple-element.47.own_stats), channel_id=1, source_target_pairs={{4,0},{8,4},{12,8},{5,1},{9,5},{13,9},{6,2},{10,6},{14,10},{7,3},{... | collective-permute-start | bytes 24584 | tf_op jit(solution)/shard_map/ppermute | solution.py:48

commit v5 on v4

--- a/solution.py
+++ b/solution.py
@@ -9,6 +9,7 @@
 
 HEAD_DIM = 128
 GROUP = 4
+PAIR = 2
 
 masked_fill = -1e30
 score_scale = HEAD_DIM ** (-0.5)
@@ -43,11 +44,6 @@
     return lax.ppermute(rows, ("dp", "blk", "head"), route)
 
 
-def to_previous(rows):
-    blocks = lax.axis_size("blk")
-    return lax.ppermute(rows, "blk", [(i, i - 1) for i in range(1, blocks)])
-
-
 def is_even():
     return lax.rem(lax.axis_index("blk"), 2) == 0
 
@@ -263,19 +259,23 @@
         values, stats, tops, grown_t, slopes_t = rest[1 + sharers // 2 :]
         for step in range(sharers):
             values[place(step, rows), :] = values_in[step][...]
-        for head in range(heads):
-            columns = pl.ds(head * HEAD_DIM, HEAD_DIM)
-            scores = by_rows(k[:, columns], q[:, columns]) * exp2_scale + bias[...]
-            row_max = jnp.max(scores, axis=0, keepdims=True)
-            grown = jnp.exp2(scores - row_max)
-            total = jnp.sum(grown, axis=0, keepdims=True)
-            dchances = by_rows(values[:, columns], u[:, columns])
-            offset = jnp.sum(grown * dchances, axis=0, keepdims=True) / total
-            stats[pl.ds(head, 1), :] = row_max + jnp.log2(total)
-            stats[pl.ds(heads + head, 1), :] = offset
-            tops[pl.ds(head, 1), :] = row_max
-            grown_t[head] = grown.astype(jnp.bfloat16)
-            slopes_t[head] = (grown * (dchances - offset)).astype(jnp.bfloat16)
+        for start in range(0, heads, GROUP):
+            group = range(start, min(start + GROUP, heads))
+            cols = [pl.ds(head * HEAD_DIM, HEAD_DIM) for head in group]
+            scores = [by_rows(k[:, c], q[:, c]) * exp2_scale + bias[...] for c in cols]
+            maxes = [jnp.max(x, axis=0, keepdims=True) for x in scores]
+            grown = [jnp.exp2(x - m) for x, m in zip(scores, maxes)]
+            totals = [jnp.sum(x, axis=0, keepdims=True) for x in grown]
+            dchances = [by_rows(values[:, c], u[:, c]) for c in cols]
+            offsets = [
+                jnp.sum(x * d, axis=0, keepdims=True) / total for x, d, total in zip(grown, dchances, totals)
+            ]
+            for n, head in enumerate(group):
+                stats[pl.ds(head, 1), :] = maxes[n] + jnp.log2(totals[n])
+                stats[pl.ds(heads + head, 1), :] = offsets[n]
+                tops[pl.ds(head, 1), :] = maxes[n]
+                grown_t[head] = grown[n].astype(jnp.bfloat16)
+                slopes_t[head] = (grown[n] * (dchances[n] - offsets[n])).astype(jnp.bfloat16)
 
     square = bf16(heads, block_rows, block_rows)
     return pl.pallas_call(
@@ -290,53 +290,73 @@
         in_specs=[VMEM] * (6 + sharers // 2),
         out_specs=[VMEM] * 5,
         compiler_params=pltpu.CompilerParams(vmem_limit_bytes=12 * 2**20),
-        cost_estimate=weighed(0),
+        cost_estimate=weighed(2e10),
         name="own_scores",
     )(keys, queries, upstream, bias, after, *chip_values, *far_values)
 
 
-def own_products(keys, values, grown_t, slopes_t, next_upstream):
+def own_products(keys, queries, upstream, values, grown_t, slopes_t, next_upstream):
     block_rows, width = keys.shape
     heads = width // HEAD_DIM
 
-    def kernel(k, v, grown_t, slopes_t, nu, summed, grown_keys, slope_keys, later):
+    def kernel(k, q, u, v, grown_t, slopes_t, nu, sums, slope_keys, query_t, up_t, later):
         for head in range(heads):
             columns = pl.ds(head * HEAD_DIM, HEAD_DIM)
             key, value = k[:, columns], v[:, columns]
-            both = by_columns(grown_t[head], jnp.concatenate([value, key], axis=1))
-            summed[:, columns] = both[:, :HEAD_DIM]
-            grown_keys[:, columns] = both[:, HEAD_DIM:]
-            slope_keys[:, columns] = by_columns(slopes_t[head], key)
+            sums[head] = by_columns(jnp.concatenate([value, key], axis=1), grown_t[head])
+            slope_keys[head] = by_columns(key, slopes_t[head])
+            query_t[head] = jnp.transpose(q[:, columns]).astype(jnp.float32)
+            up_t[head] = jnp.transpose(u[:, columns]).astype(jnp.float32)
             later[head] = by_rows(value, nu[:, columns])
 
-    wide = jax.ShapeDtypeStruct((block_rows, width), jnp.float32)
-    return pl.pallas_call(
-        kernel,
-        out_shape=[wide, wide, wide, jax.ShapeDtypeStruct((heads, block_rows, block_rows), jnp.float32)],
-        in_specs=[VMEM] * 5,
-        out_specs=[VMEM] * 4,
+    def turned(tall):
+        return jax.ShapeDtypeStruct((heads, tall, block_rows), jnp.float32)
+
+    return pl.pallas_call(
+        kernel,
+        out_shape=[turned(2 * HEAD_DIM)] + [turned(HEAD_DIM)] * 3 + [turned(block_rows)],
+        in_specs=[VMEM] * 7,
+        out_specs=[VMEM] * 5,
         compiler_params=pltpu.CompilerParams(vmem_limit_bytes=16 * 2**20),
-        cost_estimate=weighed(2e10),
+        cost_estimate=weighed(0),
         name="own_products",
-    )(keys, values, grown_t, slopes_t, next_upstream)
-
-
-def past_keys(queries, upstream, first_got, second_got, stats, own, previous_values, past_bias):
+    )(keys, queries, upstream, values, grown_t, slopes_t, next_upstream)
+
+
+def past_dchances(upstream, previous_values):
     pairs = len(previous_values)
-    block_rows, width = queries.shape
+    block_rows, width = upstream.shape
     rows = block_rows // pairs // 2
     heads = width // HEAD_DIM
 
+    def kernel(u, *rest):
+        pieces, (values, dchances) = rest[:pairs], rest[pairs:]
+        for step in range(2 * pairs):
+            values[place(step, rows), :] = pieces[step // 2][pl.ds(step % 2 * rows, rows), :]
+        for head in range(heads):
+            columns = pl.ds(head * HEAD_DIM, HEAD_DIM)
+            dchances[head] = by_rows(values[:, columns], u[:, columns])
+
+    return pl.pallas_call(
+        kernel,
+        out_shape=[bf16(block_rows, width), jax.ShapeDtypeStruct((heads, block_rows, block_rows), jnp.float32)],
+        in_specs=[VMEM] * (1 + pairs),
+        out_specs=[VMEM] * 2,
+        compiler_params=small_kernel(),
+        cost_estimate=weighed(0),
+        name="past_dchances",
+    )(upstream, *previous_values)
+
+
+def past_keys(queries, first_got, second_got, stats, tops, own, past_values, dchances, past_bias):
+    block_rows, width = queries.shape
+    heads = width // HEAD_DIM
+
     def kernel(
-        q, u, first, second, own_stats, tops, grown_t, slopes_t, summed, grown_keys, slope_keys, past_bias, *rest
+        q, first, second, own_stats, tops, sums, slope_keys, query_t, up_t, pv, dchances, past_bias,
+        attended, query_grads, scaled_query, shifted_query, scaled_up
     ):
-        pieces = rest[:pairs]
-        attended, query_grads, key_part, value_part, pv, factors = rest[pairs:]
         even = is_even()
-        for step in range(2 * pairs):
-            pv[place(step, rows), :] = pieces[step // 2][pl.ds(step % 2 * rows, rows), :]
-        factors[...] = jnp.zeros(factors.shape, jnp.float32)
-
         for start in range(0, heads, GROUP):
             group = range(start, min(start + GROUP, heads))
             cols = [pl.ds(head * HEAD_DIM, HEAD_DIM) for head in group]
@@ -348,88 +368,87 @@
             grown = [jnp.exp2(x - m) for x, m in zip(scores, maxes)]
             own = [jnp.exp2(own_stats[pl.ds(head, 1), :] - m) for head, m in zip(group, maxes)]
             shares = [1.0 / (o + jnp.sum(x, axis=0, keepdims=True)) for o, x in zip(own, grown)]
-            dchances = [by_rows(pv[:, c], u[:, c]) for c in cols]
             offsets = [
-                y * (own_stats[pl.ds(heads + head, 1), :] * o + jnp.sum(x * d, axis=0, keepdims=True))
-                for head, o, x, y, d in zip(group, own, grown, shares, dchances)
-            ]
-            for n, head in enumerate(group):
-                factor = jnp.exp2(tops[pl.ds(head, 1), :] - maxes[n]) * shares[n]
-                factors[pl.ds(head, 1), :] = factor
-                factors[pl.ds(heads + head, 1), :] = factor * (offsets[n] - own_stats[pl.ds(heads + head, 1), :])
+                y * (own_stats[pl.ds(heads + head, 1), :] * o + jnp.sum(x * dchances[head], axis=0, keepdims=True))
+                for head, o, x, y in zip(group, own, grown, shares)
+            ]
+            factors = [jnp.exp2(tops[pl.ds(head, 1), :] - m) * y for head, m, y in zip(group, maxes, shares)]
+            shifts = [
+                f * (o - own_stats[pl.ds(heads + head, 1), :]) for head, f, o in zip(group, factors, offsets)
+            ]
             chances = [x * y for x, y in zip(grown, shares)]
             weights = [x.astype(jnp.bfloat16) for x in chances]
-            dscores = [(x * (d - o)).astype(jnp.bfloat16) for x, d, o in zip(chances, dchances, offsets)]
-            turned = jnp.transpose(factors[...])
+            dscores = [(x * (dchances[head] - o)).astype(jnp.bfloat16) for x, head, o in zip(chances, group, offsets)]
             for n, (head, c) in enumerate(zip(group, cols)):
-                factor, shift = turned[:, head : head + 1], turned[:, heads + head : heads + head + 1]
-                attended[:, c] = (factor * summed[:, c] + by_columns(weights[n], pv[:, c])).astype(jnp.bfloat16)
-                query_grads[:, c] = (
-                    score_scale * (factor * slope_keys[:, c] - shift * grown_keys[:, c] + by_columns(dscores[n], keys[n]))
-                ).astype(jnp.bfloat16)
-                wide_query = q[:, c].astype(jnp.float32)
-                scaled_query = (wide_query * factor).astype(jnp.bfloat16)
-                shifted_query = (wide_query * shift).astype(jnp.bfloat16)
-                scaled_up = (u[:, c].astype(jnp.float32) * factor).astype(jnp.bfloat16)
-                key_part[:, c] = product(slopes_t[head], scaled_query) - product(grown_t[head], shifted_query)
-                value_part[:, c] = product(grown_t[head], scaled_up)
-
-    wide = jax.ShapeDtypeStruct((block_rows, width), jnp.float32)
-    return pl.pallas_call(
-        kernel,
-        out_shape=[bf16(block_rows, width)] * 2 + [wide] * 2,
-        in_specs=[VMEM] * (12 + pairs),
-        out_specs=[VMEM] * 4,
-        scratch_shapes=[
-            pltpu.VMEM((block_rows, width), jnp.bfloat16),
-            pltpu.VMEM((HEAD_DIM, block_rows), jnp.float32),
-        ],
+                factor, shift = factors[n], shifts[n]
+                attended_t = factor * sums[head, :HEAD_DIM] + by_columns(pv[:, c], weights[n])
+                attended[:, c] = jnp.transpose(attended_t.astype(jnp.bfloat16))
+                grads_t = (
+                    factor * slope_keys[head] - shift * sums[head, HEAD_DIM:] + by_columns(keys[n], dscores[n])
+                )
+                query_grads[:, c] = jnp.transpose((score_scale * grads_t).astype(jnp.bfloat16))
+                scaled_query[head] = (query_t[head] * factor).astype(jnp.bfloat16)
+                shifted_query[head] = (query_t[head] * -shift).astype(jnp.bfloat16)
+                scaled_up[head] = (up_t[head] * factor).astype(jnp.bfloat16)
+
+    return pl.pallas_call(
+        kernel,
+        out_shape=[bf16(block_rows, width)] * 2 + [bf16(heads, HEAD_DIM, block_rows)] * 3,
+        in_specs=[VMEM] * 12,
+        out_specs=[VMEM] * 5,
         compiler_params=pltpu.CompilerParams(vmem_limit_bytes=20 * 2**20),
         cost_estimate=weighed(0),
         name="past_keys",
-    )(queries, upstream, first_got, second_got, stats, *own, past_bias, *previous_values)
-
-
-def next_rows(keys, first_got, second_got, next_upstream, next_stats, later, next_bias, done, parts):
+    )(queries, first_got, second_got, stats, tops, *own, past_values, dchances, past_bias)
+
+
+def next_rows(
+    keys, first_got, second_got, next_upstream, first_stats, second_stats, later, next_bias, grown_t, slopes_t,
+    done, scaled
+):
     block_rows, width = keys.shape
     heads = width // HEAD_DIM
 
-    def kernel(k, first, second, nu, stats, later, next_bias, attended, query_grads, key_part, value_part, *rest):
+    def kernel(
+        k, first, second, nu, first_stats, second_stats, later, next_bias, grown_t, slopes_t,
+        attended, query_grads, scaled_query, shifted_query, scaled_up, *rest
+    ):
         outs, (key_grads, value_grads, sems) = rest[:4], rest[4:]
         copies = [pltpu.make_async_copy(source, outs[i], sems.at[i]) for i, source in enumerate((attended, query_grads))]
         for c in copies:
             c.start()
         even = is_even()
-        for start in range(0, heads, GROUP):
-            group = range(start, min(start + GROUP, heads))
+        stats = jnp.where(even, first_stats[...], second_stats[...])
+        for start in range(0, heads, PAIR):
+            group = range(start, min(start + PAIR, heads))
             cols = [pl.ds(head * HEAD_DIM, HEAD_DIM) for head in group]
             queries = [jnp.where(even, first[:, c], second[:, c]) for c in cols]
             scores = [by_rows(k[:, c], query) * exp2_scale + next_bias[...] for c, query in zip(cols, queries)]
-            maxes = [jnp.max(x, axis=0, keepdims=True) for x in scores]
+            mixed = [
+                by_rows(grown_t[head], jnp.concatenate([scaled_up[head], shifted_query[head]], axis=0)) for head in group
+            ]
+            sloped = [by_rows(slopes_t[head], scaled_query[head]) for head in group]
+            far = [stats[head : head + 1] for head in group]
+            maxes = [jnp.maximum(f, jnp.max(x, axis=0, keepdims=True)) for f, x in zip(far, scores)]
             grown = [jnp.exp2(x - m) for x, m in zip(scores, maxes)]
-            totals = [jnp.sum(x, axis=0, keepdims=True) for x in grown]
+            far = [jnp.exp2(f - m) for f, m in zip(far, maxes)]
+            shares = [1.0 / (f + jnp.sum(x, axis=0, keepdims=True)) for f, x in zip(far, grown)]
             offsets = [
-                jnp.sum(x * later[head], axis=0, keepdims=True) / total
-                for x, head, total in zip(grown, group, totals)
-            ]
-            scales = []
-            for n, head in enumerate(group):
-                far_norm, far_offset = stats[pl.ds(head, 1), :], stats[pl.ds(heads + head, 1), :]
-                near_norm = maxes[n] + jnp.log2(totals[n])
-                top = jnp.maximum(far_norm, near_norm)
-                far_part, near_part = jnp.exp2(far_norm - top), jnp.exp2(near_norm - top)
-                whole = 1.0 / (far_part + near_part)
-                offsets[n] = (far_part * far_offset + near_part * offsets[n]) * whole
-                scales.append(jnp.exp2(maxes[n] - top) * whole)
-            chances = [x * y for x, y in zip(grown, scales)]
+                y * (stats[heads + head : heads + head + 1] * f + jnp.sum(x * later[head], axis=0, keepdims=True))
+                for head, f, x, y in zip(group, far, grown, shares)
+            ]
+            chances = [x * y for x, y in zip(grown, shares)]
             weights = [x.astype(jnp.bfloat16) for x in chances]
             dscores = [
                 (x * (later[head] - offset)).astype(jnp.bfloat16)
                 for x, head, offset in zip(chances, group, offsets)
             ]
-            for n, c in enumerate(cols):
-                key_grads[:, c] = (score_scale * (key_part[:, c] + product(dscores[n], queries[n]))).astype(jnp.bfloat16)
-                value_grads[:, c] = (value_part[:, c] + product(weights[n], nu[:, c])).astype(jnp.bfloat16)
+            for n, (head, c) in enumerate(zip(group, cols)):
+                value_grads[:, c] = (mixed[n][:, :HEAD_DIM] + product(weights[n], nu[:, c])).astype(jnp.bfloat16)
+                key_grads[:, c] = (
+                    score_scale
+                    * (mixed[n][:, HEAD_DIM:] + sloped[n] + product(dscores[n], queries[n]))
+                ).astype(jnp.bfloat16)
             wide = pl.ds(start * HEAD_DIM, len(group) * HEAD_DIM)
             for i, source in ((2, key_grads), (3, value_grads)):
                 copies.append(pltpu.make_async_copy(source.at[:, wide], outs[i].at[:, wide], sems.at[len(copies)]))
@@ -440,13 +459,16 @@
     return pl.pallas_call(
         kernel,
         out_shape=[bf16(block_rows, width)] * 4,
-        in_specs=[VMEM] * 11,
+        in_specs=[VMEM] * 15,
         out_specs=[ANY] * 4,
         scratch_shapes=[pltpu.VMEM((block_rows, width), jnp.bfloat16)] * 2
         + [pltpu.SemaphoreType.DMA((2 + 2 * heads,))],
         compiler_params=pltpu.CompilerParams(vmem_limit_bytes=16 * 2**20),
         name="next_rows",
-    )(keys, first_got, second_got, next_upstream, next_stats, later, next_bias, *done, *parts)
+    )(
+        keys, first_got, second_got, next_upstream, first_stats, second_stats, later, next_bias, grown_t, slopes_t,
+        *done, *scaled,
+    )
 
 
 def on_device(queries, key_states, value_states, upstream, clip_lengths):
@@ -465,16 +487,16 @@
     values, stats, tops, grown_t, slopes_t = own_scores(
         keys, query_rows, pieces[:2], far_values, upstream, own_bias, next_upstream
     )
-    next_stats = to_previous(stats)
-    summed, grown_keys, slope_keys, later = own_products(keys, values, grown_t, slopes_t, next_upstream)
-    own = (tops, grown_t, slopes_t, summed, grown_keys, slope_keys)
-    attended, query_grads, key_part, value_part = past_keys(
-        query_rows, upstream, first_got, second_got, stats, own, previous, past_bias
+    first_stats, second_stats = block_exchange(stats, 0), block_exchange(stats, 1)
+    *own, later = own_products(keys, query_rows, upstream, values, grown_t, slopes_t, next_upstream)
+    past_values, dchances = past_dchances(upstream, previous)
+    attended, query_grads, *scaled = past_keys(
+        query_rows, first_got, second_got, stats, tops, own, past_values, dchances, past_bias
     )
     return tuple(
         next_rows(
-            keys, first_got, second_got, next_upstream, next_stats, later, next_bias,
-            (attended, query_grads), (key_part, value_part),
+            keys, first_got, second_got, next_upstream, first_stats, second_stats, later, next_bias, grown_t,
+            slopes_t, (attended, query_grads), scaled,
         )
     )
 

time: 25 us -> 24.4 us (0.976)
  waiting for transfers between devices: 4.78 us -> 3.27 us
  starting transfers between devices: 11.8 us -> 13.2 us
  Pallas kernels: 7.23 us -> 6.82 us
    ppermute x4 -> x6, starting transfers between devices: 4.27 us -> 6.97 us  [block_exchange(): return lax.ppermute(rows, ('dp', 'blk', 'head'), route)]
    ppermute x4 -> x6, waiting for transfers between devices: 2.5 us -> 0.99 us  [block_exchange(): return lax.ppermute(rows, ('dp', 'blk', 'head'), route)]
    ppermute x1 -> x0, starting transfers between devices: 1.29 us -> none  [to_previous(): return lax.ppermute(rows, 'blk', [(i, i - 1) for i in range(1, blocks)])]
    pallas_call x2 -> x3, Pallas kernels: 2.39 us -> 1.95 us  [the longest x1 1.11 us: past_keys(): pl.pallas_call(kernel, out_shape=[bf16(block_rows, width)] * 2 + [bf16(he...]
  transfers between devices with their start and end apart: 10 -> 11, of which waited for: 2 -> 2; matrix products, arithmetic and copies ran while one was open for 0% -> 0% of each run, Pallas kernels for 16% -> 15%
where the time goes in v5:
time: 24.4 us; the launch traced here: 24.1 us
  starting transfers between devices  13.2 us (54%)
  Pallas kernels  6.82 us (28%)
  waiting for transfers between devices  3.27 us (13%)
  between operations  0.74 us (3%)
    ppermute x6, starting transfers between devices, block_exchange(): return lax.ppermute(rows, ('dp', 'blk', 'head'), route)  6.97 us
    ppermute x5, starting transfers between devices, partner_exchange(): return lax.ppermute(rows, 'head', route)  6.26 us
    ppermute x5, waiting for transfers between devices, partner_exchange(): return lax.ppermute(rows, 'head', route)  2.28 us
    pallas_call x1, Pallas kernels, next_rows(): pl.pallas_call(kernel, out_shape=[bf16(block_rows, width)] * 4, in_specs=...  2 us
    pallas_call x1, Pallas kernels, cut_pieces(): pl.pallas_call(kernel, out_shape=[bf16(height, width) for height in heigh...  1.31 us
    pallas_call x1, Pallas kernels, past_keys(): pl.pallas_call(kernel, out_shape=[bf16(block_rows, width)] * 2 + [bf16(he...  1.11 us
    ppermute x6, waiting for transfers between devices, block_exchange(): return lax.ppermute(rows, ('dp', 'blk', 'head'), route)  0.99 us
    pallas_call x1, Pallas kernels, stack_far_values(): pl.pallas_call(kernel, out_shape=[jax.ShapeDtypeStruct((block_rows, block...  0.73 us
  transfers between devices with their start and end apart: 11, of which 2 were waited for; matrix products, arithmetic and copies ran while one was open for 0% of the time, Pallas kernels for 15%

profile of v5, /device:TPU:0, one launch (start us, length us, event | category | flops | bytes accessed | tf_op | source)
XLA Modules:
  0.0 24.1 jit_solution(11834269966068755431)
XLA Ops:
  0.6 0.0 copy-start
  0.6 1.3 %cut_pieces.1 = (bf16[256,512]{1,0:T(8,128)(2,1)S(1)}, bf16[256,512]{1,0:T(8,128)(2,1)S(1)}, bf16[128,512]{1,0:T(8,128)(2,1)S(1)}, bf16[128,512]{1,0:T(8,128)(2,1)S(1)}) custom-call(bf16[64,2048]{1,0:T(8,128)(2,1)} %q.1, bf16[64,2048]{1,0:T(8,128)(2,1)} %k.1, bf16[64,2048]{1,0:T(8,128)(2,1)} %v.1), custom_call_target="tpu_custom_call" | custom-call | tf_op jit(solution)/shard_map/cut_pieces/pallas_call | solution.py:87
  2.0 0.5 %collective-permute-start = (bf16[256,512]{1,0:T(8,128)(2,1)S(1)}, bf16[256,512]{1,0:T(8,128)(2,1)S(1)}, u32[]{:S(2)}, u32[]{:S(2)}) collective-permute-start(bf16[256,512]{1,0:T(8,128)(2,1)S(1)} %get-tuple-element.39), channel_id=1, source_target_pairs={{0,1},{1,0},{2,3},{3,2},{4,5},{5,4},{6,7},{7,6},{8,9},{9,8},{10,11... | collective-permute-start | bytes 786440 | tf_op jit(solution)/shard_map/ppermute | solution.py:29
  2.5 2.6 %collective-permute-start.1 = (bf16[128,512]{1,0:T(8,128)(2,1)S(1)}, bf16[128,512]{1,0:T(8,128)(2,1)S(1)}, u32[]{:S(2)}, u32[]{:S(2)}) collective-permute-start(bf16[128,512]{1,0:T(8,128)(2,1)S(1)} %get-tuple-element.40), channel_id=1, source_target_pairs={{0,2},{1,3},{2,0},{3,1},{4,6},{5,7},{6,4},{7,5},{8,10},{9,11},{10,... | collective-permute-start | bytes 393224 | tf_op jit(solution)/shard_map/ppermute | solution.py:29
  5.0 0.1 collective-permute-start.2
  5.1 0.0 collective-permute-done.refs_1_.theirs.rest_1_
  5.1 0.0 copy-done
  5.2 0.0 copy-start.1
  5.2 1.9 %collective-permute-start.5 = (bf16[256,512]{1,0:T(8,128)(2,1)S(1)}, bf16[256,512]{1,0:T(8,128)(2,1)S(1)}, u32[]{:S(2)}, u32[]{:S(2)}) collective-permute-start(bf16[256,512]{1,0:T(8,128)(2,1)S(1)} %get-tuple-element.45), channel_id=1, source_target_pairs={{0,4},{1,5},{2,6},{3,7},{4,0},{5,1},{6,2},{7,3},{8,12},{9,13},{10,... | collective-permute-start | bytes 786440 | tf_op jit(solution)/shard_map/ppermute | solution.py:44
  7.0 0.1 collective-permute-start.6
  7.1 0.0 copy-done.1
  7.1 0.7 %stack_far_values.1 = (f32[256,256]{1,0:T(8,128)S(1)}, f32[256,256]{1,0:T(8,128)S(1)}, f32[256,256]{1,0:T(8,128)S(1)}, bf16[128,512]{1,0:T(8,128)(2,1)S(1)}) custom-call(bf16[256,512]{1,0:T(8,128)(2,1)S(1)} %get-tuple-element.38.refs_0_.mine.rest_0_, bf16[256,512]{1,0:T(8,128)(2,1)S(1)} %collective-permute-done.refs_1_.theirs.rest_1_, s32[4]{0:T(128)S(1)} %copy-done.1), custom_call_target="tpu_custom_call" | custom-call | flops 5000000000 | tf_op jit(solution)/shard_map/stack_far_values/pallas_call | solution.py:115
  7.9 1.6 %collective-permute-start.7 = (bf16[128,512]{1,0:T(8,128)(2,1)S(1)}, bf16[128,512]{1,0:T(8,128)(2,1)S(1)}, u32[]{:S(2)}, u32[]{:S(2)}) collective-permute-start(bf16[128,512]{1,0:T(8,128)(2,1)S(1)} %get-tuple-element.50), channel_id=1, source_target_pairs={{0,2},{1,3},{2,0},{3,1},{4,6},{5,7},{6,4},{7,5},{8,10},{9,11},{10,... | collective-permute-start | bytes 393224 | tf_op jit(solution)/shard_map/ppermute | solution.py:29
  9.4 0.0 collective-permute-done.1.refs_2_
  9.4 2.3 %collective-permute-done.2.refs_3_ = bf16[128,512]{1,0:T(8,128)(2,1)S(1)} collective-permute-done((bf16[128,512]{1,0:T(8,128)(2,1)S(1)}, bf16[128,512]{1,0:T(8,128)(2,1)S(1)}, u32[]{:S(2)}, u32[]{:S(2)}) %collective-permute-start.2) | collective-permute-done | bytes 131104 | tf_op jit(solution)/shard_map/ppermute | solution.py:29
  11.7 0.1 join_keys_queries.1
  11.8 1.7 %collective-permute-start.3 = (bf16[256,512]{1,0:T(8,128)(2,1)S(1)}, bf16[256,512]{1,0:T(8,128)(2,1)S(1)}, u32[]{:S(2)}, u32[]{:S(2)}) collective-permute-start(bf16[256,512]{1,0:T(8,128)(2,1)S(1)} %get-tuple-element.43), channel_id=1, source_target_pairs={{0,4},{1,5},{2,6},{3,7},{4,0},{5,1},{6,2},{7,3},{8,12},{9,13},{10,... | collective-permute-start | bytes 786440 | tf_op jit(solution)/shard_map/ppermute | solution.py:44
  13.5 0.6 %collective-permute-start.4 = (bf16[256,512]{1,0:T(8,128)(2,1)S(1)}, bf16[256,512]{1,0:T(8,128)(2,1)S(1)}, u32[]{:S(2)}, u32[]{:S(2)}) collective-permute-start(bf16[256,512]{1,0:T(8,128)(2,1)S(1)} %get-tuple-element.44), channel_id=1, source_target_pairs={{0,1},{1,0},{2,3},{3,2},{4,8},{5,9},{6,10},{7,11},{8,4},{9,5},{10,... | collective-permute-start | bytes 786440 | tf_op jit(solution)/shard_map/ppermute | solution.py:44
  14.1 0.0 collective-permute-done.5.first
  14.1 0.0 collective-permute-done.6.second
  14.1 1.6 %collective-permute-start.10 = (bf16[128,512]{1,0:T(8,128)(2,1)S(1)}, bf16[128,512]{1,0:T(8,128)(2,1)S(1)}, u32[]{:S(2)}, u32[]{:S(2)}) collective-permute-start(bf16[128,512]{1,0:T(8,128)(2,1)S(1)} %get-tuple-element.63), channel_id=1, source_target_pairs={{0,2},{1,3},{2,0},{3,1},{4,6},{5,7},{6,4},{7,5},{8,10},{9,11},{10,... | collective-permute-start | bytes 393224 | tf_op jit(solution)/shard_map/ppermute | solution.py:29
  15.7 0.0 collective-permute-done.7.rest_2_
  15.7 0.7 %own_scores.1 = (bf16[256,512]{1,0:T(8,128)(2,1)S(1)}, f32[8,256]{1,0:T(8,128)S(1)}, f32[4,256]{1,0:T(4,128)S(1)}, bf16[4,256,256]{2,1,0:T(8,128)(2,1)S(1)}, bf16[4,256,256]{2,1,0:T(8,128)(2,1)S(1)}) custom-call(bf16[256,512]{1,0:T(8,128)(2,1)S(1)} %get-tuple-element.42.k, bf16[256,512]{1,0:T(8,128)(2,1)S(1)} %get-tuple-element.48.q, ...), custom_call_target="tpu_custom_call" | custom-call | flops 20000000000 | tf_op jit(solution)/shard_map/own_scores/pallas_call | solution.py:281
  16.4 2.7 %collective-permute-start.8 = (f32[8,256]{1,0:T(8,128)S(1)}, f32[8,256]{1,0:T(8,128)S(1)}, u32[]{:S(2)}, u32[]{:S(2)}) collective-permute-start(f32[8,256]{1,0:T(8,128)S(1)} %get-tuple-element.51.own_stats), channel_id=1, source_target_pairs={{0,4},{1,5},{2,6},{3,7},{4,0},{5,1},{6,2},{7,3},{8,12},{9,13},{10,... | collective-permute-start | bytes 24584 | tf_op jit(solution)/shard_map/ppermute | solution.py:44
  19.1 0.0 collective-permute-start.9
  19.1 0.5 %own_products.1 = (f32[4,256,256]{2,1,0:T(8,128)S(1)}, f32[4,128,256]{2,1,0:T(8,128)S(1)}, f32[4,128,256]{2,1,0:T(8,128)S(1)}, f32[4,128,256]{2,1,0:T(8,128)S(1)}, f32[4,256,256]{2,1,0:T(8,128)S(1)}) custom-call(bf16[256,512]{1,0:T(8,128)(2,1)S(1)} %get-tuple-element.42.k, bf16[256,512]{1,0:T(8,128)(2,1)S(1)} %get-tuple-element.48.q, ...), custom_call_target="tpu_custom_call" | custom-call | tf_op jit(solution)/shard_map/own_products/pallas_call | solution.py:315
  19.6 0.0 collective-permute-done.10.rest_1_
  19.7 0.3 %past_dchances.1 = (bf16[256,512]{1,0:T(8,128)(2,1)S(1)}, f32[4,256,256]{2,1,0:T(8,128)S(1)}) custom-call(bf16[256,512]{1,0:T(8,128)(2,1)S(1)} %copy-done, bf16[128,512]{1,0:T(8,128)(2,1)S(1)} %get-tuple-element.62.rest_0_, bf16[128,512]{1,0:T(8,128)(2,1)S(1)} %collective-permute-done.10.rest_1_), custom_call_target="tpu_custom_call" | custom-call | tf_op jit(solution)/shard_map/past_dchances/pallas_call | solution.py:340
  20.0 1.0 %collective-permute-done.3.first = bf16[256,512]{1,0:T(8,128)(2,1)S(1)} collective-permute-done((bf16[256,512]{1,0:T(8,128)(2,1)S(1)}, bf16[256,512]{1,0:T(8,128)(2,1)S(1)}, u32[]{:S(2)}, u32[]{:S(2)}) %collective-permute-start.3) | collective-permute-done | bytes 262176 | tf_op jit(solution)/shard_map/ppermute | solution.py:44
  20.9 0.0 collective-permute-done.4.second
  20.9 1.1 %past_keys.1 = (bf16[256,512]{1,0:T(8,128)(2,1)S(1)}, bf16[256,512]{1,0:T(8,128)(2,1)S(1)}, bf16[4,128,256]{2,1,0:T(8,128)(2,1)S(1)}, bf16[4,128,256]{2,1,0:T(8,128)(2,1)S(1)}, bf16[4,128,256]{2,1,0:T(8,128)(2,1)S(1)}) custom-call(bf16[256,512]{1,0:T(8,128)(2,1)S(1)} %get-tuple-element.48.q, bf16[256,512]{1,0:T(8,128)(2,1)S(1)} %collective-permute-done.3.first, ...), custom_call_target="tpu_custom_call" | custom-call | tf_op jit(solution)/shard_map/past_keys/pallas_call | solution.py:394
  22.1 0.0 collective-permute-done.8.first_stats
  22.1 0.0 collective-permute-done.9.second_stats
  22.1 2.0 %next_rows.1 = (bf16[256,512]{1,0:T(8,128)(2,1)}, bf16[256,512]{1,0:T(8,128)(2,1)}, bf16[256,512]{1,0:T(8,128)(2,1)}, bf16[256,512]{1,0:T(8,128)(2,1)}) custom-call(bf16[256,512]{1,0:T(8,128)(2,1)S(1)} %get-tuple-element.42.k, bf16[256,512]{1,0:T(8,128)(2,1)S(1)} %collective-permute-done.3.first, bf16[256,512]{1,0:T(8,128)(2,1)S(1)} %collective-permute-done.4.second, ...), custom_call_target="tpu_custom_call" | custom-call | tf_op jit(solution)/shard_map/next_rows/pallas_call | solution.py:459
  (2 shorter events, 0.1 us)
Async XLA Ops:
  0.6 4.5 %copy-start = (bf16[256,512]{1,0:T(8,128)(2,1)S(1)}, bf16[256,512]{1,0:T(8,128)(2,1)}, u32[]{:S(2)}) copy-start(bf16[256,512]{1,0:T(8,128)(2,1)} %u.7) | copy-start | bytes 786436
  2.0 3.2 %collective-permute-start = (bf16[256,512]{1,0:T(8,128)(2,1)S(1)}, bf16[256,512]{1,0:T(8,128)(2,1)S(1)}, u32[]{:S(2)}, u32[]{:S(2)}) collective-permute-start(bf16[256,512]{1,0:T(8,128)(2,1)S(1)} %get-tuple-element.39), channel_id=1, source_target_pairs={{0,1},{1,0},{2,3},{3,2},{4,5},{5,4},{6,7},{7,6},{8,9},{9,8},{10,11... | collective-permute-start | bytes 786440 | tf_op jit(solution)/shard_map/ppermute | solution.py:29
  2.5 6.9 %collective-permute-start.1 = (bf16[128,512]{1,0:T(8,128)(2,1)S(1)}, bf16[128,512]{1,0:T(8,128)(2,1)S(1)}, u32[]{:S(2)}, u32[]{:S(2)}) collective-permute-start(bf16[128,512]{1,0:T(8,128)(2,1)S(1)} %get-tuple-element.40), channel_id=1, source_target_pairs={{0,2},{1,3},{2,0},{3,1},{4,6},{5,7},{6,4},{7,5},{8,10},{9,11},{10,... | collective-permute-start | bytes 393224 | tf_op jit(solution)/shard_map/ppermute | solution.py:29
  5.0 6.6 %collective-permute-start.2 = (bf16[128,512]{1,0:T(8,128)(2,1)S(1)}, bf16[128,512]{1,0:T(8,128)(2,1)S(1)}, u32[]{:S(2)}, u32[]{:S(2)}) collective-permute-start(bf16[128,512]{1,0:T(8,128)(2,1)S(1)} %get-tuple-element.41), channel_id=1, source_target_pairs={{0,3},{1,2},{2,1},{3,0},{4,7},{5,6},{6,5},{7,4},{8,11},{9,10},{10,... | collective-permute-start | bytes 393224 | tf_op jit(solution)/shard_map/ppermute | solution.py:29
  5.2 2.0 %copy-start.1 = (s32[4]{0:T(128)S(1)}, s32[4]{0:T(128)}, u32[]{:S(2)}) copy-start(s32[4]{0:T(128)} %lengths.1) | copy-start | bytes 52
  5.2 8.9 %collective-permute-start.5 = (bf16[256,512]{1,0:T(8,128)(2,1)S(1)}, bf16[256,512]{1,0:T(8,128)(2,1)S(1)}, u32[]{:S(2)}, u32[]{:S(2)}) collective-permute-start(bf16[256,512]{1,0:T(8,128)(2,1)S(1)} %get-tuple-element.45), channel_id=1, source_target_pairs={{0,4},{1,5},{2,6},{3,7},{4,0},{5,1},{6,2},{7,3},{8,12},{9,13},{10,... | collective-permute-start | bytes 786440 | tf_op jit(solution)/shard_map/ppermute | solution.py:44
  7.0 7.1 %collective-permute-start.6 = (bf16[256,512]{1,0:T(8,128)(2,1)S(1)}, bf16[256,512]{1,0:T(8,128)(2,1)S(1)}, u32[]{:S(2)}, u32[]{:S(2)}) collective-permute-start(bf16[256,512]{1,0:T(8,128)(2,1)S(1)} %get-tuple-element.46), channel_id=1, source_target_pairs={{0,1},{1,0},{2,3},{3,2},{4,8},{5,9},{6,10},{7,11},{8,4},{9,5},{10,... | collective-permute-start | bytes 786440 | tf_op jit(solution)/shard_map/ppermute | solution.py:44
  7.9 7.9 %collective-permute-start.7 = (bf16[128,512]{1,0:T(8,128)(2,1)S(1)}, bf16[128,512]{1,0:T(8,128)(2,1)S(1)}, u32[]{:S(2)}, u32[]{:S(2)}) collective-permute-start(bf16[128,512]{1,0:T(8,128)(2,1)S(1)} %get-tuple-element.50), channel_id=1, source_target_pairs={{0,2},{1,3},{2,0},{3,1},{4,6},{5,7},{6,4},{7,5},{8,10},{9,11},{10,... | collective-permute-start | bytes 393224 | tf_op jit(solution)/shard_map/ppermute | solution.py:29
  11.8 9.2 %collective-permute-start.3 = (bf16[256,512]{1,0:T(8,128)(2,1)S(1)}, bf16[256,512]{1,0:T(8,128)(2,1)S(1)}, u32[]{:S(2)}, u32[]{:S(2)}) collective-permute-start(bf16[256,512]{1,0:T(8,128)(2,1)S(1)} %get-tuple-element.43), channel_id=1, source_target_pairs={{0,4},{1,5},{2,6},{3,7},{4,0},{5,1},{6,2},{7,3},{8,12},{9,13},{10,... | collective-permute-start | bytes 786440 | tf_op jit(solution)/shard_map/ppermute | solution.py:44
  13.5 7.5 %collective-permute-start.4 = (bf16[256,512]{1,0:T(8,128)(2,1)S(1)}, bf16[256,512]{1,0:T(8,128)(2,1)S(1)}, u32[]{:S(2)}, u32[]{:S(2)}) collective-permute-start(bf16[256,512]{1,0:T(8,128)(2,1)S(1)} %get-tuple-element.44), channel_id=1, source_target_pairs={{0,1},{1,0},{2,3},{3,2},{4,8},{5,9},{6,10},{7,11},{8,4},{9,5},{10,... | collective-permute-start | bytes 786440 | tf_op jit(solution)/shard_map/ppermute | solution.py:44
  14.1 5.5 %collective-permute-start.10 = (bf16[128,512]{1,0:T(8,128)(2,1)S(1)}, bf16[128,512]{1,0:T(8,128)(2,1)S(1)}, u32[]{:S(2)}, u32[]{:S(2)}) collective-permute-start(bf16[128,512]{1,0:T(8,128)(2,1)S(1)} %get-tuple-element.63), channel_id=1, source_target_pairs={{0,2},{1,3},{2,0},{3,1},{4,6},{5,7},{6,4},{7,5},{8,10},{9,11},{10,... | collective-permute-start | bytes 393224 | tf_op jit(solution)/shard_map/ppermute | solution.py:29
  16.4 5.7 %collective-permute-start.8 = (f32[8,256]{1,0:T(8,128)S(1)}, f32[8,256]{1,0:T(8,128)S(1)}, u32[]{:S(2)}, u32[]{:S(2)}) collective-permute-start(f32[8,256]{1,0:T(8,128)S(1)} %get-tuple-element.51.own_stats), channel_id=1, source_target_pairs={{0,4},{1,5},{2,6},{3,7},{4,0},{5,1},{6,2},{7,3},{8,12},{9,13},{10,... | collective-permute-start | bytes 24584 | tf_op jit(solution)/shard_map/ppermute | solution.py:44
  19.1 3.0 %collective-permute-start.9 = (f32[8,256]{1,0:T(8,128)S(1)}, f32[8,256]{1,0:T(8,128)S(1)}, u32[]{:S(2)}, u32[]{:S(2)}) collective-permute-start(f32[8,256]{1,0:T(8,128)S(1)} %get-tuple-element.51.own_stats), channel_id=1, source_target_pairs={{0,1},{1,0},{2,3},{3,2},{4,8},{5,9},{6,10},{7,11},{8,4},{9,5},{10,... | collective-permute-start | bytes 24584 | tf_op jit(solution)/shard_map/ppermute | solution.py:44

commit v6 on v5

--- a/solution.py
+++ b/solution.py
@@ -290,7 +290,7 @@
         in_specs=[VMEM] * (6 + sharers // 2),
         out_specs=[VMEM] * 5,
         compiler_params=pltpu.CompilerParams(vmem_limit_bytes=12 * 2**20),
-        cost_estimate=weighed(2e10),
+        cost_estimate=weighed(0),
         name="own_scores",
     )(keys, queries, upstream, bias, after, *chip_values, *far_values)
 
@@ -318,7 +318,7 @@
         in_specs=[VMEM] * 7,
         out_specs=[VMEM] * 5,
         compiler_params=pltpu.CompilerParams(vmem_limit_bytes=16 * 2**20),
-        cost_estimate=weighed(0),
+        cost_estimate=weighed(1e9),
         name="own_products",
     )(keys, queries, upstream, values, grown_t, slopes_t, next_upstream)
 
@@ -343,131 +343,195 @@
         in_specs=[VMEM] * (1 + pairs),
         out_specs=[VMEM] * 2,
         compiler_params=small_kernel(),
-        cost_estimate=weighed(0),
+        cost_estimate=weighed(1e9),
         name="past_dchances",
     )(upstream, *previous_values)
 
 
-def past_keys(queries, first_got, second_got, stats, tops, own, past_values, dchances, past_bias):
-    block_rows, width = queries.shape
-    heads = width // HEAD_DIM
-
-    def kernel(
-        q, first, second, own_stats, tops, sums, slope_keys, query_t, up_t, pv, dchances, past_bias,
-        attended, query_grads, scaled_query, shifted_query, scaled_up
-    ):
-        even = is_even()
-        for start in range(0, heads, GROUP):
-            group = range(start, min(start + GROUP, heads))
-            cols = [pl.ds(head * HEAD_DIM, HEAD_DIM) for head in group]
-            keys = [jnp.where(even, second[:, c], first[:, c]) for c in cols]
-            scores = [by_rows(key, q[:, c]) * exp2_scale + past_bias[...] for key, c in zip(keys, cols)]
-            maxes = [
-                jnp.maximum(tops[pl.ds(head, 1), :], jnp.max(x, axis=0, keepdims=True)) for head, x in zip(group, scores)
-            ]
+def add_past(refs, past_key, results, heads):
+    q, own_stats, tops, sums, slope_keys, query_t, up_t, pv, dchances, bias = refs
+    attended, query_grads, scaled_query, shifted_query, scaled_up = results
+    for start in range(0, heads, GROUP):
+        group = range(start, min(start + GROUP, heads))
+        cols = [pl.ds(head * HEAD_DIM, HEAD_DIM) for head in group]
+        tops_here = [tops[pl.ds(head, 1), :] for head in group]
+        own_offsets = [own_stats[pl.ds(heads + head, 1), :] for head in group]
+        if past_key is None:
+            factors = [jnp.exp2(top - own_stats[pl.ds(head, 1), :]) for head, top in zip(group, tops_here)]
+        else:
+            keys = [past_key[:, c] for c in cols]
+            scores = [by_rows(key, q[:, c]) * exp2_scale + bias[...] for key, c in zip(keys, cols)]
+            maxes = [jnp.maximum(top, jnp.max(x, axis=0, keepdims=True)) for top, x in zip(tops_here, scores)]
             grown = [jnp.exp2(x - m) for x, m in zip(scores, maxes)]
             own = [jnp.exp2(own_stats[pl.ds(head, 1), :] - m) for head, m in zip(group, maxes)]
             shares = [1.0 / (o + jnp.sum(x, axis=0, keepdims=True)) for o, x in zip(own, grown)]
             offsets = [
-                y * (own_stats[pl.ds(heads + head, 1), :] * o + jnp.sum(x * dchances[head], axis=0, keepdims=True))
-                for head, o, x, y in zip(group, own, grown, shares)
+                y * (offset * o + jnp.sum(x * dchances[head], axis=0, keepdims=True))
+                for head, offset, o, x, y in zip(group, own_offsets, own, grown, shares)
             ]
-            factors = [jnp.exp2(tops[pl.ds(head, 1), :] - m) * y for head, m, y in zip(group, maxes, shares)]
-            shifts = [
-                f * (o - own_stats[pl.ds(heads + head, 1), :]) for head, f, o in zip(group, factors, offsets)
-            ]
+            factors = [jnp.exp2(top - m) * y for top, m, y in zip(tops_here, maxes, shares)]
+            shifts = [f * (o - offset) for f, o, offset in zip(factors, offsets, own_offsets)]
             chances = [x * y for x, y in zip(grown, shares)]
             weights = [x.astype(jnp.bfloat16) for x in chances]
             dscores = [(x * (dchances[head] - o)).astype(jnp.bfloat16) for x, head, o in zip(chances, group, offsets)]
-            for n, (head, c) in enumerate(zip(group, cols)):
-                factor, shift = factors[n], shifts[n]
-                attended_t = factor * sums[head, :HEAD_DIM] + by_columns(pv[:, c], weights[n])
-                attended[:, c] = jnp.transpose(attended_t.astype(jnp.bfloat16))
-                grads_t = (
-                    factor * slope_keys[head] - shift * sums[head, HEAD_DIM:] + by_columns(keys[n], dscores[n])
-                )
-                query_grads[:, c] = jnp.transpose((score_scale * grads_t).astype(jnp.bfloat16))
-                scaled_query[head] = (query_t[head] * factor).astype(jnp.bfloat16)
-                shifted_query[head] = (query_t[head] * -shift).astype(jnp.bfloat16)
-                scaled_up[head] = (up_t[head] * factor).astype(jnp.bfloat16)
-
-    return pl.pallas_call(
-        kernel,
-        out_shape=[bf16(block_rows, width)] * 2 + [bf16(heads, HEAD_DIM, block_rows)] * 3,
-        in_specs=[VMEM] * 12,
-        out_specs=[VMEM] * 5,
+        for n, (head, c) in enumerate(zip(group, cols)):
+            factor = factors[n]
+            attended_t = factor * sums[head, :HEAD_DIM]
+            grads_t = factor * slope_keys[head]
+            if past_key is None:
+                shifted_query[head] = jnp.zeros(shifted_query.shape[1:], jnp.bfloat16)
+            else:
+                attended_t = attended_t + by_columns(pv[:, c], weights[n])
+                grads_t = grads_t - shifts[n] * sums[head, HEAD_DIM:] + by_columns(keys[n], dscores[n])
+                shifted_query[head] = (query_t[head] * -shifts[n]).astype(jnp.bfloat16)
+            attended[:, c] = jnp.transpose(attended_t.astype(jnp.bfloat16))
+            query_grads[:, c] = jnp.transpose((score_scale * grads_t).astype(jnp.bfloat16))
+            scaled_query[head] = (query_t[head] * factor).astype(jnp.bfloat16)
+            scaled_up[head] = (up_t[head] * factor).astype(jnp.bfloat16)
+
+
+def own_gradients(grown_t, slopes_t, scaled, head):
+    scaled_query, shifted_query, scaled_up = scaled
+    mixed = by_rows(grown_t[head], jnp.concatenate([scaled_up[head], shifted_query[head]], axis=0))
+    return mixed[:, :HEAD_DIM], mixed[:, HEAD_DIM:] + by_rows(slopes_t[head], scaled_query[head])
+
+
+def next_part(refs, later_query, group, heads, extra=None):
+    k, nu, stats, later, bias = refs
+    cols = [pl.ds(head * HEAD_DIM, HEAD_DIM) for head in group]
+    scores = [by_rows(k[:, c], later_query[:, c]) * exp2_scale + bias[...] for c in cols]
+    more = [extra(head) for head in group] if extra else None
+    far = [stats[pl.ds(head, 1), :] for head in group]
+    maxes = [jnp.maximum(f, jnp.max(x, axis=0, keepdims=True)) for f, x in zip(far, scores)]
+    grown = [jnp.exp2(x - m) for x, m in zip(scores, maxes)]
+    far = [jnp.exp2(f - m) for f, m in zip(far, maxes)]
+    shares = [1.0 / (f + jnp.sum(x, axis=0, keepdims=True)) for f, x in zip(far, grown)]
+    offsets = [
+        y * (stats[pl.ds(heads + head, 1), :] * f + jnp.sum(x * later[head], axis=0, keepdims=True))
+        for head, f, x, y in zip(group, far, grown, shares)
+    ]
+    chances = [x * y for x, y in zip(grown, shares)]
+    weights = [x.astype(jnp.bfloat16) for x in chances]
+    dscores = [(x * (later[head] - o)).astype(jnp.bfloat16) for x, head, o in zip(chances, group, offsets)]
+    parts = [
+        [product(weights[n], nu[:, c]), product(dscores[n], later_query[:, c])] for n, c in enumerate(cols)
+    ]
+    if more:
+        parts = [[x + y for x, y in zip(*pair)] for pair in zip(parts, more)]
+    return parts
+
+
+def first_half(keys, first_got, next_upstream, first_stats, later, next_bias, past_refs):
+    block_rows, width = keys.shape
+    heads = width // HEAD_DIM
+    past_count = len(past_refs)
+
+    def kernel(k, first, nu, stats, later, next_bias, *rest):
+        past_in, results = rest[:past_count], rest[past_count : past_count + 5]
+        value_part, key_part = rest[past_count + 5 :]
+
+        @pl.when(is_even())
+        def _():
+            for start in range(0, heads, GROUP):
+                group = range(start, min(start + GROUP, heads))
+                parts = next_part((k, nu, stats, later, next_bias), first, group, heads)
+                for head, (value, key) in zip(group, parts):
+                    columns = pl.ds(head * HEAD_DIM, HEAD_DIM)
+                    value_part[:, columns] = value
+                    key_part[:, columns] = key
+
+        @pl.when(jnp.logical_not(is_even()))
+        def _():
+            add_past(past_in, first, results, heads)
+
+    wide = jax.ShapeDtypeStruct((block_rows, width), jnp.float32)
+    out = pl.pallas_call(
+        kernel,
+        out_shape=[bf16(block_rows, width)] * 2 + [bf16(heads, HEAD_DIM, block_rows)] * 3 + [wide] * 2,
+        in_specs=[VMEM] * (6 + past_count),
+        out_specs=[VMEM] * 7,
         compiler_params=pltpu.CompilerParams(vmem_limit_bytes=20 * 2**20),
         cost_estimate=weighed(0),
-        name="past_keys",
-    )(queries, first_got, second_got, stats, tops, *own, past_values, dchances, past_bias)
-
-
-def next_rows(
-    keys, first_got, second_got, next_upstream, first_stats, second_stats, later, next_bias, grown_t, slopes_t,
-    done, scaled
-):
+        name="first_half",
+    )(keys, first_got, next_upstream, first_stats, later, next_bias, *past_refs)
+    return out[:5], out[5:]
+
+
+def second_half(keys, second_got, next_upstream, second_stats, later, next_bias, grown_t, slopes_t, past_refs, done, parts):
     block_rows, width = keys.shape
     heads = width // HEAD_DIM
-
-    def kernel(
-        k, first, second, nu, first_stats, second_stats, later, next_bias, grown_t, slopes_t,
-        attended, query_grads, scaled_query, shifted_query, scaled_up, *rest
-    ):
-        outs, (key_grads, value_grads, sems) = rest[:4], rest[4:]
-        copies = [pltpu.make_async_copy(source, outs[i], sems.at[i]) for i, source in enumerate((attended, query_grads))]
-        for c in copies:
-            c.start()
-        even = is_even()
-        stats = jnp.where(even, first_stats[...], second_stats[...])
-        for start in range(0, heads, PAIR):
-            group = range(start, min(start + PAIR, heads))
-            cols = [pl.ds(head * HEAD_DIM, HEAD_DIM) for head in group]
-            queries = [jnp.where(even, first[:, c], second[:, c]) for c in cols]
-            scores = [by_rows(k[:, c], query) * exp2_scale + next_bias[...] for c, query in zip(cols, queries)]
-            mixed = [
-                by_rows(grown_t[head], jnp.concatenate([scaled_up[head], shifted_query[head]], axis=0)) for head in group
-            ]
-            sloped = [by_rows(slopes_t[head], scaled_query[head]) for head in group]
-            far = [stats[head : head + 1] for head in group]
-            maxes = [jnp.maximum(f, jnp.max(x, axis=0, keepdims=True)) for f, x in zip(far, scores)]
-            grown = [jnp.exp2(x - m) for x, m in zip(scores, maxes)]
-            far = [jnp.exp2(f - m) for f, m in zip(far, maxes)]
-            shares = [1.0 / (f + jnp.sum(x, axis=0, keepdims=True)) for f, x in zip(far, grown)]
-            offsets = [
-                y * (stats[heads + head : heads + head + 1] * f + jnp.sum(x * later[head], axis=0, keepdims=True))
-                for head, f, x, y in zip(group, far, grown, shares)
-            ]
-            chances = [x * y for x, y in zip(grown, shares)]
-            weights = [x.astype(jnp.bfloat16) for x in chances]
-            dscores = [
-                (x * (later[head] - offset)).astype(jnp.bfloat16)
-                for x, head, offset in zip(chances, group, offsets)
-            ]
-            for n, (head, c) in enumerate(zip(group, cols)):
-                value_grads[:, c] = (mixed[n][:, :HEAD_DIM] + product(weights[n], nu[:, c])).astype(jnp.bfloat16)
-                key_grads[:, c] = (
-                    score_scale
-                    * (mixed[n][:, HEAD_DIM:] + sloped[n] + product(dscores[n], queries[n]))
-                ).astype(jnp.bfloat16)
-            wide = pl.ds(start * HEAD_DIM, len(group) * HEAD_DIM)
-            for i, source in ((2, key_grads), (3, value_grads)):
-                copies.append(pltpu.make_async_copy(source.at[:, wide], outs[i].at[:, wide], sems.at[len(copies)]))
-                copies[-1].start()
-        for c in copies:
-            c.wait()
+    past_count = len(past_refs)
+
+    def kernel(k, second, nu, stats, later, next_bias, grown_t, slopes_t, *rest):
+        past_in, rest = rest[:past_count], rest[past_count:]
+        done, (value_part, key_part), outs, rest = rest[:5], rest[5:7], rest[7:11], rest[11:]
+        here, (key_grads, value_grads, sems) = rest[:5], rest[5:]
+
+        def send(rows, i, slot, columns=slice(None)):
+            copy = pltpu.make_async_copy(rows.at[:, columns], outs[i].at[:, columns], sems.at[slot])
+            copy.start()
+            return copy
+
+        def finish(rows, from_next):
+            copies = [send(rows[0], 0, 0), send(rows[1], 1, 1)]
+            for start in range(0, heads, PAIR):
+                group = range(start, min(start + PAIR, heads))
+                for head, (value, key) in zip(group, from_next(group, rows[2:])):
+                    columns = pl.ds(head * HEAD_DIM, HEAD_DIM)
+                    value_grads[:, columns] = value.astype(jnp.bfloat16)
+                    key_grads[:, columns] = (score_scale * key).astype(jnp.bfloat16)
+                columns = pl.ds(start * HEAD_DIM, len(group) * HEAD_DIM)
+                copies.append(send(key_grads, 2, len(copies), columns))
+                copies.append(send(value_grads, 3, len(copies), columns))
+            for copy in copies:
+                copy.wait()
+
+        def added(group, scaled):
+            parts = []
+            for head in group:
+                value, key = own_gradients(grown_t, slopes_t, scaled, head)
+                columns = pl.ds(head * HEAD_DIM, HEAD_DIM)
+                parts.append([value + value_part[:, columns], key + key_part[:, columns]])
+            return parts
+
+        def computed(group, scaled):
+            return next_part(
+                (k, nu, stats, later, next_bias), second, group, heads,
+                lambda head: own_gradients(grown_t, slopes_t, scaled, head),
+            )
+
+        block = lax.axis_index("blk")
+
+        @pl.when(block == 0)
+        def _():
+            add_past(past_in, None, here, heads)
+
+        @pl.when(jnp.logical_and(is_even(), block > 0))
+        def _():
+            add_past(past_in, second, here, heads)
+
+        @pl.when(is_even())
+        def _():
+            finish(here, added)
+
+        @pl.when(jnp.logical_not(is_even()))
+        def _():
+            finish(done, computed)
 
     return pl.pallas_call(
         kernel,
         out_shape=[bf16(block_rows, width)] * 4,
-        in_specs=[VMEM] * 15,
+        in_specs=[VMEM] * (15 + past_count),
         out_specs=[ANY] * 4,
         scratch_shapes=[pltpu.VMEM((block_rows, width), jnp.bfloat16)] * 2
+        + [pltpu.VMEM((heads, HEAD_DIM, block_rows), jnp.bfloat16)] * 3
+        + [pltpu.VMEM((block_rows, width), jnp.bfloat16)] * 2
         + [pltpu.SemaphoreType.DMA((2 + 2 * heads,))],
-        compiler_params=pltpu.CompilerParams(vmem_limit_bytes=16 * 2**20),
-        name="next_rows",
+        compiler_params=pltpu.CompilerParams(vmem_limit_bytes=20 * 2**20),
+        cost_estimate=weighed(0),
+        name="second_half",
     )(
-        keys, first_got, second_got, next_upstream, first_stats, second_stats, later, next_bias, grown_t, slopes_t,
-        *done, *scaled,
+        keys, second_got, next_upstream, second_stats, later, next_bias, grown_t, slopes_t, *past_refs, *done, *parts,
     )
 
 
@@ -490,13 +554,11 @@
     first_stats, second_stats = block_exchange(stats, 0), block_exchange(stats, 1)
     *own, later = own_products(keys, query_rows, upstream, values, grown_t, slopes_t, next_upstream)
     past_values, dchances = past_dchances(upstream, previous)
-    attended, query_grads, *scaled = past_keys(
-        query_rows, first_got, second_got, stats, tops, own, past_values, dchances, past_bias
-    )
+    past_refs = (query_rows, stats, tops, *own, past_values, dchances, past_bias)
+    done, parts = first_half(keys, first_got, next_upstream, first_stats, later, next_bias, past_refs)
     return tuple(
-        next_rows(
-            keys, first_got, second_got, next_upstream, first_stats, second_stats, later, next_bias, grown_t,
-            slopes_t, (attended, query_grads), scaled,
+        second_half(
+            keys, second_got, next_upstream, second_stats, later, next_bias, grown_t, slopes_t, past_refs, done, parts
         )
     )
 

time: 24.4 us -> 23.7 us (0.971)
  Pallas kernels: 6.82 us -> 6.18 us
    pallas_call x2, Pallas kernels: 3.1 us -> 2.47 us  [the longest x1 1.51 us: second_half(): pl.pallas_call(kernel, out_shape=[bf16(block_rows, width)] * 4, in_specs=...]
  transfers between devices with their start and end apart: 11 -> 11, of which waited for: 2 -> 3; matrix products, arithmetic and copies ran while one was open for 0% -> 0% of each run, Pallas kernels for 15% -> 14%
where the time goes in v6:
time: 23.7 us; the launch traced here: 23.5 us
  starting transfers between devices  13.2 us (56%)
  Pallas kernels  6.18 us (26%)
  waiting for transfers between devices  3.34 us (14%)
  between operations  0.74 us (3%)
    ppermute x6, starting transfers between devices, block_exchange(): return lax.ppermute(rows, ('dp', 'blk', 'head'), route)  6.98 us
    ppermute x5, starting transfers between devices, partner_exchange(): return lax.ppermute(rows, 'head', route)  6.26 us
    ppermute x5, waiting for transfers between devices, partner_exchange(): return lax.ppermute(rows, 'head', route)  2.28 us
    pallas_call x1, Pallas kernels, second_half(): pl.pallas_call(kernel, out_shape=[bf16(block_rows, width)] * 4, in_specs=...  1.51 us
    pallas_call x1, Pallas kernels, cut_pieces(): pl.pallas_call(kernel, out_shape=[bf16(height, width) for height in heigh...  1.31 us
    ppermute x6, waiting for transfers between devices, block_exchange(): return lax.ppermute(rows, ('dp', 'blk', 'head'), route)  1.07 us
    pallas_call x1, Pallas kernels, first_half(): pl.pallas_call(kernel, out_shape=[bf16(block_rows, width)] * 2 + [bf16(he...  0.96 us
    pallas_call x1, Pallas kernels, stack_far_values(): pl.pallas_call(kernel, out_shape=[jax.ShapeDtypeStruct((block_rows, block...  0.73 us
  transfers between devices with their start and end apart: 11, of which 3 were waited for; matrix products, arithmetic and copies ran while one was open for 0% of the time, Pallas kernels for 14%

profile of v6, /device:TPU:0, one launch (start us, length us, event | category | flops | bytes accessed | tf_op | source)
XLA Modules:
  0.0 23.5 jit_solution(3900029705633216083)
XLA Ops:
  0.6 0.0 copy-start
  0.6 1.3 %cut_pieces.1 = (bf16[256,512]{1,0:T(8,128)(2,1)S(1)}, bf16[256,512]{1,0:T(8,128)(2,1)S(1)}, bf16[128,512]{1,0:T(8,128)(2,1)S(1)}, bf16[128,512]{1,0:T(8,128)(2,1)S(1)}) custom-call(bf16[64,2048]{1,0:T(8,128)(2,1)} %q.1, bf16[64,2048]{1,0:T(8,128)(2,1)} %k.1, bf16[64,2048]{1,0:T(8,128)(2,1)} %v.1), custom_call_target="tpu_custom_call" | custom-call | tf_op jit(solution)/shard_map/cut_pieces/pallas_call | solution.py:87
  2.0 0.5 %collective-permute-start = (bf16[256,512]{1,0:T(8,128)(2,1)S(1)}, bf16[256,512]{1,0:T(8,128)(2,1)S(1)}, u32[]{:S(2)}, u32[]{:S(2)}) collective-permute-start(bf16[256,512]{1,0:T(8,128)(2,1)S(1)} %get-tuple-element.41), channel_id=1, source_target_pairs={{0,1},{1,0},{2,3},{3,2},{4,5},{5,4},{6,7},{7,6},{8,9},{9,8},{10,11... | collective-permute-start | bytes 786440 | tf_op jit(solution)/shard_map/ppermute | solution.py:29
  2.5 2.6 %collective-permute-start.1 = (bf16[128,512]{1,0:T(8,128)(2,1)S(1)}, bf16[128,512]{1,0:T(8,128)(2,1)S(1)}, u32[]{:S(2)}, u32[]{:S(2)}) collective-permute-start(bf16[128,512]{1,0:T(8,128)(2,1)S(1)} %get-tuple-element.42), channel_id=1, source_target_pairs={{0,2},{1,3},{2,0},{3,1},{4,6},{5,7},{6,4},{7,5},{8,10},{9,11},{10,... | collective-permute-start | bytes 393224 | tf_op jit(solution)/shard_map/ppermute | solution.py:29
  5.0 0.1 collective-permute-start.2
  5.1 0.0 collective-permute-done.refs_1_.theirs.rest_1_
  5.1 0.0 copy-done
  5.2 0.0 copy-start.1
  5.2 1.9 %collective-permute-start.4 = (bf16[256,512]{1,0:T(8,128)(2,1)S(1)}, bf16[256,512]{1,0:T(8,128)(2,1)S(1)}, u32[]{:S(2)}, u32[]{:S(2)}) collective-permute-start(bf16[256,512]{1,0:T(8,128)(2,1)S(1)} %get-tuple-element.46), channel_id=1, source_target_pairs={{0,4},{1,5},{2,6},{3,7},{4,0},{5,1},{6,2},{7,3},{8,12},{9,13},{10,... | collective-permute-start | bytes 786440 | tf_op jit(solution)/shard_map/ppermute | solution.py:44
  7.0 0.1 collective-permute-start.5
  7.1 0.0 copy-done.1
  7.1 0.7 %stack_far_values.1 = (f32[256,256]{1,0:T(8,128)S(1)}, f32[256,256]{1,0:T(8,128)S(1)}, f32[256,256]{1,0:T(8,128)S(1)}, bf16[128,512]{1,0:T(8,128)(2,1)S(1)}) custom-call(bf16[256,512]{1,0:T(8,128)(2,1)S(1)} %get-tuple-element.40.refs_0_.mine.rest_0_, bf16[256,512]{1,0:T(8,128)(2,1)S(1)} %collective-permute-done.refs_1_.theirs.rest_1_, s32[4]{0:T(128)S(1)} %copy-done.1), custom_call_target="tpu_custom_call" | custom-call | flops 5000000000 | tf_op jit(solution)/shard_map/stack_far_values/pallas_call | solution.py:115
  7.9 1.6 %collective-permute-start.6 = (bf16[128,512]{1,0:T(8,128)(2,1)S(1)}, bf16[128,512]{1,0:T(8,128)(2,1)S(1)}, u32[]{:S(2)}, u32[]{:S(2)}) collective-permute-start(bf16[128,512]{1,0:T(8,128)(2,1)S(1)} %get-tuple-element.51), channel_id=1, source_target_pairs={{0,2},{1,3},{2,0},{3,1},{4,6},{5,7},{6,4},{7,5},{8,10},{9,11},{10,... | collective-permute-start | bytes 393224 | tf_op jit(solution)/shard_map/ppermute | solution.py:29
  9.4 0.0 collective-permute-done.1.refs_2_
  9.4 2.3 %collective-permute-done.2.refs_3_ = bf16[128,512]{1,0:T(8,128)(2,1)S(1)} collective-permute-done((bf16[128,512]{1,0:T(8,128)(2,1)S(1)}, bf16[128,512]{1,0:T(8,128)(2,1)S(1)}, u32[]{:S(2)}, u32[]{:S(2)}) %collective-permute-start.2) | collective-permute-done | bytes 131104 | tf_op jit(solution)/shard_map/ppermute | solution.py:29
  11.7 0.1 join_keys_queries.1
  11.8 1.7 %collective-permute-start.9 = (bf16[256,512]{1,0:T(8,128)(2,1)S(1)}, bf16[256,512]{1,0:T(8,128)(2,1)S(1)}, u32[]{:S(2)}, u32[]{:S(2)}) collective-permute-start(bf16[256,512]{1,0:T(8,128)(2,1)S(1)} %get-tuple-element.68), channel_id=1, source_target_pairs={{0,4},{1,5},{2,6},{3,7},{4,0},{5,1},{6,2},{7,3},{8,12},{9,13},{10,... | collective-permute-start | bytes 786440 | tf_op jit(solution)/shard_map/ppermute | solution.py:44
  13.5 0.6 %collective-permute-start.3 = (bf16[256,512]{1,0:T(8,128)(2,1)S(1)}, bf16[256,512]{1,0:T(8,128)(2,1)S(1)}, u32[]{:S(2)}, u32[]{:S(2)}) collective-permute-start(bf16[256,512]{1,0:T(8,128)(2,1)S(1)} %get-tuple-element.45), channel_id=1, source_target_pairs={{0,1},{1,0},{2,3},{3,2},{4,8},{5,9},{6,10},{7,11},{8,4},{9,5},{10,... | collective-permute-start | bytes 786440 | tf_op jit(solution)/shard_map/ppermute | solution.py:44
  14.1 0.0 collective-permute-done.4.first
  14.1 0.0 collective-permute-done.5.second
  14.2 1.6 %collective-permute-start.8 = (bf16[128,512]{1,0:T(8,128)(2,1)S(1)}, bf16[128,512]{1,0:T(8,128)(2,1)S(1)}, u32[]{:S(2)}, u32[]{:S(2)}) collective-permute-start(bf16[128,512]{1,0:T(8,128)(2,1)S(1)} %get-tuple-element.64), channel_id=1, source_target_pairs={{0,2},{1,3},{2,0},{3,1},{4,6},{5,7},{6,4},{7,5},{8,10},{9,11},{10,... | collective-permute-start | bytes 393224 | tf_op jit(solution)/shard_map/ppermute | solution.py:29
  15.7 0.0 collective-permute-done.6.rest_2_
  15.7 0.7 %own_scores.1 = (bf16[256,512]{1,0:T(8,128)(2,1)S(1)}, f32[8,256]{1,0:T(8,128)S(1)}, f32[4,256]{1,0:T(4,128)S(1)}, bf16[4,256,256]{2,1,0:T(8,128)(2,1)S(1)}, bf16[4,256,256]{2,1,0:T(8,128)(2,1)S(1)}) custom-call(bf16[256,512]{1,0:T(8,128)(2,1)S(1)} %get-tuple-element.44.k, bf16[256,512]{1,0:T(8,128)(2,1)S(1)} %get-tuple-element.49.q.rest_0_, ...), custom_call_target="tpu_custom_call" | custom-call | tf_op jit(solution)/shard_map/own_scores/pallas_call | solution.py:281
  16.4 2.7 %collective-permute-start.10 = (f32[8,256]{1,0:T(8,128)S(1)}, f32[8,256]{1,0:T(8,128)S(1)}, u32[]{:S(2)}, u32[]{:S(2)}) collective-permute-start(f32[8,256]{1,0:T(8,128)S(1)} %get-tuple-element.52.rest_1_), channel_id=1, source_target_pairs={{0,4},{1,5},{2,6},{3,7},{4,0},{5,1},{6,2},{7,3},{8,12},{9,13},{10,... | collective-permute-start | bytes 24584 | tf_op jit(solution)/shard_map/ppermute | solution.py:44
  19.1 0.0 collective-permute-start.7
  19.1 0.5 %own_products.1 = (f32[4,256,256]{2,1,0:T(8,128)S(1)}, f32[4,128,256]{2,1,0:T(8,128)S(1)}, f32[4,128,256]{2,1,0:T(8,128)S(1)}, f32[4,128,256]{2,1,0:T(8,128)S(1)}, f32[4,256,256]{2,1,0:T(8,128)S(1)}) custom-call(bf16[256,512]{1,0:T(8,128)(2,1)S(1)} %get-tuple-element.44.k, bf16[256,512]{1,0:T(8,128)(2,1)S(1)} %get-tuple-element.49.q.rest_0_, ...), custom_call_target="tpu_custom_call" | custom-call | flops 1000000000 | tf_op jit(solution)/shard_map/own_products/pallas_call | solution.py:315
  19.6 0.0 collective-permute-done.8.rest_1_
  19.7 0.3 %past_dchances.1 = (bf16[256,512]{1,0:T(8,128)(2,1)S(1)}, f32[4,256,256]{2,1,0:T(8,128)S(1)}) custom-call(bf16[256,512]{1,0:T(8,128)(2,1)S(1)} %copy-done, bf16[128,512]{1,0:T(8,128)(2,1)S(1)} %get-tuple-element.63.rest_0_, bf16[128,512]{1,0:T(8,128)(2,1)S(1)} %collective-permute-done.8.rest_1_), custom_call_target="tpu_custom_call" | custom-call | flops 1000000000 | tf_op jit(solution)/shard_map/past_dchances/pallas_call | solution.py:340
  20.0 1.0 %collective-permute-done.9.first = bf16[256,512]{1,0:T(8,128)(2,1)S(1)} collective-permute-done((bf16[256,512]{1,0:T(8,128)(2,1)S(1)}, bf16[256,512]{1,0:T(8,128)(2,1)S(1)}, u32[]{:S(2)}, u32[]{:S(2)}) %collective-permute-start.9) | collective-permute-done | bytes 262176 | tf_op jit(solution)/shard_map/ppermute | solution.py:44
  20.9 0.1 collective-permute-done.10.stats
  21.0 1.0 %first_half.1 = (bf16[256,512]{1,0:T(8,128)(2,1)S(1)}, bf16[256,512]{1,0:T(8,128)(2,1)S(1)}, bf16[4,128,256]{2,1,0:T(8,128)(2,1)S(1)}, bf16[4,128,256]{2,1,0:T(8...) custom-call(bf16[256,512]{1,0:T(8,128)(2,1)S(1)} %get-tuple-element.44.k, ...), custom_call_target="tpu_custom_call" | custom-call | tf_op jit(solution)/shard_map/first_half/pallas_call | solution.py:448
  22.0 0.0 collective-permute-done.3.second
  22.0 0.0 collective-permute-done.7.stats
  22.0 1.5 %second_half.1 = (bf16[256,512]{1,0:T(8,128)(2,1)}, bf16[256,512]{1,0:T(8,128)(2,1)}, bf16[256,512]{1,0:T(8,128)(2,1)}, bf16[256,512]{1,0:T(8,128)(2,1)}) custom-call(bf16[256,512]{1,0:T(8,128)(2,1)S(1)} %get-tuple-element.44.k, bf16[256,512]{1,0:T(8,128)(2,1)S(1)} %collective-permute-done.3.second, bf16[256,512]{1,0:T(8,128)(2,1)S(1)} %get-tuple-element.48._.nu, ...), custom_call_target="tpu_custom_call" | custom-call | tf_op jit(solution)/shard_map/second_half/pallas_call | solution.py:521
  (2 shorter events, 0.1 us)
Async XLA Ops:
  0.6 4.5 %copy-start = (bf16[256,512]{1,0:T(8,128)(2,1)S(1)}, bf16[256,512]{1,0:T(8,128)(2,1)}, u32[]{:S(2)}) copy-start(bf16[256,512]{1,0:T(8,128)(2,1)} %u.7) | copy-start | bytes 786436
  2.0 3.2 %collective-permute-start = (bf16[256,512]{1,0:T(8,128)(2,1)S(1)}, bf16[256,512]{1,0:T(8,128)(2,1)S(1)}, u32[]{:S(2)}, u32[]{:S(2)}) collective-permute-start(bf16[256,512]{1,0:T(8,128)(2,1)S(1)} %get-tuple-element.41), channel_id=1, source_target_pairs={{0,1},{1,0},{2,3},{3,2},{4,5},{5,4},{6,7},{7,6},{8,9},{9,8},{10,11... | collective-permute-start | bytes 786440 | tf_op jit(solution)/shard_map/ppermute | solution.py:29
  2.5 6.9 %collective-permute-start.1 = (bf16[128,512]{1,0:T(8,128)(2,1)S(1)}, bf16[128,512]{1,0:T(8,128)(2,1)S(1)}, u32[]{:S(2)}, u32[]{:S(2)}) collective-permute-start(bf16[128,512]{1,0:T(8,128)(2,1)S(1)} %get-tuple-element.42), channel_id=1, source_target_pairs={{0,2},{1,3},{2,0},{3,1},{4,6},{5,7},{6,4},{7,5},{8,10},{9,11},{10,... | collective-permute-start | bytes 393224 | tf_op jit(solution)/shard_map/ppermute | solution.py:29
  5.0 6.6 %collective-permute-start.2 = (bf16[128,512]{1,0:T(8,128)(2,1)S(1)}, bf16[128,512]{1,0:T(8,128)(2,1)S(1)}, u32[]{:S(2)}, u32[]{:S(2)}) collective-permute-start(bf16[128,512]{1,0:T(8,128)(2,1)S(1)} %get-tuple-element.43), channel_id=1, source_target_pairs={{0,3},{1,2},{2,1},{3,0},{4,7},{5,6},{6,5},{7,4},{8,11},{9,10},{10,... | collective-permute-start | bytes 393224 | tf_op jit(solution)/shard_map/ppermute | solution.py:29
  5.2 2.0 %copy-start.1 = (s32[4]{0:T(128)S(1)}, s32[4]{0:T(128)}, u32[]{:S(2)}) copy-start(s32[4]{0:T(128)} %lengths.1) | copy-start | bytes 52
  5.2 8.9 %collective-permute-start.4 = (bf16[256,512]{1,0:T(8,128)(2,1)S(1)}, bf16[256,512]{1,0:T(8,128)(2,1)S(1)}, u32[]{:S(2)}, u32[]{:S(2)}) collective-permute-start(bf16[256,512]{1,0:T(8,128)(2,1)S(1)} %get-tuple-element.46), channel_id=1, source_target_pairs={{0,4},{1,5},{2,6},{3,7},{4,0},{5,1},{6,2},{7,3},{8,12},{9,13},{10,... | collective-permute-start | bytes 786440 | tf_op jit(solution)/shard_map/ppermute | solution.py:44
  7.0 7.1 %collective-permute-start.5 = (bf16[256,512]{1,0:T(8,128)(2,1)S(1)}, bf16[256,512]{1,0:T(8,128)(2,1)S(1)}, u32[]{:S(2)}, u32[]{:S(2)}) collective-permute-start(bf16[256,512]{1,0:T(8,128)(2,1)S(1)} %get-tuple-element.47), channel_id=1, source_target_pairs={{0,1},{1,0},{2,3},{3,2},{4,8},{5,9},{6,10},{7,11},{8,4},{9,5},{10,... | collective-permute-start | bytes 786440 | tf_op jit(solution)/shard_map/ppermute | solution.py:44
  7.9 7.9 %collective-permute-start.6 = (bf16[128,512]{1,0:T(8,128)(2,1)S(1)}, bf16[128,512]{1,0:T(8,128)(2,1)S(1)}, u32[]{:S(2)}, u32[]{:S(2)}) collective-permute-start(bf16[128,512]{1,0:T(8,128)(2,1)S(1)} %get-tuple-element.51), channel_id=1, source_target_pairs={{0,2},{1,3},{2,0},{3,1},{4,6},{5,7},{6,4},{7,5},{8,10},{9,11},{10,... | collective-permute-start | bytes 393224 | tf_op jit(solution)/shard_map/ppermute | solution.py:29
  11.8 9.2 %collective-permute-start.9 = (bf16[256,512]{1,0:T(8,128)(2,1)S(1)}, bf16[256,512]{1,0:T(8,128)(2,1)S(1)}, u32[]{:S(2)}, u32[]{:S(2)}) collective-permute-start(bf16[256,512]{1,0:T(8,128)(2,1)S(1)} %get-tuple-element.68), channel_id=1, source_target_pairs={{0,4},{1,5},{2,6},{3,7},{4,0},{5,1},{6,2},{7,3},{8,12},{9,13},{10,... | collective-permute-start | bytes 786440 | tf_op jit(solution)/shard_map/ppermute | solution.py:44
  13.5 8.5 %collective-permute-start.3 = (bf16[256,512]{1,0:T(8,128)(2,1)S(1)}, bf16[256,512]{1,0:T(8,128)(2,1)S(1)}, u32[]{:S(2)}, u32[]{:S(2)}) collective-permute-start(bf16[256,512]{1,0:T(8,128)(2,1)S(1)} %get-tuple-element.45), channel_id=1, source_target_pairs={{0,1},{1,0},{2,3},{3,2},{4,8},{5,9},{6,10},{7,11},{8,4},{9,5},{10,... | collective-permute-start | bytes 786440 | tf_op jit(solution)/shard_map/ppermute | solution.py:44
  14.2 5.5 %collective-permute-start.8 = (bf16[128,512]{1,0:T(8,128)(2,1)S(1)}, bf16[128,512]{1,0:T(8,128)(2,1)S(1)}, u32[]{:S(2)}, u32[]{:S(2)}) collective-permute-start(bf16[128,512]{1,0:T(8,128)(2,1)S(1)} %get-tuple-element.64), channel_id=1, source_target_pairs={{0,2},{1,3},{2,0},{3,1},{4,6},{5,7},{6,4},{7,5},{8,10},{9,11},{10,... | collective-permute-start | bytes 393224 | tf_op jit(solution)/shard_map/ppermute | solution.py:29
  16.4 4.6 %collective-permute-start.10 = (f32[8,256]{1,0:T(8,128)S(1)}, f32[8,256]{1,0:T(8,128)S(1)}, u32[]{:S(2)}, u32[]{:S(2)}) collective-permute-start(f32[8,256]{1,0:T(8,128)S(1)} %get-tuple-element.52.rest_1_), channel_id=1, source_target_pairs={{0,4},{1,5},{2,6},{3,7},{4,0},{5,1},{6,2},{7,3},{8,12},{9,13},{10,... | collective-permute-start | bytes 24584 | tf_op jit(solution)/shard_map/ppermute | solution.py:44
  19.1 2.9 %collective-permute-start.7 = (f32[8,256]{1,0:T(8,128)S(1)}, f32[8,256]{1,0:T(8,128)S(1)}, u32[]{:S(2)}, u32[]{:S(2)}) collective-permute-start(f32[8,256]{1,0:T(8,128)S(1)} %get-tuple-element.52.rest_1_), channel_id=1, source_target_pairs={{0,1},{1,0},{2,3},{3,2},{4,8},{5,9},{6,10},{7,11},{8,4},{9,5},{10,... | collective-permute-start | bytes 24584 | tf_op jit(solution)/shard_map/ppermute | solution.py:44

commit v7 on v6

--- a/solution.py
+++ b/solution.py
@@ -323,77 +323,110 @@
     )(keys, queries, upstream, values, grown_t, slopes_t, next_upstream)
 
 
-def past_dchances(upstream, previous_values):
+def past_part(refs, past_key, group, heads):
+    q, own_stats, tops, _, _, _, _, pv, dchances, bias = refs
+    cols = [pl.ds(head * HEAD_DIM, HEAD_DIM) for head in group]
+    tops = [tops[pl.ds(head, 1), :] for head in group]
+    own_norms = [own_stats[pl.ds(head, 1), :] for head in group]
+    own_offsets = [own_stats[pl.ds(heads + head, 1), :] for head in group]
+    if past_key is None:
+        return [(jnp.exp2(top - norm), None, None) for top, norm in zip(tops, own_norms)]
+    keys = [past_key[:, c] for c in cols]
+    scores = [by_rows(key, q[:, c]) * exp2_scale + bias[...] for key, c in zip(keys, cols)]
+    maxes = [jnp.maximum(top, jnp.max(x, axis=0, keepdims=True)) for top, x in zip(tops, scores)]
+    grown = [jnp.exp2(x - m) for x, m in zip(scores, maxes)]
+    own = [jnp.exp2(norm - m) for norm, m in zip(own_norms, maxes)]
+    shares = [1.0 / (o + jnp.sum(x, axis=0, keepdims=True)) for o, x in zip(own, grown)]
+    offsets = [
+        y * (offset * o + jnp.sum(x * dchances[head], axis=0, keepdims=True))
+        for head, offset, o, x, y in zip(group, own_offsets, own, grown, shares)
+    ]
+    factors = [jnp.exp2(top - m) * y for top, m, y in zip(tops, maxes, shares)]
+    shifts = [f * (o - offset) for f, o, offset in zip(factors, offsets, own_offsets)]
+    chances = [x * y for x, y in zip(grown, shares)]
+    weights = [x.astype(jnp.bfloat16) for x in chances]
+    dscores = [(x * (dchances[head] - o)).astype(jnp.bfloat16) for x, head, o in zip(chances, group, offsets)]
+    return list(zip(factors, shifts, zip(weights, dscores, keys)))
+
+
+def scaled_rows(refs, part, head):
+    _, _, _, _, _, query_t, up_t, _, _, _ = refs
+    factor, shift, _ = part
+    query, up = query_t[head], up_t[head]
+    if shift is None:
+        shifted = jnp.zeros(query.shape, jnp.bfloat16)
+    else:
+        shifted = (query * -shift).astype(jnp.bfloat16)
+    return (query * factor).astype(jnp.bfloat16), shifted, (up * factor).astype(jnp.bfloat16)
+
+
+def done_rows(refs, part, head):
+    _, _, _, sums, slope_keys, _, _, pv, _, _ = refs
+    factor, shift, past = part
+    attended, grads = factor * sums[head, :HEAD_DIM], factor * slope_keys[head]
+    if past is not None:
+        weights, dscores, key = past
+        attended = attended + product(pv[head], weights)
+        grads = grads - shift * sums[head, HEAD_DIM:] + by_columns(key, dscores)
+    return (
+        jnp.transpose(attended.astype(jnp.bfloat16)),
+        jnp.transpose((score_scale * grads).astype(jnp.bfloat16)),
+    )
+
+
+def own_gradients(grown_t, slopes_t, scaled, head):
+    scaled_query, shifted_query, scaled_up = scaled
+    mixed = by_rows(grown_t[head], jnp.concatenate([scaled_up, shifted_query], axis=0))
+    return mixed[:, :HEAD_DIM], mixed[:, HEAD_DIM:] + by_rows(slopes_t[head], scaled_query)
+
+
+def before_exchanges(upstream, previous_values, queries, stats, tops, own, grown_t, slopes_t):
     pairs = len(previous_values)
     block_rows, width = upstream.shape
     rows = block_rows // pairs // 2
     heads = width // HEAD_DIM
 
-    def kernel(u, *rest):
-        pieces, (values, dchances) = rest[:pairs], rest[pairs:]
-        for step in range(2 * pairs):
-            values[place(step, rows), :] = pieces[step // 2][pl.ds(step % 2 * rows, rows), :]
-        for head in range(heads):
-            columns = pl.ds(head * HEAD_DIM, HEAD_DIM)
-            dchances[head] = by_rows(values[:, columns], u[:, columns])
-
+    def kernel(u, q, own_stats, tops, sums, slope_keys, query_t, up_t, grown_t, slopes_t, *rest):
+        pieces, (turned, dchances, attended, query_grads, value_own, key_own, values) = rest[:pairs], rest[pairs:]
+        first = lax.axis_index("blk") == 0
+
+        @pl.when(jnp.logical_not(first))
+        def _():
+            for step in range(2 * pairs):
+                values[place(step, rows), :] = pieces[step // 2][pl.ds(step % 2 * rows, rows), :]
+            for head in range(heads):
+                columns = pl.ds(head * HEAD_DIM, HEAD_DIM)
+                dchances[head] = by_rows(values[:, columns], u[:, columns])
+                turned[head] = jnp.transpose(values[:, columns])
+
+        @pl.when(first)
+        def _():
+            refs = (q, own_stats, tops, sums, slope_keys, query_t, up_t, turned, dchances, None)
+            for head, part in enumerate(past_part(refs, None, range(heads), heads)):
+                columns = pl.ds(head * HEAD_DIM, HEAD_DIM)
+                attended[:, columns], query_grads[:, columns] = done_rows(refs, part, head)
+                value_own[:, columns], key_own[:, columns] = own_gradients(
+                    grown_t, slopes_t, scaled_rows(refs, part, head), head
+                )
+
+    wide = jax.ShapeDtypeStruct((block_rows, width), jnp.float32)
     return pl.pallas_call(
         kernel,
-        out_shape=[bf16(block_rows, width), jax.ShapeDtypeStruct((heads, block_rows, block_rows), jnp.float32)],
-        in_specs=[VMEM] * (1 + pairs),
-        out_specs=[VMEM] * 2,
-        compiler_params=small_kernel(),
+        out_shape=[
+            bf16(heads, HEAD_DIM, block_rows),
+            jax.ShapeDtypeStruct((heads, block_rows, block_rows), jnp.float32),
+            bf16(block_rows, width),
+            bf16(block_rows, width),
+            wide,
+            wide,
+        ],
+        in_specs=[VMEM] * (10 + pairs),
+        out_specs=[VMEM] * 6,
+        scratch_shapes=[pltpu.VMEM((block_rows, width), jnp.bfloat16)],
+        compiler_params=pltpu.CompilerParams(vmem_limit_bytes=12 * 2**20),
         cost_estimate=weighed(1e9),
-        name="past_dchances",
-    )(upstream, *previous_values)
-
-
-def add_past(refs, past_key, results, heads):
-    q, own_stats, tops, sums, slope_keys, query_t, up_t, pv, dchances, bias = refs
-    attended, query_grads, scaled_query, shifted_query, scaled_up = results
-    for start in range(0, heads, GROUP):
-        group = range(start, min(start + GROUP, heads))
-        cols = [pl.ds(head * HEAD_DIM, HEAD_DIM) for head in group]
-        tops_here = [tops[pl.ds(head, 1), :] for head in group]
-        own_offsets = [own_stats[pl.ds(heads + head, 1), :] for head in group]
-        if past_key is None:
-            factors = [jnp.exp2(top - own_stats[pl.ds(head, 1), :]) for head, top in zip(group, tops_here)]
-        else:
-            keys = [past_key[:, c] for c in cols]
-            scores = [by_rows(key, q[:, c]) * exp2_scale + bias[...] for key, c in zip(keys, cols)]
-            maxes = [jnp.maximum(top, jnp.max(x, axis=0, keepdims=True)) for top, x in zip(tops_here, scores)]
-            grown = [jnp.exp2(x - m) for x, m in zip(scores, maxes)]
-            own = [jnp.exp2(own_stats[pl.ds(head, 1), :] - m) for head, m in zip(group, maxes)]
-            shares = [1.0 / (o + jnp.sum(x, axis=0, keepdims=True)) for o, x in zip(own, grown)]
-            offsets = [
-                y * (offset * o + jnp.sum(x * dchances[head], axis=0, keepdims=True))
-                for head, offset, o, x, y in zip(group, own_offsets, own, grown, shares)
-            ]
-            factors = [jnp.exp2(top - m) * y for top, m, y in zip(tops_here, maxes, shares)]
-            shifts = [f * (o - offset) for f, o, offset in zip(factors, offsets, own_offsets)]
-            chances = [x * y for x, y in zip(grown, shares)]
-            weights = [x.astype(jnp.bfloat16) for x in chances]
-            dscores = [(x * (dchances[head] - o)).astype(jnp.bfloat16) for x, head, o in zip(chances, group, offsets)]
-        for n, (head, c) in enumerate(zip(group, cols)):
-            factor = factors[n]
-            attended_t = factor * sums[head, :HEAD_DIM]
-            grads_t = factor * slope_keys[head]
-            if past_key is None:
-                shifted_query[head] = jnp.zeros(shifted_query.shape[1:], jnp.bfloat16)
-            else:
-                attended_t = attended_t + by_columns(pv[:, c], weights[n])
-                grads_t = grads_t - shifts[n] * sums[head, HEAD_DIM:] + by_columns(keys[n], dscores[n])
-                shifted_query[head] = (query_t[head] * -shifts[n]).astype(jnp.bfloat16)
-            attended[:, c] = jnp.transpose(attended_t.astype(jnp.bfloat16))
-            query_grads[:, c] = jnp.transpose((score_scale * grads_t).astype(jnp.bfloat16))
-            scaled_query[head] = (query_t[head] * factor).astype(jnp.bfloat16)
-            scaled_up[head] = (up_t[head] * factor).astype(jnp.bfloat16)
-
-
-def own_gradients(grown_t, slopes_t, scaled, head):
-    scaled_query, shifted_query, scaled_up = scaled
-    mixed = by_rows(grown_t[head], jnp.concatenate([scaled_up[head], shifted_query[head]], axis=0))
-    return mixed[:, :HEAD_DIM], mixed[:, HEAD_DIM:] + by_rows(slopes_t[head], scaled_query[head])
+        name="before_exchanges",
+    )(upstream, queries, stats, tops, *own, grown_t, slopes_t, *previous_values)
 
 
 def next_part(refs, later_query, group, heads, extra=None):
@@ -442,7 +475,13 @@
 
         @pl.when(jnp.logical_not(is_even()))
         def _():
-            add_past(past_in, first, results, heads)
+            for start in range(0, heads, GROUP):
+                group = range(start, min(start + GROUP, heads))
+                for head, part in zip(group, past_part(past_in, first, group, heads)):
+                    columns = pl.ds(head * HEAD_DIM, HEAD_DIM)
+                    results[0][:, columns], results[1][:, columns] = done_rows(past_in, part, head)
+                    for target, rows in zip(results[2:], scaled_rows(past_in, part, head)):
+                        target[head] = rows
 
     wide = jax.ShapeDtypeStruct((block_rows, width), jnp.float32)
     out = pl.pallas_call(
@@ -457,26 +496,30 @@
     return out[:5], out[5:]
 
 
-def second_half(keys, second_got, next_upstream, second_stats, later, next_bias, grown_t, slopes_t, past_refs, done, parts):
+def second_half(keys, second_got, next_upstream, second_stats, later, next_bias, grown_t, slopes_t, past_refs, done, parts, early):
     block_rows, width = keys.shape
     heads = width // HEAD_DIM
     past_count = len(past_refs)
 
     def kernel(k, second, nu, stats, later, next_bias, grown_t, slopes_t, *rest):
         past_in, rest = rest[:past_count], rest[past_count:]
-        done, (value_part, key_part), outs, rest = rest[:5], rest[5:7], rest[7:11], rest[11:]
-        here, (key_grads, value_grads, sems) = rest[:5], rest[5:]
+        done, (value_part, key_part), early, outs, rest = rest[:5], rest[5:7], rest[7:11], rest[11:15], rest[15:]
+        attended, query_grads, key_grads, value_grads, sems = rest
 
         def send(rows, i, slot, columns=slice(None)):
             copy = pltpu.make_async_copy(rows.at[:, columns], outs[i].at[:, columns], sems.at[slot])
             copy.start()
             return copy
 
-        def finish(rows, from_next):
-            copies = [send(rows[0], 0, 0), send(rows[1], 1, 1)]
+        def all_but_past():
+            copies = [send(done[0], 0, 0), send(done[1], 1, 1)]
             for start in range(0, heads, PAIR):
                 group = range(start, min(start + PAIR, heads))
-                for head, (value, key) in zip(group, from_next(group, rows[2:])):
+                parts = next_part(
+                    (k, nu, stats, later, next_bias), second, group, heads,
+                    lambda head: own_gradients(grown_t, slopes_t, [rows[head] for rows in done[2:]], head),
+                )
+                for head, (value, key) in zip(group, parts):
                     columns = pl.ds(head * HEAD_DIM, HEAD_DIM)
                     value_grads[:, columns] = value.astype(jnp.bfloat16)
                     key_grads[:, columns] = (score_scale * key).astype(jnp.bfloat16)
@@ -486,52 +529,68 @@
             for copy in copies:
                 copy.wait()
 
-        def added(group, scaled):
-            parts = []
-            for head in group:
-                value, key = own_gradients(grown_t, slopes_t, scaled, head)
-                columns = pl.ds(head * HEAD_DIM, HEAD_DIM)
-                parts.append([value + value_part[:, columns], key + key_part[:, columns]])
-            return parts
-
-        def computed(group, scaled):
-            return next_part(
-                (k, nu, stats, later, next_bias), second, group, heads,
-                lambda head: own_gradients(grown_t, slopes_t, scaled, head),
-            )
+        def all_but_next(past_key):
+            past = past_part(past_in, past_key, range(heads), heads)
+            copies = []
+            half = (heads + 1) // 2
+            groups = (range(half), range(half, heads))
+
+            def write_rows(group):
+                for head in group:
+                    columns = pl.ds(head * HEAD_DIM, HEAD_DIM)
+                    attended[:, columns], query_grads[:, columns] = done_rows(past_in, past[head], head)
+                columns = pl.ds(group.start * HEAD_DIM, len(group) * HEAD_DIM)
+                copies.append(send(attended, 0, len(copies), columns))
+                copies.append(send(query_grads, 1, len(copies), columns))
+
+            def write_gradients(group):
+                for head in group:
+                    value, key = own_gradients(grown_t, slopes_t, scaled_rows(past_in, past[head], head), head)
+                    columns = pl.ds(head * HEAD_DIM, HEAD_DIM)
+                    value_grads[:, columns] = (value + value_part[:, columns]).astype(jnp.bfloat16)
+                    key_grads[:, columns] = (score_scale * (key + key_part[:, columns])).astype(jnp.bfloat16)
+                columns = pl.ds(group.start * HEAD_DIM, len(group) * HEAD_DIM)
+                copies.append(send(key_grads, 2, len(copies), columns))
+                copies.append(send(value_grads, 3, len(copies), columns))
+
+            write_rows(groups[0])
+            write_rows(groups[1])
+            write_gradients(groups[0])
+            write_gradients(groups[1])
+            for copy in copies:
+                copy.wait()
 
         block = lax.axis_index("blk")
 
         @pl.when(block == 0)
         def _():
-            add_past(past_in, None, here, heads)
+            copies = [send(early[0], 0, 0), send(early[1], 1, 1)]
+            value_grads[...] = (early[2][...] + value_part[...]).astype(jnp.bfloat16)
+            key_grads[...] = (score_scale * (early[3][...] + key_part[...])).astype(jnp.bfloat16)
+            copies += [send(key_grads, 2, 2), send(value_grads, 3, 3)]
+            for copy in copies:
+                copy.wait()
 
         @pl.when(jnp.logical_and(is_even(), block > 0))
         def _():
-            add_past(past_in, second, here, heads)
-
-        @pl.when(is_even())
-        def _():
-            finish(here, added)
+            all_but_next(second)
 
         @pl.when(jnp.logical_not(is_even()))
         def _():
-            finish(done, computed)
+            all_but_past()
 
     return pl.pallas_call(
         kernel,
         out_shape=[bf16(block_rows, width)] * 4,
-        in_specs=[VMEM] * (15 + past_count),
+        in_specs=[VMEM] * (19 + past_count),
         out_specs=[ANY] * 4,
-        scratch_shapes=[pltpu.VMEM((block_rows, width), jnp.bfloat16)] * 2
-        + [pltpu.VMEM((heads, HEAD_DIM, block_rows), jnp.bfloat16)] * 3
-        + [pltpu.VMEM((block_rows, width), jnp.bfloat16)] * 2
-        + [pltpu.SemaphoreType.DMA((2 + 2 * heads,))],
+        scratch_shapes=[pltpu.VMEM((block_rows, width), jnp.bfloat16)] * 4
+        + [pltpu.SemaphoreType.DMA((4 * heads,))],
         compiler_params=pltpu.CompilerParams(vmem_limit_bytes=20 * 2**20),
         cost_estimate=weighed(0),
         name="second_half",
     )(
-        keys, second_got, next_upstream, second_stats, later, next_bias, grown_t, slopes_t, *past_refs, *done, *parts,
+        keys, second_got, next_upstream, second_stats, later, next_bias, grown_t, slopes_t, *past_refs, *done, *parts, *early,
     )
 
 
@@ -553,12 +612,15 @@
     )
     first_stats, second_stats = block_exchange(stats, 0), block_exchange(stats, 1)
     *own, later = own_products(keys, query_rows, upstream, values, grown_t, slopes_t, next_upstream)
-    past_values, dchances = past_dchances(upstream, previous)
+    past_values, dchances, *early = before_exchanges(
+        upstream, previous, query_rows, stats, tops, own, grown_t, slopes_t
+    )
     past_refs = (query_rows, stats, tops, *own, past_values, dchances, past_bias)
     done, parts = first_half(keys, first_got, next_upstream, first_stats, later, next_bias, past_refs)
     return tuple(
         second_half(
-            keys, second_got, next_upstream, second_stats, later, next_bias, grown_t, slopes_t, past_refs, done, parts
+            keys, second_got, next_upstream, second_stats, later, next_bias, grown_t, slopes_t, past_refs, done, parts,
+            early,
         )
     )
 

time: 23.7 us -> 23.6 us (level); the launches traced: 23.5 us -> 23.2 us
    pallas_call x1, Pallas kernels: 1.51 us -> 1.16 us  [second_half(): pl.pallas_call(kernel, out_shape=[bf16(block_rows, width)] * 4, in_specs=...]
  transfers between devices with their start and end apart: 11 -> 11, of which waited for: 3 -> 3; matrix products, arithmetic and copies ran while one was open for 0% -> 0% of each run, Pallas kernels for 14% -> 15%
where the time goes in v7:
time: 23.6 us; the launch traced here: 23.2 us
  starting transfers between devices  13.2 us (56%)
  Pallas kernels  6.04 us (26%)
  waiting for transfers between devices  3.14 us (13%)
  between operations  0.75 us (3%)
    ppermute x6, starting transfers between devices, block_exchange(): return lax.ppermute(rows, ('dp', 'blk', 'head'), route)  6.98 us
    ppermute x5, starting transfers between devices, partner_exchange(): return lax.ppermute(rows, 'head', route)  6.26 us
    ppermute x5, waiting for transfers between devices, partner_exchange(): return lax.ppermute(rows, 'head', route)  2.28 us
    pallas_call x1, Pallas kernels, cut_pieces(): pl.pallas_call(kernel, out_shape=[bf16(height, width) for height in heigh...  1.31 us
    pallas_call x1, Pallas kernels, second_half(): pl.pallas_call(kernel, out_shape=[bf16(block_rows, width)] * 4, in_specs=...  1.16 us
    pallas_call x1, Pallas kernels, first_half(): pl.pallas_call(kernel, out_shape=[bf16(block_rows, width)] * 2 + [bf16(he...  0.96 us
    ppermute x6, waiting for transfers between devices, block_exchange(): return lax.ppermute(rows, ('dp', 'blk', 'head'), route)  0.87 us
    pallas_call x1, Pallas kernels, stack_far_values(): pl.pallas_call(kernel, out_shape=[jax.ShapeDtypeStruct((block_rows, block...  0.73 us
  transfers between devices with their start and end apart: 11, of which 3 were waited for; matrix products, arithmetic and copies ran while one was open for 0% of the time, Pallas kernels for 15%

profile of v7, /device:TPU:0, one launch (start us, length us, event | category | flops | bytes accessed | tf_op | source)
XLA Modules:
  0.0 23.2 jit_solution(16943980875202584529)
XLA Ops:
  0.6 0.0 copy-start
  0.6 1.3 %cut_pieces.1 = (bf16[256,512]{1,0:T(8,128)(2,1)S(1)}, bf16[256,512]{1,0:T(8,128)(2,1)S(1)}, bf16[128,512]{1,0:T(8,128)(2,1)S(1)}, bf16[128,512]{1,0:T(8,128)(2,1)S(1)}) custom-call(bf16[64,2048]{1,0:T(8,128)(2,1)} %q.1, bf16[64,2048]{1,0:T(8,128)(2,1)} %k.1, bf16[64,2048]{1,0:T(8,128)(2,1)} %v.1), custom_call_target="tpu_custom_call" | custom-call | tf_op jit(solution)/shard_map/cut_pieces/pallas_call | solution.py:87
  2.0 0.5 %collective-permute-start = (bf16[256,512]{1,0:T(8,128)(2,1)S(1)}, bf16[256,512]{1,0:T(8,128)(2,1)S(1)}, u32[]{:S(2)}, u32[]{:S(2)}) collective-permute-start(bf16[256,512]{1,0:T(8,128)(2,1)S(1)} %get-tuple-element.45), channel_id=1, source_target_pairs={{0,1},{1,0},{2,3},{3,2},{4,5},{5,4},{6,7},{7,6},{8,9},{9,8},{10,11... | collective-permute-start | bytes 786440 | tf_op jit(solution)/shard_map/ppermute | solution.py:29
  2.5 2.6 %collective-permute-start.1 = (bf16[128,512]{1,0:T(8,128)(2,1)S(1)}, bf16[128,512]{1,0:T(8,128)(2,1)S(1)}, u32[]{:S(2)}, u32[]{:S(2)}) collective-permute-start(bf16[128,512]{1,0:T(8,128)(2,1)S(1)} %get-tuple-element.46), channel_id=1, source_target_pairs={{0,2},{1,3},{2,0},{3,1},{4,6},{5,7},{6,4},{7,5},{8,10},{9,11},{10,... | collective-permute-start | bytes 393224 | tf_op jit(solution)/shard_map/ppermute | solution.py:29
  5.0 0.1 collective-permute-start.2
  5.1 0.0 collective-permute-done.refs_1_.theirs.rest_1_
  5.1 0.0 copy-done
  5.2 0.0 copy-start.1
  5.2 1.9 %collective-permute-start.4 = (bf16[256,512]{1,0:T(8,128)(2,1)S(1)}, bf16[256,512]{1,0:T(8,128)(2,1)S(1)}, u32[]{:S(2)}, u32[]{:S(2)}) collective-permute-start(bf16[256,512]{1,0:T(8,128)(2,1)S(1)} %get-tuple-element.50), channel_id=1, source_target_pairs={{0,4},{1,5},{2,6},{3,7},{4,0},{5,1},{6,2},{7,3},{8,12},{9,13},{10,... | collective-permute-start | bytes 786440 | tf_op jit(solution)/shard_map/ppermute | solution.py:44
  7.0 0.1 collective-permute-start.5
  7.1 0.0 copy-done.1
  7.1 0.7 %stack_far_values.1 = (f32[256,256]{1,0:T(8,128)S(1)}, f32[256,256]{1,0:T(8,128)S(1)}, f32[256,256]{1,0:T(8,128)S(1)}, bf16[128,512]{1,0:T(8,128)(2,1)S(1)}) custom-call(bf16[256,512]{1,0:T(8,128)(2,1)S(1)} %get-tuple-element.44.refs_0_.mine.rest_0_, bf16[256,512]{1,0:T(8,128)(2,1)S(1)} %collective-permute-done.refs_1_.theirs.rest_1_, s32[4]{0:T(128)S(1)} %copy-done.1), custom_call_target="tpu_custom_call" | custom-call | flops 5000000000 | tf_op jit(solution)/shard_map/stack_far_values/pallas_call | solution.py:115
  7.9 1.6 %collective-permute-start.6 = (bf16[128,512]{1,0:T(8,128)(2,1)S(1)}, bf16[128,512]{1,0:T(8,128)(2,1)S(1)}, u32[]{:S(2)}, u32[]{:S(2)}) collective-permute-start(bf16[128,512]{1,0:T(8,128)(2,1)S(1)} %get-tuple-element.55), channel_id=1, source_target_pairs={{0,2},{1,3},{2,0},{3,1},{4,6},{5,7},{6,4},{7,5},{8,10},{9,11},{10,... | collective-permute-start | bytes 393224 | tf_op jit(solution)/shard_map/ppermute | solution.py:29
  9.4 0.0 collective-permute-done.1.refs_2_
  9.4 2.3 %collective-permute-done.2.refs_3_ = bf16[128,512]{1,0:T(8,128)(2,1)S(1)} collective-permute-done((bf16[128,512]{1,0:T(8,128)(2,1)S(1)}, bf16[128,512]{1,0:T(8,128)(2,1)S(1)}, u32[]{:S(2)}, u32[]{:S(2)}) %collective-permute-start.2) | collective-permute-done | bytes 131104 | tf_op jit(solution)/shard_map/ppermute | solution.py:29
  11.7 0.1 join_keys_queries.1
  11.8 1.7 %collective-permute-start.9 = (bf16[256,512]{1,0:T(8,128)(2,1)S(1)}, bf16[256,512]{1,0:T(8,128)(2,1)S(1)}, u32[]{:S(2)}, u32[]{:S(2)}) collective-permute-start(bf16[256,512]{1,0:T(8,128)(2,1)S(1)} %get-tuple-element.72), channel_id=1, source_target_pairs={{0,4},{1,5},{2,6},{3,7},{4,0},{5,1},{6,2},{7,3},{8,12},{9,13},{10,... | collective-permute-start | bytes 786440 | tf_op jit(solution)/shard_map/ppermute | solution.py:44
  13.5 0.6 %collective-permute-start.3 = (bf16[256,512]{1,0:T(8,128)(2,1)S(1)}, bf16[256,512]{1,0:T(8,128)(2,1)S(1)}, u32[]{:S(2)}, u32[]{:S(2)}) collective-permute-start(bf16[256,512]{1,0:T(8,128)(2,1)S(1)} %get-tuple-element.49), channel_id=1, source_target_pairs={{0,1},{1,0},{2,3},{3,2},{4,8},{5,9},{6,10},{7,11},{8,4},{9,5},{10,... | collective-permute-start | bytes 786440 | tf_op jit(solution)/shard_map/ppermute | solution.py:44
  14.1 0.0 collective-permute-done.4.first
  14.1 0.0 collective-permute-done.5.second
  14.1 1.6 %collective-permute-start.8 = (bf16[128,512]{1,0:T(8,128)(2,1)S(1)}, bf16[128,512]{1,0:T(8,128)(2,1)S(1)}, u32[]{:S(2)}, u32[]{:S(2)}) collective-permute-start(bf16[128,512]{1,0:T(8,128)(2,1)S(1)} %get-tuple-element.68), channel_id=1, source_target_pairs={{0,2},{1,3},{2,0},{3,1},{4,6},{5,7},{6,4},{7,5},{8,10},{9,11},{10,... | collective-permute-start | bytes 393224 | tf_op jit(solution)/shard_map/ppermute | solution.py:29
  15.7 0.0 collective-permute-done.6.rest_2_
  15.7 0.7 %own_scores.1 = (bf16[256,512]{1,0:T(8,128)(2,1)S(1)}, f32[8,256]{1,0:T(8,128)S(1)}, f32[4,256]{1,0:T(4,128)S(1)}, bf16[4,256,256]{2,1,0:T(8,128)(2,1)S(1)}, bf16[4,256,256]{2,1,0:T(8,128)(2,1)S(1)}) custom-call(bf16[256,512]{1,0:T(8,128)(2,1)S(1)} %get-tuple-element.48.k, bf16[256,512]{1,0:T(8,128)(2,1)S(1)} %get-tuple-element.53.q.rest_0_, ...), custom_call_target="tpu_custom_call" | custom-call | tf_op jit(solution)/shard_map/own_scores/pallas_call | solution.py:281
  16.4 2.7 %collective-permute-start.10 = (f32[8,256]{1,0:T(8,128)S(1)}, f32[8,256]{1,0:T(8,128)S(1)}, u32[]{:S(2)}, u32[]{:S(2)}) collective-permute-start(f32[8,256]{1,0:T(8,128)S(1)} %get-tuple-element.56.own_stats.rest_1_), channel_id=1, source_target_pairs={{0,4},{1,5},{2,6},{3,7},{4,0},{5,1},{6,2},{7,3},{8,12},{9,13},{10,... | collective-permute-start | bytes 24584 | tf_op jit(solution)/shard_map/ppermute | solution.py:44
  19.1 0.0 collective-permute-start.7
  19.1 0.5 %own_products.1 = (f32[4,256,256]{2,1,0:T(8,128)S(1)}, f32[4,128,256]{2,1,0:T(8,128)S(1)}, f32[4,128,256]{2,1,0:T(8,128)S(1)}, f32[4,128,256]{2,1,0:T(8,128)S(1)}, f32[4,256,256]{2,1,0:T(8,128)S(1)}) custom-call(bf16[256,512]{1,0:T(8,128)(2,1)S(1)} %get-tuple-element.48.k, bf16[256,512]{1,0:T(8,128)(2,1)S(1)} %get-tuple-element.53.q.rest_0_, ...), custom_call_target="tpu_custom_call" | custom-call | flops 1000000000 | tf_op jit(solution)/shard_map/own_products/pallas_call | solution.py:315
  19.6 0.0 collective-permute-done.8.rest_1_
  19.7 0.5 %before_exchanges.1 = (bf16[4,128,256]{2,1,0:T(8,128)(2,1)S(1)}, f32[4,256,256]{2,1,0:T(8,128)S(1)}, bf16[256,512]{1,0:T(8,128)(2,1)S(1)}, bf16[256,512]{1,0:T(8...) custom-call(bf16[256,512]{1,0:T(8,128)(2,1)S(1)} %copy-done, ...), custom_call_target="tpu_custom_call" | custom-call | flops 1000000000 | tf_op jit(solution)/shard_map/before_exchanges/pallas_call | solution.py:413
  20.2 0.8 %collective-permute-done.9.first = bf16[256,512]{1,0:T(8,128)(2,1)S(1)} collective-permute-done((bf16[256,512]{1,0:T(8,128)(2,1)S(1)}, bf16[256,512]{1,0:T(8,128)(2,1)S(1)}, u32[]{:S(2)}, u32[]{:S(2)}) %collective-permute-start.9) | collective-permute-done | bytes 262176 | tf_op jit(solution)/shard_map/ppermute | solution.py:44
  20.9 0.1 collective-permute-done.10.stats
  21.0 1.0 %first_half.1 = (bf16[256,512]{1,0:T(8,128)(2,1)S(1)}, bf16[256,512]{1,0:T(8,128)(2,1)S(1)}, bf16[4,128,256]{2,1,0:T(8,128)(2,1)S(1)}, bf16[4,128,256]{2,1,0:T(8...) custom-call(bf16[256,512]{1,0:T(8,128)(2,1)S(1)} %get-tuple-element.48.k, ...), custom_call_target="tpu_custom_call" | custom-call | tf_op jit(solution)/shard_map/first_half/pallas_call | solution.py:487
  22.0 0.0 collective-permute-done.3.second
  22.0 0.0 collective-permute-done.7.stats
  22.0 1.2 %second_half.1 = (bf16[256,512]{1,0:T(8,128)(2,1)}, bf16[256,512]{1,0:T(8,128)(2,1)}, bf16[256,512]{1,0:T(8,128)(2,1)}, bf16[256,512]{1,0:T(8,128)(2,1)}) custom-call(bf16[256,512]{1,0:T(8,128)(2,1)S(1)} %get-tuple-element.48.k, bf16[256,512]{1,0:T(8,128)(2,1)S(1)} %collective-permute-done.3.second, bf16[256,512]{1,0:T(8,128)(2,1)S(1)} %get-tuple-element.52._.nu, ...), custom_call_target="tpu_custom_call" | custom-call | tf_op jit(solution)/shard_map/second_half/pallas_call | solution.py:582
  (2 shorter events, 0.1 us)
Async XLA Ops:
  0.6 4.5 %copy-start = (bf16[256,512]{1,0:T(8,128)(2,1)S(1)}, bf16[256,512]{1,0:T(8,128)(2,1)}, u32[]{:S(2)}) copy-start(bf16[256,512]{1,0:T(8,128)(2,1)} %u.7) | copy-start | bytes 786436
  2.0 3.2 %collective-permute-start = (bf16[256,512]{1,0:T(8,128)(2,1)S(1)}, bf16[256,512]{1,0:T(8,128)(2,1)S(1)}, u32[]{:S(2)}, u32[]{:S(2)}) collective-permute-start(bf16[256,512]{1,0:T(8,128)(2,1)S(1)} %get-tuple-element.45), channel_id=1, source_target_pairs={{0,1},{1,0},{2,3},{3,2},{4,5},{5,4},{6,7},{7,6},{8,9},{9,8},{10,11... | collective-permute-start | bytes 786440 | tf_op jit(solution)/shard_map/ppermute | solution.py:29
  2.5 6.9 %collective-permute-start.1 = (bf16[128,512]{1,0:T(8,128)(2,1)S(1)}, bf16[128,512]{1,0:T(8,128)(2,1)S(1)}, u32[]{:S(2)}, u32[]{:S(2)}) collective-permute-start(bf16[128,512]{1,0:T(8,128)(2,1)S(1)} %get-tuple-element.46), channel_id=1, source_target_pairs={{0,2},{1,3},{2,0},{3,1},{4,6},{5,7},{6,4},{7,5},{8,10},{9,11},{10,... | collective-permute-start | bytes 393224 | tf_op jit(solution)/shard_map/ppermute | solution.py:29
  5.0 6.6 %collective-permute-start.2 = (bf16[128,512]{1,0:T(8,128)(2,1)S(1)}, bf16[128,512]{1,0:T(8,128)(2,1)S(1)}, u32[]{:S(2)}, u32[]{:S(2)}) collective-permute-start(bf16[128,512]{1,0:T(8,128)(2,1)S(1)} %get-tuple-element.47), channel_id=1, source_target_pairs={{0,3},{1,2},{2,1},{3,0},{4,7},{5,6},{6,5},{7,4},{8,11},{9,10},{10,... | collective-permute-start | bytes 393224 | tf_op jit(solution)/shard_map/ppermute | solution.py:29
  5.2 2.0 %copy-start.1 = (s32[4]{0:T(128)S(1)}, s32[4]{0:T(128)}, u32[]{:S(2)}) copy-start(s32[4]{0:T(128)} %lengths.1) | copy-start | bytes 52
  5.2 8.9 %collective-permute-start.4 = (bf16[256,512]{1,0:T(8,128)(2,1)S(1)}, bf16[256,512]{1,0:T(8,128)(2,1)S(1)}, u32[]{:S(2)}, u32[]{:S(2)}) collective-permute-start(bf16[256,512]{1,0:T(8,128)(2,1)S(1)} %get-tuple-element.50), channel_id=1, source_target_pairs={{0,4},{1,5},{2,6},{3,7},{4,0},{5,1},{6,2},{7,3},{8,12},{9,13},{10,... | collective-permute-start | bytes 786440 | tf_op jit(solution)/shard_map/ppermute | solution.py:44
  7.0 7.1 %collective-permute-start.5 = (bf16[256,512]{1,0:T(8,128)(2,1)S(1)}, bf16[256,512]{1,0:T(8,128)(2,1)S(1)}, u32[]{:S(2)}, u32[]{:S(2)}) collective-permute-start(bf16[256,512]{1,0:T(8,128)(2,1)S(1)} %get-tuple-element.51), channel_id=1, source_target_pairs={{0,1},{1,0},{2,3},{3,2},{4,8},{5,9},{6,10},{7,11},{8,4},{9,5},{10,... | collective-permute-start | bytes 786440 | tf_op jit(solution)/shard_map/ppermute | solution.py:44
  7.9 7.9 %collective-permute-start.6 = (bf16[128,512]{1,0:T(8,128)(2,1)S(1)}, bf16[128,512]{1,0:T(8,128)(2,1)S(1)}, u32[]{:S(2)}, u32[]{:S(2)}) collective-permute-start(bf16[128,512]{1,0:T(8,128)(2,1)S(1)} %get-tuple-element.55), channel_id=1, source_target_pairs={{0,2},{1,3},{2,0},{3,1},{4,6},{5,7},{6,4},{7,5},{8,10},{9,11},{10,... | collective-permute-start | bytes 393224 | tf_op jit(solution)/shard_map/ppermute | solution.py:29
  11.8 9.2 %collective-permute-start.9 = (bf16[256,512]{1,0:T(8,128)(2,1)S(1)}, bf16[256,512]{1,0:T(8,128)(2,1)S(1)}, u32[]{:S(2)}, u32[]{:S(2)}) collective-permute-start(bf16[256,512]{1,0:T(8,128)(2,1)S(1)} %get-tuple-element.72), channel_id=1, source_target_pairs={{0,4},{1,5},{2,6},{3,7},{4,0},{5,1},{6,2},{7,3},{8,12},{9,13},{10,... | collective-permute-start | bytes 786440 | tf_op jit(solution)/shard_map/ppermute | solution.py:44
  13.5 8.5 %collective-permute-start.3 = (bf16[256,512]{1,0:T(8,128)(2,1)S(1)}, bf16[256,512]{1,0:T(8,128)(2,1)S(1)}, u32[]{:S(2)}, u32[]{:S(2)}) collective-permute-start(bf16[256,512]{1,0:T(8,128)(2,1)S(1)} %get-tuple-element.49), channel_id=1, source_target_pairs={{0,1},{1,0},{2,3},{3,2},{4,8},{5,9},{6,10},{7,11},{8,4},{9,5},{10,... | collective-permute-start | bytes 786440 | tf_op jit(solution)/shard_map/ppermute | solution.py:44
  14.1 5.5 %collective-permute-start.8 = (bf16[128,512]{1,0:T(8,128)(2,1)S(1)}, bf16[128,512]{1,0:T(8,128)(2,1)S(1)}, u32[]{:S(2)}, u32[]{:S(2)}) collective-permute-start(bf16[128,512]{1,0:T(8,128)(2,1)S(1)} %get-tuple-element.68), channel_id=1, source_target_pairs={{0,2},{1,3},{2,0},{3,1},{4,6},{5,7},{6,4},{7,5},{8,10},{9,11},{10,... | collective-permute-start | bytes 393224 | tf_op jit(solution)/shard_map/ppermute | solution.py:29
  16.4 4.6 %collective-permute-start.10 = (f32[8,256]{1,0:T(8,128)S(1)}, f32[8,256]{1,0:T(8,128)S(1)}, u32[]{:S(2)}, u32[]{:S(2)}) collective-permute-start(f32[8,256]{1,0:T(8,128)S(1)} %get-tuple-element.56.own_stats.rest_1_), channel_id=1, source_target_pairs={{0,4},{1,5},{2,6},{3,7},{4,0},{5,1},{6,2},{7,3},{8,12},{9,13},{10,... | collective-permute-start | bytes 24584 | tf_op jit(solution)/shard_map/ppermute | solution.py:44
  19.1 2.9 %collective-permute-start.7 = (f32[8,256]{1,0:T(8,128)S(1)}, f32[8,256]{1,0:T(8,128)S(1)}, u32[]{:S(2)}, u32[]{:S(2)}) collective-permute-start(f32[8,256]{1,0:T(8,128)S(1)} %get-tuple-element.56.own_stats.rest_1_), channel_id=1, source_target_pairs={{0,1},{1,0},{2,3},{3,2},{4,8},{5,9},{6,10},{7,11},{8,4},{9,5},{10,... | collective-permute-start | bytes 24584 | tf_op jit(solution)/shard_map/ppermute | solution.py:44

commit v8 on v7

--- a/solution.py
+++ b/solution.py
@@ -26,6 +26,22 @@
 
 def partner_exchange(rows, step):
     route = [(i, i ^ step) for i in range(lax.axis_size("head"))]
+    return lax.ppermute(rows, "head", route)
+
+
+def sent_step(step, sharer):
+    if step < 2:
+        return step
+    above = sharer // (1 << (step.bit_length() - 1)) % 2
+    return step - step % 2 + (above if step % 2 == 0 else 1 - above)
+
+
+def got_step(step, sharer):
+    return step if step < 2 else sent_step(step ^ 1, sharer)
+
+
+def pieces_exchange(rows, step):
+    route = [(i, i ^ sent_step(step, i)) for i in range(lax.axis_size("head"))]
     return lax.ppermute(rows, "head", route)
 
 
@@ -75,10 +91,10 @@
             copies.append(pltpu.make_async_copy(source, target, sems.at[len(copies)]))
 
         for step in range(sharers):
-            columns = place(step, width)
+            columns = place(sent_step(step, lax.axis_index("head")), width)
             copy(k.at[:, columns], pieces[step].at[pl.ds(0, rows)])
             copy(q.at[:, columns], pieces[step].at[pl.ds(rows, rows)])
-            copy(v.at[:, columns], pieces[step % 2].at[pl.ds((2 + step // 2) * rows, rows)])
+            copy(v.at[:, place(step, width)], pieces[step % 2].at[pl.ds((2 + step // 2) * rows, rows)])
         for c in copies:
             c.start()
         for c in copies:
@@ -166,7 +182,7 @@
         pieces_in = refs[:sharers]
         keys, queries, first, second = refs[sharers:]
         for step in range(sharers):
-            where = place(step, rows)
+            where = place(got_step(step, lax.axis_index("head")), rows)
             keys[where, :] = pieces_in[step][pl.ds(0, rows), :]
             queries[where, :] = pieces_in[step][pl.ds(rows, rows), :]
 
@@ -598,7 +614,7 @@
     sharers = lax.axis_size("head")
     rows = queries.shape[0]
     pieces = cut_pieces(queries, key_states, value_states)
-    pieces = [pieces[0]] + [partner_exchange(pieces[step], step) for step in range(1, sharers)]
+    pieces = [pieces[0]] + [pieces_exchange(pieces[step], step) for step in range(1, sharers)]
     first, second = stack_values(pieces[0], pieces[1], upstream, rows)
     first_got, second_got = block_exchange(first, 0), block_exchange(second, 1)
     far_values, (own_bias, past_bias, next_bias) = stack_far_values(pieces[0], pieces[1], clip_lengths, rows)

time: 23.6 us -> 23.6 us (level)
  the two profiles are of different devices: /device:TPU:0 before, /device:TPU:19 now
where the time goes in v8:
time: 23.6 us; the launch traced here: 23.4 us
  waiting for transfers between devices  8.48 us (36%)
  starting transfers between devices  7.27 us (31%)
  Pallas kernels  6.95 us (29%)
  between operations  0.74 us (3%)
    ppermute x3, waiting for transfers between devices, pieces_exchange(): return lax.ppermute(rows, 'head', route)  4.55 us
    ppermute x6, starting transfers between devices, block_exchange(): return lax.ppermute(rows, ('dp', 'blk', 'head'), route)  3.68 us
    ppermute x6, waiting for transfers between devices, block_exchange(): return lax.ppermute(rows, ('dp', 'blk', 'head'), route)  2.73 us
    pallas_call x1, Pallas kernels, second_half(): pl.pallas_call(kernel, out_shape=[bf16(block_rows, width)] * 4, in_specs=...  2.24 us
    ppermute x3, starting transfers between devices, pieces_exchange(): return lax.ppermute(rows, 'head', route)  2.21 us
    ppermute x2, starting transfers between devices, partner_exchange(): return lax.ppermute(rows, 'head', route)  1.38 us
    pallas_call x1, Pallas kernels, cut_pieces(): pl.pallas_call(kernel, out_shape=[bf16(height, width) for height in heigh...  1.31 us
    ppermute x2, waiting for transfers between devices, partner_exchange(): return lax.ppermute(rows, 'head', route)  1.2 us
  transfers between devices with their start and end apart: 11, of which 6 were waited for; matrix products, arithmetic and copies ran while one was open for 0% of the time, Pallas kernels for 15%

profile of v8, /device:TPU:19, one launch (start us, length us, event | category | flops | bytes accessed | tf_op | source)
XLA Modules:
  0.0 23.4 jit_solution(4923896362158575009)
XLA Ops:
  0.6 0.0 copy-start
  0.6 1.3 %cut_pieces.1 = (bf16[256,512]{1,0:T(8,128)(2,1)S(1)}, bf16[256,512]{1,0:T(8,128)(2,1)S(1)}, bf16[128,512]{1,0:T(8,128)(2,1)S(1)}, bf16[128,512]{1,0:T(8,128)(2,1)S(1)}) custom-call(bf16[64,2048]{1,0:T(8,128)(2,1)} %q.1, bf16[64,2048]{1,0:T(8,128)(2,1)} %k.1, bf16[64,2048]{1,0:T(8,128)(2,1)} %v.1), custom_call_target="tpu_custom_call" | custom-call | tf_op jit(solution)/shard_map/cut_pieces/pallas_call | solution.py:103
  2.0 0.7 %collective-permute-start = (bf16[256,512]{1,0:T(8,128)(2,1)S(1)}, bf16[256,512]{1,0:T(8,128)(2,1)S(1)}, u32[]{:S(2)}, u32[]{:S(2)}) collective-permute-start(bf16[256,512]{1,0:T(8,128)(2,1)S(1)} %get-tuple-element.45), channel_id=1, source_target_pairs={{0,1},{1,0},{2,3},{3,2},{4,5},{5,4},{6,7},{7,6},{8,9},{9,8},{10,11... | collective-permute-start | bytes 786440 | tf_op jit(solution)/shard_map/ppermute | solution.py:45
  2.7 0.2 collective-permute-start.1
  2.9 1.3 %collective-permute-start.2 = (bf16[128,512]{1,0:T(8,128)(2,1)S(1)}, bf16[128,512]{1,0:T(8,128)(2,1)S(1)}, u32[]{:S(2)}, u32[]{:S(2)}) collective-permute-start(bf16[128,512]{1,0:T(8,128)(2,1)S(1)} %get-tuple-element.47), channel_id=1, source_target_pairs={{0,3},{1,2},{2,0},{3,1},{4,7},{5,6},{6,4},{7,5},{8,11},{9,10},{10,... | collective-permute-start | bytes 393224 | tf_op jit(solution)/shard_map/ppermute | solution.py:45
  4.2 0.0 collective-permute-done.refs_1_.theirs.rest_1_
  4.2 0.0 copy-done
  4.2 0.0 copy-start.1
  4.2 1.4 %collective-permute-start.4 = (bf16[256,512]{1,0:T(8,128)(2,1)S(1)}, bf16[256,512]{1,0:T(8,128)(2,1)S(1)}, u32[]{:S(2)}, u32[]{:S(2)}) collective-permute-start(bf16[256,512]{1,0:T(8,128)(2,1)S(1)} %get-tuple-element.50), channel_id=1, source_target_pairs={{0,4},{1,5},{2,6},{3,7},{4,0},{5,1},{6,2},{7,3},{8,12},{9,13},{10,... | collective-permute-start | bytes 786440 | tf_op jit(solution)/shard_map/ppermute | solution.py:60
  5.6 0.0 collective-permute-start.5
  5.6 0.0 copy-done.1
  5.6 0.7 %stack_far_values.1 = (f32[256,256]{1,0:T(8,128)S(1)}, f32[256,256]{1,0:T(8,128)S(1)}, f32[256,256]{1,0:T(8,128)S(1)}, bf16[128,512]{1,0:T(8,128)(2,1)S(1)}) custom-call(bf16[256,512]{1,0:T(8,128)(2,1)S(1)} %get-tuple-element.44.refs_0_.mine.rest_0_, bf16[256,512]{1,0:T(8,128)(2,1)S(1)} %collective-permute-done.refs_1_.theirs.rest_1_, s32[4]{0:T(128)S(1)} %copy-done.1), custom_call_target="tpu_custom_call" | custom-call | flops 5000000000 | tf_op jit(solution)/shard_map/stack_far_values/pallas_call | solution.py:131
  6.3 0.6 %collective-permute-start.6 = (bf16[128,512]{1,0:T(8,128)(2,1)S(1)}, bf16[128,512]{1,0:T(8,128)(2,1)S(1)}, u32[]{:S(2)}, u32[]{:S(2)}) collective-permute-start(bf16[128,512]{1,0:T(8,128)(2,1)S(1)} %get-tuple-element.55), channel_id=1, source_target_pairs={{0,2},{1,3},{2,0},{3,1},{4,6},{5,7},{6,4},{7,5},{8,10},{9,11},{10,... | collective-permute-start | bytes 393224 | tf_op jit(solution)/shard_map/ppermute | solution.py:29
  6.9 0.8 %collective-permute-done.1.refs_2_ = bf16[128,512]{1,0:T(8,128)(2,1)S(1)} collective-permute-done((bf16[128,512]{1,0:T(8,128)(2,1)S(1)}, bf16[128,512]{1,0:T(8,128)(2,1)S(1)}, u32[]{:S(2)}, u32[]{:S(2)}) %collective-permute-start.1) | collective-permute-done | bytes 131104 | tf_op jit(solution)/shard_map/ppermute | solution.py:45
  7.8 3.7 %collective-permute-done.2.refs_3_ = bf16[128,512]{1,0:T(8,128)(2,1)S(1)} collective-permute-done((bf16[128,512]{1,0:T(8,128)(2,1)S(1)}, bf16[128,512]{1,0:T(8,128)(2,1)S(1)}, u32[]{:S(2)}, u32[]{:S(2)}) %collective-permute-start.2) | collective-permute-done | bytes 131104 | tf_op jit(solution)/shard_map/ppermute | solution.py:45
  11.5 0.1 join_keys_queries.1
  11.6 1.4 %collective-permute-start.9 = (bf16[256,512]{1,0:T(8,128)(2,1)S(1)}, bf16[256,512]{1,0:T(8,128)(2,1)S(1)}, u32[]{:S(2)}, u32[]{:S(2)}) collective-permute-start(bf16[256,512]{1,0:T(8,128)(2,1)S(1)} %get-tuple-element.72), channel_id=1, source_target_pairs={{0,4},{1,5},{2,6},{3,7},{4,0},{5,1},{6,2},{7,3},{8,12},{9,13},{10,... | collective-permute-start | bytes 786440 | tf_op jit(solution)/shard_map/ppermute | solution.py:60
  12.9 0.0 collective-permute-start.3
  12.9 0.0 collective-permute-done.4.first
  12.9 0.0 collective-permute-done.5.second
  12.9 0.1 cut_previous_values.1
  13.0 0.8 %collective-permute-start.8 = (bf16[128,512]{1,0:T(8,128)(2,1)S(1)}, bf16[128,512]{1,0:T(8,128)(2,1)S(1)}, u32[]{:S(2)}, u32[]{:S(2)}) collective-permute-start(bf16[128,512]{1,0:T(8,128)(2,1)S(1)} %get-tuple-element.68), channel_id=1, source_target_pairs={{0,2},{1,3},{2,0},{3,1},{4,6},{5,7},{6,4},{7,5},{8,10},{9,11},{10,... | collective-permute-start | bytes 393224 | tf_op jit(solution)/shard_map/ppermute | solution.py:29
  13.8 0.0 collective-permute-done.6.rest_2_
  13.8 0.7 %own_scores.1 = (bf16[256,512]{1,0:T(8,128)(2,1)S(1)}, f32[8,256]{1,0:T(8,128)S(1)}, f32[4,256]{1,0:T(4,128)S(1)}, bf16[4,256,256]{2,1,0:T(8,128)(2,1)S(1)}, bf16[4,256,256]{2,1,0:T(8,128)(2,1)S(1)}) custom-call(bf16[256,512]{1,0:T(8,128)(2,1)S(1)} %get-tuple-element.48.k, bf16[256,512]{1,0:T(8,128)(2,1)S(1)} %get-tuple-element.53.q.rest_0_, ...), custom_call_target="tpu_custom_call" | custom-call | tf_op jit(solution)/shard_map/own_scores/pallas_call | solution.py:297
  14.5 1.0 %collective-permute-start.10 = (f32[8,256]{1,0:T(8,128)S(1)}, f32[8,256]{1,0:T(8,128)S(1)}, u32[]{:S(2)}, u32[]{:S(2)}) collective-permute-start(f32[8,256]{1,0:T(8,128)S(1)} %get-tuple-element.56.own_stats.rest_1_), channel_id=1, source_target_pairs={{0,4},{1,5},{2,6},{3,7},{4,0},{5,1},{6,2},{7,3},{8,12},{9,13},{10,... | collective-permute-start | bytes 24584 | tf_op jit(solution)/shard_map/ppermute | solution.py:60
  15.4 0.0 collective-permute-start.7
  15.4 0.5 %own_products.1 = (f32[4,256,256]{2,1,0:T(8,128)S(1)}, f32[4,128,256]{2,1,0:T(8,128)S(1)}, f32[4,128,256]{2,1,0:T(8,128)S(1)}, f32[4,128,256]{2,1,0:T(8,128)S(1)}, f32[4,256,256]{2,1,0:T(8,128)S(1)}) custom-call(bf16[256,512]{1,0:T(8,128)(2,1)S(1)} %get-tuple-element.48.k, bf16[256,512]{1,0:T(8,128)(2,1)S(1)} %get-tuple-element.53.q.rest_0_, ...), custom_call_target="tpu_custom_call" | custom-call | flops 1000000000 | tf_op jit(solution)/shard_map/own_products/pallas_call | solution.py:331
  16.0 1.2 %collective-permute-done.8.rest_1_ = bf16[128,512]{1,0:T(8,128)(2,1)S(1)} collective-permute-done((bf16[128,512]{1,0:T(8,128)(2,1)S(1)}, bf16[128,512]{1,0:T(8,128)(2,1)S(1)}, u32[]{:S(2)}, u32[]{:S(2)}) %collective-permute-start.8) | collective-permute-done | bytes 131104 | tf_op jit(solution)/shard_map/ppermute | solution.py:29
  17.2 0.3 %before_exchanges.1 = (bf16[4,128,256]{2,1,0:T(8,128)(2,1)S(1)}, f32[4,256,256]{2,1,0:T(8,128)S(1)}, bf16[256,512]{1,0:T(8,128)(2,1)S(1)}, bf16[256,512]{1,0:T(8...) custom-call(bf16[256,512]{1,0:T(8,128)(2,1)S(1)} %copy-done, ...), custom_call_target="tpu_custom_call" | custom-call | flops 1000000000 | tf_op jit(solution)/shard_map/before_exchanges/pallas_call | solution.py:429
  17.5 2.5 %collective-permute-done.9.first = bf16[256,512]{1,0:T(8,128)(2,1)S(1)} collective-permute-done((bf16[256,512]{1,0:T(8,128)(2,1)S(1)}, bf16[256,512]{1,0:T(8,128)(2,1)S(1)}, u32[]{:S(2)}, u32[]{:S(2)}) %collective-permute-start.9) | collective-permute-done | bytes 262176 | tf_op jit(solution)/shard_map/ppermute | solution.py:60
  20.0 0.1 collective-permute-done.10.stats
  20.1 1.0 %first_half.1 = (bf16[256,512]{1,0:T(8,128)(2,1)S(1)}, bf16[256,512]{1,0:T(8,128)(2,1)S(1)}, bf16[4,128,256]{2,1,0:T(8,128)(2,1)S(1)}, bf16[4,128,256]{2,1,0:T(8...) custom-call(bf16[256,512]{1,0:T(8,128)(2,1)S(1)} %get-tuple-element.48.k, ...), custom_call_target="tpu_custom_call" | custom-call | tf_op jit(solution)/shard_map/first_half/pallas_call | solution.py:503
  21.0 0.0 collective-permute-done.3.second
  21.1 0.1 collective-permute-done.7.stats
  21.2 2.2 %second_half.1 = (bf16[256,512]{1,0:T(8,128)(2,1)}, bf16[256,512]{1,0:T(8,128)(2,1)}, bf16[256,512]{1,0:T(8,128)(2,1)}, bf16[256,512]{1,0:T(8,128)(2,1)}) custom-call(bf16[256,512]{1,0:T(8,128)(2,1)S(1)} %get-tuple-element.48.k, bf16[256,512]{1,0:T(8,128)(2,1)S(1)} %collective-permute-done.3.second, bf16[256,512]{1,0:T(8,128)(2,1)S(1)} %get-tuple-element.52._.nu, ...), custom_call_target="tpu_custom_call" | custom-call | tf_op jit(solution)/shard_map/second_half/pallas_call | solution.py:598
  (1 shorter events, 0.0 us)
Async XLA Ops:
  0.6 3.5 %copy-start = (bf16[256,512]{1,0:T(8,128)(2,1)S(1)}, bf16[256,512]{1,0:T(8,128)(2,1)}, u32[]{:S(2)}) copy-start(bf16[256,512]{1,0:T(8,128)(2,1)} %u.7) | copy-start | bytes 786436
  2.0 2.2 %collective-permute-start = (bf16[256,512]{1,0:T(8,128)(2,1)S(1)}, bf16[256,512]{1,0:T(8,128)(2,1)S(1)}, u32[]{:S(2)}, u32[]{:S(2)}) collective-permute-start(bf16[256,512]{1,0:T(8,128)(2,1)S(1)} %get-tuple-element.45), channel_id=1, source_target_pairs={{0,1},{1,0},{2,3},{3,2},{4,5},{5,4},{6,7},{7,6},{8,9},{9,8},{10,11... | collective-permute-start | bytes 786440 | tf_op jit(solution)/shard_map/ppermute | solution.py:45
  2.7 5.1 %collective-permute-start.1 = (bf16[128,512]{1,0:T(8,128)(2,1)S(1)}, bf16[128,512]{1,0:T(8,128)(2,1)S(1)}, u32[]{:S(2)}, u32[]{:S(2)}) collective-permute-start(bf16[128,512]{1,0:T(8,128)(2,1)S(1)} %get-tuple-element.46), channel_id=1, source_target_pairs={{0,2},{1,3},{2,1},{3,0},{4,6},{5,7},{6,5},{7,4},{8,10},{9,11},{10,... | collective-permute-start | bytes 393224 | tf_op jit(solution)/shard_map/ppermute | solution.py:45
  2.9 8.6 %collective-permute-start.2 = (bf16[128,512]{1,0:T(8,128)(2,1)S(1)}, bf16[128,512]{1,0:T(8,128)(2,1)S(1)}, u32[]{:S(2)}, u32[]{:S(2)}) collective-permute-start(bf16[128,512]{1,0:T(8,128)(2,1)S(1)} %get-tuple-element.47), channel_id=1, source_target_pairs={{0,3},{1,2},{2,0},{3,1},{4,7},{5,6},{6,4},{7,5},{8,11},{9,10},{10,... | collective-permute-start | bytes 393224 | tf_op jit(solution)/shard_map/ppermute | solution.py:45
  4.2 1.4 %copy-start.1 = (s32[4]{0:T(128)S(1)}, s32[4]{0:T(128)}, u32[]{:S(2)}) copy-start(s32[4]{0:T(128)} %lengths.1) | copy-start | bytes 52
  4.2 8.7 %collective-permute-start.4 = (bf16[256,512]{1,0:T(8,128)(2,1)S(1)}, bf16[256,512]{1,0:T(8,128)(2,1)S(1)}, u32[]{:S(2)}, u32[]{:S(2)}) collective-permute-start(bf16[256,512]{1,0:T(8,128)(2,1)S(1)} %get-tuple-element.50), channel_id=1, source_target_pairs={{0,4},{1,5},{2,6},{3,7},{4,0},{5,1},{6,2},{7,3},{8,12},{9,13},{10,... | collective-permute-start | bytes 786440 | tf_op jit(solution)/shard_map/ppermute | solution.py:60
  5.6 7.3 %collective-permute-start.5 = (bf16[256,512]{1,0:T(8,128)(2,1)S(1)}, bf16[256,512]{1,0:T(8,128)(2,1)S(1)}, u32[]{:S(2)}, u32[]{:S(2)}) collective-permute-start(bf16[256,512]{1,0:T(8,128)(2,1)S(1)} %get-tuple-element.51), channel_id=1, source_target_pairs={{0,1},{1,0},{2,3},{3,2},{4,8},{5,9},{6,10},{7,11},{8,4},{9,5},{10,... | collective-permute-start | bytes 786440 | tf_op jit(solution)/shard_map/ppermute | solution.py:60
  6.3 7.5 %collective-permute-start.6 = (bf16[128,512]{1,0:T(8,128)(2,1)S(1)}, bf16[128,512]{1,0:T(8,128)(2,1)S(1)}, u32[]{:S(2)}, u32[]{:S(2)}) collective-permute-start(bf16[128,512]{1,0:T(8,128)(2,1)S(1)} %get-tuple-element.55), channel_id=1, source_target_pairs={{0,2},{1,3},{2,0},{3,1},{4,6},{5,7},{6,4},{7,5},{8,10},{9,11},{10,... | collective-permute-start | bytes 393224 | tf_op jit(solution)/shard_map/ppermute | solution.py:29
  11.6 8.4 %collective-permute-start.9 = (bf16[256,512]{1,0:T(8,128)(2,1)S(1)}, bf16[256,512]{1,0:T(8,128)(2,1)S(1)}, u32[]{:S(2)}, u32[]{:S(2)}) collective-permute-start(bf16[256,512]{1,0:T(8,128)(2,1)S(1)} %get-tuple-element.72), channel_id=1, source_target_pairs={{0,4},{1,5},{2,6},{3,7},{4,0},{5,1},{6,2},{7,3},{8,12},{9,13},{10,... | collective-permute-start | bytes 786440 | tf_op jit(solution)/shard_map/ppermute | solution.py:60
  12.9 8.1 %collective-permute-start.3 = (bf16[256,512]{1,0:T(8,128)(2,1)S(1)}, bf16[256,512]{1,0:T(8,128)(2,1)S(1)}, u32[]{:S(2)}, u32[]{:S(2)}) collective-permute-start(bf16[256,512]{1,0:T(8,128)(2,1)S(1)} %get-tuple-element.49), channel_id=1, source_target_pairs={{0,1},{1,0},{2,3},{3,2},{4,8},{5,9},{6,10},{7,11},{8,4},{9,5},{10,... | collective-permute-start | bytes 786440 | tf_op jit(solution)/shard_map/ppermute | solution.py:60
  13.0 4.2 %collective-permute-start.8 = (bf16[128,512]{1,0:T(8,128)(2,1)S(1)}, bf16[128,512]{1,0:T(8,128)(2,1)S(1)}, u32[]{:S(2)}, u32[]{:S(2)}) collective-permute-start(bf16[128,512]{1,0:T(8,128)(2,1)S(1)} %get-tuple-element.68), channel_id=1, source_target_pairs={{0,2},{1,3},{2,0},{3,1},{4,6},{5,7},{6,4},{7,5},{8,10},{9,11},{10,... | collective-permute-start | bytes 393224 | tf_op jit(solution)/shard_map/ppermute | solution.py:29
  14.5 5.6 %collective-permute-start.10 = (f32[8,256]{1,0:T(8,128)S(1)}, f32[8,256]{1,0:T(8,128)S(1)}, u32[]{:S(2)}, u32[]{:S(2)}) collective-permute-start(f32[8,256]{1,0:T(8,128)S(1)} %get-tuple-element.56.own_stats.rest_1_), channel_id=1, source_target_pairs={{0,4},{1,5},{2,6},{3,7},{4,0},{5,1},{6,2},{7,3},{8,12},{9,13},{10,... | collective-permute-start | bytes 24584 | tf_op jit(solution)/shard_map/ppermute | solution.py:60
  15.4 5.8 %collective-permute-start.7 = (f32[8,256]{1,0:T(8,128)S(1)}, f32[8,256]{1,0:T(8,128)S(1)}, u32[]{:S(2)}, u32[]{:S(2)}) collective-permute-start(f32[8,256]{1,0:T(8,128)S(1)} %get-tuple-element.56.own_stats.rest_1_), channel_id=1, source_target_pairs={{0,1},{1,0},{2,3},{3,2},{4,8},{5,9},{6,10},{7,11},{8,4},{9,5},{10,... | collective-permute-start | bytes 24584 | tf_op jit(solution)/shard_map/ppermute | solution.py:60

commit v9 on v7

--- a/solution.py
+++ b/solution.py
@@ -65,20 +65,21 @@
     sharers = lax.axis_size("head")
     rows, features = queries.shape
     width = features // sharers
-    heights = [(2 + sharers // 2) * rows if step < 2 else 2 * rows for step in range(sharers)]
+    heights = [(2 + sharers // 2) * rows if step == 1 else 2 * rows for step in range(1, sharers)]
 
     def kernel(q, k, v, *rest):
-        pieces, sems = rest[:sharers], rest[sharers]
+        pieces, sems = rest[: sharers - 1], rest[sharers - 1]
         copies = []
 
         def copy(source, target):
             copies.append(pltpu.make_async_copy(source, target, sems.at[len(copies)]))
 
-        for step in range(sharers):
+        for step in range(1, sharers):
             columns = place(step, width)
-            copy(k.at[:, columns], pieces[step].at[pl.ds(0, rows)])
-            copy(q.at[:, columns], pieces[step].at[pl.ds(rows, rows)])
-            copy(v.at[:, columns], pieces[step % 2].at[pl.ds((2 + step // 2) * rows, rows)])
+            copy(k.at[:, columns], pieces[step - 1].at[pl.ds(0, rows)])
+            copy(q.at[:, columns], pieces[step - 1].at[pl.ds(rows, rows)])
+            if step % 2:
+                copy(v.at[:, columns], pieces[0].at[pl.ds((2 + step // 2) * rows, rows)])
         for c in copies:
             c.start()
         for c in copies:
@@ -88,23 +89,22 @@
         kernel,
         out_shape=[bf16(height, width) for height in heights],
         in_specs=[ANY] * 3,
-        out_specs=[VMEM] * sharers,
+        out_specs=[VMEM] * (sharers - 1),
         scratch_shapes=[pltpu.SemaphoreType.DMA((3 * sharers,))],
-        compiler_params=pltpu.CompilerParams(vmem_limit_bytes=53 * 2**20),
+        compiler_params=pltpu.CompilerParams(vmem_limit_bytes=int(53.25 * 2**20)),
         name="cut_pieces",
     )(queries, key_states, value_states)
 
 
-def stack_far_values(own, got, clip_lengths, rows):
-    pairs = own.shape[0] // rows - 2
-    width = own.shape[1]
+def stack_far_values(own_values, got, clip_lengths, rows):
+    pairs = got.shape[0] // rows - 2
+    width = got.shape[1]
     block_rows = 2 * pairs * rows
 
     def kernel(mine, theirs, lengths, own, past, ahead, *out):
         for pair in range(1, pairs):
-            where = pl.ds((2 + pair) * rows, rows)
-            out[pair - 1][pl.ds(0, rows), :] = mine[where, :]
-            out[pair - 1][pl.ds(rows, rows), :] = theirs[where, :]
+            out[pair - 1][pl.ds(0, rows), :] = mine[:, place(2 * pair, width)]
+            out[pair - 1][pl.ds(rows, rows), :] = theirs[pl.ds((2 + pair) * rows, rows), :]
         block, blocks = lax.axis_index("blk"), lax.axis_size("blk")
         tall, wide = (block_rows, 1), (1, block_rows)
         key_ids, row_ids = clip_ids(lengths, tall, 0, block, blocks), clip_ids(lengths, wide, 1, block, blocks)
@@ -121,20 +121,20 @@
         compiler_params=small_kernel(),
         cost_estimate=weighed(5e9),
         name="stack_far_values",
-    )(own, got, clip_lengths)
+    )(own_values, got, clip_lengths)
     return out[3:], out[:3]
 
 
-def stack_values(own, got, upstream, rows):
-    pairs = own.shape[0] // rows - 2
-    width = own.shape[1]
+def stack_values(own_values, got, upstream, rows):
+    pairs = got.shape[0] // rows - 2
+    width = got.shape[1]
     block_rows = upstream.shape[0]
 
     def kernel(mine, theirs, u, first, second):
         def spread(forward, backward):
             for pair in range(pairs):
                 where = pl.ds((2 + pair) * rows, rows)
-                forward[pl.ds(2 * pair * rows, rows), :] = mine[where, :]
+                forward[pl.ds(2 * pair * rows, rows), :] = mine[:, place(2 * pair, width)]
                 forward[pl.ds((2 * pair + 1) * rows, rows), :] = theirs[where, :]
             backward[...] = u[...]
 
@@ -154,21 +154,23 @@
         compiler_params=small_kernel(),
         cost_estimate=weighed(0),
         name="stack_values",
-    )(own, got, upstream)
-
-
-def join_keys_queries(pieces, rows):
-    sharers = len(pieces)
-    width = pieces[0].shape[1]
+    )(own_values, got, upstream)
+
+
+def join_keys_queries(key_states, own_queries, pieces):
+    sharers = len(pieces) + 1
+    rows, width = key_states.shape[0], pieces[0].shape[1]
     block_rows = rows * sharers
 
-    def kernel(*refs):
-        pieces_in = refs[:sharers]
-        keys, queries, first, second = refs[sharers:]
-        for step in range(sharers):
+    def kernel(k, q, *refs):
+        pieces_in = refs[: sharers - 1]
+        keys, queries, first, second = refs[sharers - 1 :]
+        keys[place(0, rows), :] = k[:, place(0, width)]
+        queries[place(0, rows), :] = q[:, place(0, width)]
+        for step in range(1, sharers):
             where = place(step, rows)
-            keys[where, :] = pieces_in[step][pl.ds(0, rows), :]
-            queries[where, :] = pieces_in[step][pl.ds(rows, rows), :]
+            keys[where, :] = pieces_in[step - 1][pl.ds(0, rows), :]
+            queries[where, :] = pieces_in[step - 1][pl.ds(rows, rows), :]
 
         @pl.when(is_even())
         def _():
@@ -183,12 +185,12 @@
     return pl.pallas_call(
         kernel,
         out_shape=[bf16(block_rows, width)] * 4,
-        in_specs=[VMEM] * sharers,
+        in_specs=[VMEM] * (sharers + 1),
         out_specs=[VMEM] * 4,
         compiler_params=small_kernel(),
         cost_estimate=weighed(0),
         name="join_keys_queries",
-    )(*pieces)
+    )(key_states, own_queries, *pieces)
 
 
 def cut_previous_values(first_got, second_got, pairs):
@@ -253,7 +255,7 @@
     heads = width // HEAD_DIM
 
     def kernel(k, q, u, bias, _, *rest):
-        values_in = [ref.at[pl.ds(2 * rows, rows)] for ref in rest[:2]]
+        values_in = [rest[0].at[:, place(0, width)], rest[1].at[pl.ds(2 * rows, rows)]]
         for ref in rest[2 : 1 + sharers // 2]:
             values_in += [ref.at[pl.ds(0, rows)], ref.at[pl.ds(rows, rows)]]
         values, stats, tops, grown_t, slopes_t = rest[1 + sharers // 2 :]
@@ -598,17 +600,17 @@
     sharers = lax.axis_size("head")
     rows = queries.shape[0]
     pieces = cut_pieces(queries, key_states, value_states)
-    pieces = [pieces[0]] + [partner_exchange(pieces[step], step) for step in range(1, sharers)]
-    first, second = stack_values(pieces[0], pieces[1], upstream, rows)
+    pieces = [partner_exchange(piece, step + 1) for step, piece in enumerate(pieces)]
+    first, second = stack_values(value_states, pieces[0], upstream, rows)
     first_got, second_got = block_exchange(first, 0), block_exchange(second, 1)
-    far_values, (own_bias, past_bias, next_bias) = stack_far_values(pieces[0], pieces[1], clip_lengths, rows)
+    far_values, (own_bias, past_bias, next_bias) = stack_far_values(value_states, pieces[0], clip_lengths, rows)
     far_values = [partner_exchange(stack, 2 * pair + 2) for pair, stack in enumerate(far_values)]
-    keys, query_rows, first, second = join_keys_queries(pieces, rows)
+    keys, query_rows, first, second = join_keys_queries(key_states, queries, pieces)
     previous, next_upstream = cut_previous_values(first_got, second_got, sharers // 2)
     first_got, second_got = block_exchange(first, 0), block_exchange(second, 1)
     previous = [partner_exchange(stack, 2 * pair) if pair else stack for pair, stack in enumerate(previous)]
     values, stats, tops, grown_t, slopes_t = own_scores(
-        keys, query_rows, pieces[:2], far_values, upstream, own_bias, next_upstream
+        keys, query_rows, (value_states, pieces[0]), far_values, upstream, own_bias, next_upstream
     )
     first_stats, second_stats = block_exchange(stats, 0), block_exchange(stats, 1)
     *own, later = own_products(keys, query_rows, upstream, values, grown_t, slopes_t, next_upstream)

time: 23.6 us -> 23.5 us (level)
  transfers between devices with their start and end apart: 11 -> 11, of which waited for: 3 -> 3; matrix products, arithmetic and copies ran while one was open for 0% -> 0% of each run, Pallas kernels for 15% -> 16%
where the time goes in v9:
time: 23.5 us; the launch traced here: 23.1 us
  starting transfers between devices  13.3 us (57%)
  Pallas kernels  5.97 us (25%)
  waiting for transfers between devices  3.08 us (13%)
  between operations  0.76 us (3%)
    ppermute x6, starting transfers between devices, block_exchange(): return lax.ppermute(rows, ('dp', 'blk', 'head'), route)  6.99 us
    ppermute x5, starting transfers between devices, partner_exchange(): return lax.ppermute(rows, 'head', route)  6.26 us
    ppermute x5, waiting for transfers between devices, partner_exchange(): return lax.ppermute(rows, 'head', route)  2.24 us
    pallas_call x1, Pallas kernels, cut_pieces(): pl.pallas_call(kernel, out_shape=[bf16(height, width) for height in heigh...  1.23 us
    pallas_call x1, Pallas kernels, second_half(): pl.pallas_call(kernel, out_shape=[bf16(block_rows, width)] * 4, in_specs=...  1.16 us
    pallas_call x1, Pallas kernels, first_half(): pl.pallas_call(kernel, out_shape=[bf16(block_rows, width)] * 2 + [bf16(he...  0.97 us
    ppermute x6, waiting for transfers between devices, block_exchange(): return lax.ppermute(rows, ('dp', 'blk', 'head'), route)  0.83 us
    pallas_call x1, Pallas kernels, stack_far_values(): pl.pallas_call(kernel, out_shape=[jax.ShapeDtypeStruct((block_rows, block...  0.73 us
  transfers between devices with their start and end apart: 11, of which 3 were waited for; matrix products, arithmetic and copies ran while one was open for 0% of the time, Pallas kernels for 16%

profile of v9, /device:TPU:0, one launch (start us, length us, event | category | flops | bytes accessed | tf_op | source)
XLA Modules:
  0.0 23.1 jit_solution(11350663073037775538)
XLA Ops:
  0.6 0.0 copy-start
  0.6 0.0 copy-start.1
  0.7 1.2 %cut_pieces.1 = (bf16[256,512]{1,0:T(8,128)(2,1)S(1)}, bf16[128,512]{1,0:T(8,128)(2,1)S(1)}, bf16[128,512]{1,0:T(8,128)(2,1)S(1)}) custom-call(bf16[64,2048]{1,0:T(8,128)(2,1)} %q.3, bf16[64,2048]{1,0:T(8,128)(2,1)} %k.3, bf16[64,2048]{1,0:T(8,128)(2,1)} %rest_0_.1), custom_call_target="tpu_custom_call" | custom-call | tf_op jit(solution)/shard_map/cut_pieces/pallas_call | solution.py:88
  1.9 0.5 %collective-permute-start = (bf16[256,512]{1,0:T(8,128)(2,1)S(1)}, bf16[256,512]{1,0:T(8,128)(2,1)S(1)}, u32[]{:S(2)}, u32[]{:S(2)}) collective-permute-start(bf16[256,512]{1,0:T(8,128)(2,1)S(1)} %get-tuple-element.43), channel_id=1, source_target_pairs={{0,1},{1,0},{2,3},{3,2},{4,5},{5,4},{6,7},{7,6},{8,9},{9,8},{10,11... | collective-permute-start | bytes 786440 | tf_op jit(solution)/shard_map/ppermute | solution.py:29
  2.4 2.6 %collective-permute-start.1 = (bf16[128,512]{1,0:T(8,128)(2,1)S(1)}, bf16[128,512]{1,0:T(8,128)(2,1)S(1)}, u32[]{:S(2)}, u32[]{:S(2)}) collective-permute-start(bf16[128,512]{1,0:T(8,128)(2,1)S(1)} %get-tuple-element.44), channel_id=1, source_target_pairs={{0,2},{1,3},{2,0},{3,1},{4,6},{5,7},{6,4},{7,5},{8,10},{9,11},{10,... | collective-permute-start | bytes 393224 | tf_op jit(solution)/shard_map/ppermute | solution.py:29
  5.0 0.1 collective-permute-start.2
  5.0 0.0 collective-permute-done.refs_0_.theirs.rest_1_
  5.0 0.0 copy-done
  5.0 0.0 copy-done.1
  5.1 0.1 stack_values.1
  5.1 0.0 copy-start.4
  5.1 1.9 %collective-permute-start.4 = (bf16[256,512]{1,0:T(8,128)(2,1)S(1)}, bf16[256,512]{1,0:T(8,128)(2,1)S(1)}, u32[]{:S(2)}, u32[]{:S(2)}) collective-permute-start(bf16[256,512]{1,0:T(8,128)(2,1)S(1)} %get-tuple-element.48), channel_id=1, source_target_pairs={{0,4},{1,5},{2,6},{3,7},{4,0},{5,1},{6,2},{7,3},{8,12},{9,13},{10,... | collective-permute-start | bytes 786440 | tf_op jit(solution)/shard_map/ppermute | solution.py:44
  7.0 0.0 copy-start.2
  7.0 0.0 copy-start.3
  7.0 0.1 collective-permute-start.5
  7.1 0.0 copy-done.4
  7.1 0.7 %stack_far_values.1 = (f32[256,256]{1,0:T(8,128)S(1)}, f32[256,256]{1,0:T(8,128)S(1)}, f32[256,256]{1,0:T(8,128)S(1)}, bf16[128,512]{1,0:T(8,128)(2,1)S(1)}) custom-call(bf16[64,2048]{1,0:T(8,128)(2,1)S(1)} %copy-done, bf16[256,512]{1,0:T(8,128)(2,1)S(1)} %collective-permute-done.refs_0_.theirs.rest_1_, s32[4]{0:T(128)S(1)} %copy-done.4), custom_call_target="tpu_custom_call" | custom-call | flops 5000000000 | tf_op jit(solution)/shard_map/stack_far_values/pallas_call | solution.py:115
  7.8 1.6 %collective-permute-start.6 = (bf16[128,512]{1,0:T(8,128)(2,1)S(1)}, bf16[128,512]{1,0:T(8,128)(2,1)S(1)}, u32[]{:S(2)}, u32[]{:S(2)}) collective-permute-start(bf16[128,512]{1,0:T(8,128)(2,1)S(1)} %get-tuple-element.53), channel_id=1, source_target_pairs={{0,2},{1,3},{2,0},{3,1},{4,6},{5,7},{6,4},{7,5},{8,10},{9,11},{10,... | collective-permute-start | bytes 393224 | tf_op jit(solution)/shard_map/ppermute | solution.py:29
  9.4 0.0 collective-permute-done.1.refs_1_
  9.4 2.2 %collective-permute-done.2.refs_2_ = bf16[128,512]{1,0:T(8,128)(2,1)S(1)} collective-permute-done((bf16[128,512]{1,0:T(8,128)(2,1)S(1)}, bf16[128,512]{1,0:T(8,128)(2,1)S(1)}, u32[]{:S(2)}, u32[]{:S(2)}) %collective-permute-start.2) | collective-permute-done | bytes 131104 | tf_op jit(solution)/shard_map/ppermute | solution.py:29
  11.6 0.0 copy-done.2
  11.6 0.0 copy-done.3
  11.6 0.1 join_keys_queries.1
  11.7 1.7 %collective-permute-start.9 = (bf16[256,512]{1,0:T(8,128)(2,1)S(1)}, bf16[256,512]{1,0:T(8,128)(2,1)S(1)}, u32[]{:S(2)}, u32[]{:S(2)}) collective-permute-start(bf16[256,512]{1,0:T(8,128)(2,1)S(1)} %get-tuple-element.70), channel_id=1, source_target_pairs={{0,4},{1,5},{2,6},{3,7},{4,0},{5,1},{6,2},{7,3},{8,12},{9,13},{10,... | collective-permute-start | bytes 786440 | tf_op jit(solution)/shard_map/ppermute | solution.py:44
  13.4 0.6 %collective-permute-start.3 = (bf16[256,512]{1,0:T(8,128)(2,1)S(1)}, bf16[256,512]{1,0:T(8,128)(2,1)S(1)}, u32[]{:S(2)}, u32[]{:S(2)}) collective-permute-start(bf16[256,512]{1,0:T(8,128)(2,1)S(1)} %get-tuple-element.47), channel_id=1, source_target_pairs={{0,1},{1,0},{2,3},{3,2},{4,8},{5,9},{6,10},{7,11},{8,4},{9,5},{10,... | collective-permute-start | bytes 786440 | tf_op jit(solution)/shard_map/ppermute | solution.py:44
  14.0 0.0 collective-permute-done.4.first
  14.0 0.0 collective-permute-done.5.second
  14.1 1.6 %collective-permute-start.8 = (bf16[128,512]{1,0:T(8,128)(2,1)S(1)}, bf16[128,512]{1,0:T(8,128)(2,1)S(1)}, u32[]{:S(2)}, u32[]{:S(2)}) collective-permute-start(bf16[128,512]{1,0:T(8,128)(2,1)S(1)} %get-tuple-element.66), channel_id=1, source_target_pairs={{0,2},{1,3},{2,0},{3,1},{4,6},{5,7},{6,4},{7,5},{8,10},{9,11},{10,... | collective-permute-start | bytes 393224 | tf_op jit(solution)/shard_map/ppermute | solution.py:29
  15.6 0.0 collective-permute-done.6.rest_2_
  15.6 0.7 %own_scores.1 = (bf16[256,512]{1,0:T(8,128)(2,1)S(1)}, f32[8,256]{1,0:T(8,128)S(1)}, f32[4,256]{1,0:T(4,128)S(1)}, bf16[4,256,256]{2,1,0:T(8,128)(2,1)S(1)}, bf16[4,256,256]{2,1,0:T(8,128)(2,1)S(1)}) custom-call(bf16[256,512]{1,0:T(8,128)(2,1)S(1)} %get-tuple-element.46.k, bf16[256,512]{1,0:T(8,128)(2,1)S(1)} %get-tuple-element.51.q.rest_0_, ...), custom_call_target="tpu_custom_call" | custom-call | tf_op jit(solution)/shard_map/own_scores/pallas_call | solution.py:283
  16.3 2.7 %collective-permute-start.10 = (f32[8,256]{1,0:T(8,128)S(1)}, f32[8,256]{1,0:T(8,128)S(1)}, u32[]{:S(2)}, u32[]{:S(2)}) collective-permute-start(f32[8,256]{1,0:T(8,128)S(1)} %get-tuple-element.54.own_stats.rest_1_), channel_id=1, source_target_pairs={{0,4},{1,5},{2,6},{3,7},{4,0},{5,1},{6,2},{7,3},{8,12},{9,13},{10,... | collective-permute-start | bytes 24584 | tf_op jit(solution)/shard_map/ppermute | solution.py:44
  19.1 0.0 collective-permute-start.7
  19.1 0.5 %own_products.1 = (f32[4,256,256]{2,1,0:T(8,128)S(1)}, f32[4,128,256]{2,1,0:T(8,128)S(1)}, f32[4,128,256]{2,1,0:T(8,128)S(1)}, f32[4,128,256]{2,1,0:T(8,128)S(1)}, f32[4,256,256]{2,1,0:T(8,128)S(1)}) custom-call(bf16[256,512]{1,0:T(8,128)(2,1)S(1)} %get-tuple-element.46.k, bf16[256,512]{1,0:T(8,128)(2,1)S(1)} %get-tuple-element.51.q.rest_0_, ...), custom_call_target="tpu_custom_call" | custom-call | flops 1000000000 | tf_op jit(solution)/shard_map/own_products/pallas_call | solution.py:317
  19.6 0.0 collective-permute-done.8.rest_1_
  19.6 0.5 %before_exchanges.1 = (bf16[4,128,256]{2,1,0:T(8,128)(2,1)S(1)}, f32[4,256,256]{2,1,0:T(8,128)S(1)}, bf16[256,512]{1,0:T(8,128)(2,1)S(1)}, bf16[256,512]{1,0:T(8...) custom-call(bf16[256,512]{1,0:T(8,128)(2,1)S(1)} %copy-done.1, ...), custom_call_target="tpu_custom_call" | custom-call | flops 1000000000 | tf_op jit(solution)/shard_map/before_exchanges/pallas_call | solution.py:415
  20.1 0.7 %collective-permute-done.9.first = bf16[256,512]{1,0:T(8,128)(2,1)S(1)} collective-permute-done((bf16[256,512]{1,0:T(8,128)(2,1)S(1)}, bf16[256,512]{1,0:T(8,128)(2,1)S(1)}, u32[]{:S(2)}, u32[]{:S(2)}) %collective-permute-start.9) | collective-permute-done | bytes 262176 | tf_op jit(solution)/shard_map/ppermute | solution.py:44
  20.8 0.1 collective-permute-done.10.stats
  20.9 1.0 %first_half.1 = (bf16[256,512]{1,0:T(8,128)(2,1)S(1)}, bf16[256,512]{1,0:T(8,128)(2,1)S(1)}, bf16[4,128,256]{2,1,0:T(8,128)(2,1)S(1)}, bf16[4,128,256]{2,1,0:T(8...) custom-call(bf16[256,512]{1,0:T(8,128)(2,1)S(1)} %get-tuple-element.46.k, ...), custom_call_target="tpu_custom_call" | custom-call | tf_op jit(solution)/shard_map/first_half/pallas_call | solution.py:489
  21.9 0.0 collective-permute-done.3.second
  21.9 0.0 collective-permute-done.7.stats
  21.9 1.2 %second_half.1 = (bf16[256,512]{1,0:T(8,128)(2,1)}, bf16[256,512]{1,0:T(8,128)(2,1)}, bf16[256,512]{1,0:T(8,128)(2,1)}, bf16[256,512]{1,0:T(8,128)(2,1)}) custom-call(bf16[256,512]{1,0:T(8,128)(2,1)S(1)} %get-tuple-element.46.k, bf16[256,512]{1,0:T(8,128)(2,1)S(1)} %collective-permute-done.3.second, bf16[256,512]{1,0:T(8,128)(2,1)S(1)} %get-tuple-element.50._.nu, ...), custom_call_target="tpu_custom_call" | custom-call | tf_op jit(solution)/shard_map/second_half/pallas_call | solution.py:584
  (1 shorter events, 0.0 us)
Async XLA Ops:
  0.6 4.4 %copy-start = (bf16[64,2048]{1,0:T(8,128)(2,1)S(1)}, bf16[64,2048]{1,0:T(8,128)(2,1)}, u32[]{:S(2)}) copy-start(bf16[64,2048]{1,0:T(8,128)(2,1)} %rest_0_.1) | copy-start | bytes 786436
  0.6 4.4 %copy-start.1 = (bf16[256,512]{1,0:T(8,128)(2,1)S(1)}, bf16[256,512]{1,0:T(8,128)(2,1)}, u32[]{:S(2)}) copy-start(bf16[256,512]{1,0:T(8,128)(2,1)} %u.7) | copy-start | bytes 786436
  1.9 3.2 %collective-permute-start = (bf16[256,512]{1,0:T(8,128)(2,1)S(1)}, bf16[256,512]{1,0:T(8,128)(2,1)S(1)}, u32[]{:S(2)}, u32[]{:S(2)}) collective-permute-start(bf16[256,512]{1,0:T(8,128)(2,1)S(1)} %get-tuple-element.43), channel_id=1, source_target_pairs={{0,1},{1,0},{2,3},{3,2},{4,5},{5,4},{6,7},{7,6},{8,9},{9,8},{10,11... | collective-permute-start | bytes 786440 | tf_op jit(solution)/shard_map/ppermute | solution.py:29
  2.4 7.0 %collective-permute-start.1 = (bf16[128,512]{1,0:T(8,128)(2,1)S(1)}, bf16[128,512]{1,0:T(8,128)(2,1)S(1)}, u32[]{:S(2)}, u32[]{:S(2)}) collective-permute-start(bf16[128,512]{1,0:T(8,128)(2,1)S(1)} %get-tuple-element.44), channel_id=1, source_target_pairs={{0,2},{1,3},{2,0},{3,1},{4,6},{5,7},{6,4},{7,5},{8,10},{9,11},{10,... | collective-permute-start | bytes 393224 | tf_op jit(solution)/shard_map/ppermute | solution.py:29
  5.0 6.6 %collective-permute-start.2 = (bf16[128,512]{1,0:T(8,128)(2,1)S(1)}, bf16[128,512]{1,0:T(8,128)(2,1)S(1)}, u32[]{:S(2)}, u32[]{:S(2)}) collective-permute-start(bf16[128,512]{1,0:T(8,128)(2,1)S(1)} %get-tuple-element.45), channel_id=1, source_target_pairs={{0,3},{1,2},{2,1},{3,0},{4,7},{5,6},{6,5},{7,4},{8,11},{9,10},{10,... | collective-permute-start | bytes 393224 | tf_op jit(solution)/shard_map/ppermute | solution.py:29
  5.1 2.0 %copy-start.4 = (s32[4]{0:T(128)S(1)}, s32[4]{0:T(128)}, u32[]{:S(2)}) copy-start(s32[4]{0:T(128)} %lengths.1) | copy-start | bytes 52
  5.1 8.9 %collective-permute-start.4 = (bf16[256,512]{1,0:T(8,128)(2,1)S(1)}, bf16[256,512]{1,0:T(8,128)(2,1)S(1)}, u32[]{:S(2)}, u32[]{:S(2)}) collective-permute-start(bf16[256,512]{1,0:T(8,128)(2,1)S(1)} %get-tuple-element.48), channel_id=1, source_target_pairs={{0,4},{1,5},{2,6},{3,7},{4,0},{5,1},{6,2},{7,3},{8,12},{9,13},{10,... | collective-permute-start | bytes 786440 | tf_op jit(solution)/shard_map/ppermute | solution.py:44
  7.0 4.6 %copy-start.2 = (bf16[64,2048]{1,0:T(8,128)(2,1)S(1)}, bf16[64,2048]{1,0:T(8,128)(2,1)}, u32[]{:S(2)}) copy-start(bf16[64,2048]{1,0:T(8,128)(2,1)} %k.3) | copy-start | bytes 786436
  7.0 4.6 %copy-start.3 = (bf16[64,2048]{1,0:T(8,128)(2,1)S(1)}, bf16[64,2048]{1,0:T(8,128)(2,1)}, u32[]{:S(2)}) copy-start(bf16[64,2048]{1,0:T(8,128)(2,1)} %q.3) | copy-start | bytes 786436
  7.0 7.0 %collective-permute-start.5 = (bf16[256,512]{1,0:T(8,128)(2,1)S(1)}, bf16[256,512]{1,0:T(8,128)(2,1)S(1)}, u32[]{:S(2)}, u32[]{:S(2)}) collective-permute-start(bf16[256,512]{1,0:T(8,128)(2,1)S(1)} %get-tuple-element.49), channel_id=1, source_target_pairs={{0,1},{1,0},{2,3},{3,2},{4,8},{5,9},{6,10},{7,11},{8,4},{9,5},{10,... | collective-permute-start | bytes 786440 | tf_op jit(solution)/shard_map/ppermute | solution.py:44
  7.8 7.8 %collective-permute-start.6 = (bf16[128,512]{1,0:T(8,128)(2,1)S(1)}, bf16[128,512]{1,0:T(8,128)(2,1)S(1)}, u32[]{:S(2)}, u32[]{:S(2)}) collective-permute-start(bf16[128,512]{1,0:T(8,128)(2,1)S(1)} %get-tuple-element.53), channel_id=1, source_target_pairs={{0,2},{1,3},{2,0},{3,1},{4,6},{5,7},{6,4},{7,5},{8,10},{9,11},{10,... | collective-permute-start | bytes 393224 | tf_op jit(solution)/shard_map/ppermute | solution.py:29
  11.7 9.1 %collective-permute-start.9 = (bf16[256,512]{1,0:T(8,128)(2,1)S(1)}, bf16[256,512]{1,0:T(8,128)(2,1)S(1)}, u32[]{:S(2)}, u32[]{:S(2)}) collective-permute-start(bf16[256,512]{1,0:T(8,128)(2,1)S(1)} %get-tuple-element.70), channel_id=1, source_target_pairs={{0,4},{1,5},{2,6},{3,7},{4,0},{5,1},{6,2},{7,3},{8,12},{9,13},{10,... | collective-permute-start | bytes 786440 | tf_op jit(solution)/shard_map/ppermute | solution.py:44
  13.4 8.5 %collective-permute-start.3 = (bf16[256,512]{1,0:T(8,128)(2,1)S(1)}, bf16[256,512]{1,0:T(8,128)(2,1)S(1)}, u32[]{:S(2)}, u32[]{:S(2)}) collective-permute-start(bf16[256,512]{1,0:T(8,128)(2,1)S(1)} %get-tuple-element.47), channel_id=1, source_target_pairs={{0,1},{1,0},{2,3},{3,2},{4,8},{5,9},{6,10},{7,11},{8,4},{9,5},{10,... | collective-permute-start | bytes 786440 | tf_op jit(solution)/shard_map/ppermute | solution.py:44
  14.1 5.5 %collective-permute-start.8 = (bf16[128,512]{1,0:T(8,128)(2,1)S(1)}, bf16[128,512]{1,0:T(8,128)(2,1)S(1)}, u32[]{:S(2)}, u32[]{:S(2)}) collective-permute-start(bf16[128,512]{1,0:T(8,128)(2,1)S(1)} %get-tuple-element.66), channel_id=1, source_target_pairs={{0,2},{1,3},{2,0},{3,1},{4,6},{5,7},{6,4},{7,5},{8,10},{9,11},{10,... | collective-permute-start | bytes 393224 | tf_op jit(solution)/shard_map/ppermute | solution.py:29
  16.3 4.6 %collective-permute-start.10 = (f32[8,256]{1,0:T(8,128)S(1)}, f32[8,256]{1,0:T(8,128)S(1)}, u32[]{:S(2)}, u32[]{:S(2)}) collective-permute-start(f32[8,256]{1,0:T(8,128)S(1)} %get-tuple-element.54.own_stats.rest_1_), channel_id=1, source_target_pairs={{0,4},{1,5},{2,6},{3,7},{4,0},{5,1},{6,2},{7,3},{8,12},{9,13},{10,... | collective-permute-start | bytes 24584 | tf_op jit(solution)/shard_map/ppermute | solution.py:44
  19.1 2.9 %collective-permute-start.7 = (f32[8,256]{1,0:T(8,128)S(1)}, f32[8,256]{1,0:T(8,128)S(1)}, u32[]{:S(2)}, u32[]{:S(2)}) collective-permute-start(f32[8,256]{1,0:T(8,128)S(1)} %get-tuple-element.54.own_stats.rest_1_), channel_id=1, source_target_pairs={{0,1},{1,0},{2,3},{3,2},{4,8},{5,9},{6,10},{7,11},{8,4},{9,5},{10,... | collective-permute-start | bytes 24584 | tf_op jit(solution)/shard_map/ppermute | solution.py:44

commit v10 on v9

--- a/solution.py
+++ b/solution.py
@@ -26,6 +26,22 @@
 
 def partner_exchange(rows, step):
     route = [(i, i ^ step) for i in range(lax.axis_size("head"))]
+    return lax.ppermute(rows, "head", route)
+
+
+def sent_step(step, sharer):
+    if step < 2:
+        return step
+    above = sharer // (1 << (step.bit_length() - 1)) % 2
+    return step - step % 2 + (above if step % 2 == 0 else 1 - above)
+
+
+def got_step(step, sharer):
+    return step if step < 2 else sent_step(step ^ 1, sharer)
+
+
+def pieces_exchange(rows, step):
+    route = [(i, i ^ sent_step(step, i)) for i in range(lax.axis_size("head"))]
     return lax.ppermute(rows, "head", route)
 
 
@@ -75,11 +91,11 @@
             copies.append(pltpu.make_async_copy(source, target, sems.at[len(copies)]))
 
         for step in range(1, sharers):
-            columns = place(step, width)
+            columns = place(sent_step(step, lax.axis_index("head")), width)
             copy(k.at[:, columns], pieces[step - 1].at[pl.ds(0, rows)])
             copy(q.at[:, columns], pieces[step - 1].at[pl.ds(rows, rows)])
             if step % 2:
-                copy(v.at[:, columns], pieces[0].at[pl.ds((2 + step // 2) * rows, rows)])
+                copy(v.at[:, place(step, width)], pieces[0].at[pl.ds((2 + step // 2) * rows, rows)])
         for c in copies:
             c.start()
         for c in copies:
@@ -168,7 +184,7 @@
         keys[place(0, rows), :] = k[:, place(0, width)]
         queries[place(0, rows), :] = q[:, place(0, width)]
         for step in range(1, sharers):
-            where = place(step, rows)
+            where = place(got_step(step, lax.axis_index("head")), rows)
             keys[where, :] = pieces_in[step - 1][pl.ds(0, rows), :]
             queries[where, :] = pieces_in[step - 1][pl.ds(rows, rows), :]
 
@@ -600,7 +616,7 @@
     sharers = lax.axis_size("head")
     rows = queries.shape[0]
     pieces = cut_pieces(queries, key_states, value_states)
-    pieces = [partner_exchange(piece, step + 1) for step, piece in enumerate(pieces)]
+    pieces = [pieces_exchange(piece, step + 1) for step, piece in enumerate(pieces)]
     first, second = stack_values(value_states, pieces[0], upstream, rows)
     first_got, second_got = block_exchange(first, 0), block_exchange(second, 1)
     far_values, (own_bias, past_bias, next_bias) = stack_far_values(value_states, pieces[0], clip_lengths, rows)

time: 23.5 us -> 23.5 us (level)
  the two profiles are of different devices: /device:TPU:0 before, /device:TPU:19 now
where the time goes in v10:
time: 23.5 us; the launch traced here: 23.4 us
  waiting for transfers between devices  8.45 us (36%)
  starting transfers between devices  7.27 us (31%)
  Pallas kernels  6.89 us (29%)
  between operations  0.75 us (3%)
    ppermute x3, waiting for transfers between devices, pieces_exchange(): return lax.ppermute(rows, 'head', route)  4.51 us
    ppermute x6, starting transfers between devices, block_exchange(): return lax.ppermute(rows, ('dp', 'blk', 'head'), route)  3.66 us
    ppermute x6, waiting for transfers between devices, block_exchange(): return lax.ppermute(rows, ('dp', 'blk', 'head'), route)  2.72 us
    pallas_call x1, Pallas kernels, second_half(): pl.pallas_call(kernel, out_shape=[bf16(block_rows, width)] * 4, in_specs=...  2.24 us
    ppermute x3, starting transfers between devices, pieces_exchange(): return lax.ppermute(rows, 'head', route)  2.21 us
    ppermute x2, starting transfers between devices, partner_exchange(): return lax.ppermute(rows, 'head', route)  1.4 us
    pallas_call x1, Pallas kernels, cut_pieces(): pl.pallas_call(kernel, out_shape=[bf16(height, width) for height in heigh...  1.23 us
    ppermute x2, waiting for transfers between devices, partner_exchange(): return lax.ppermute(rows, 'head', route)  1.21 us
  transfers between devices with their start and end apart: 11, of which 6 were waited for; matrix products, arithmetic and copies ran while one was open for 0% of the time, Pallas kernels for 15%

profile of v10, /device:TPU:19, one launch (start us, length us, event | category | flops | bytes accessed | tf_op | source)
XLA Modules:
  0.0 23.4 jit_solution(4633744283167480341)
XLA Ops:
  0.6 0.0 copy-start
  0.6 0.0 copy-start.1
  0.7 1.2 %cut_pieces.1 = (bf16[256,512]{1,0:T(8,128)(2,1)S(1)}, bf16[128,512]{1,0:T(8,128)(2,1)S(1)}, bf16[128,512]{1,0:T(8,128)(2,1)S(1)}) custom-call(bf16[64,2048]{1,0:T(8,128)(2,1)} %q.3, bf16[64,2048]{1,0:T(8,128)(2,1)} %k.3, bf16[64,2048]{1,0:T(8,128)(2,1)} %rest_0_.1), custom_call_target="tpu_custom_call" | custom-call | tf_op jit(solution)/shard_map/cut_pieces/pallas_call | solution.py:104
  1.9 0.7 %collective-permute-start = (bf16[256,512]{1,0:T(8,128)(2,1)S(1)}, bf16[256,512]{1,0:T(8,128)(2,1)S(1)}, u32[]{:S(2)}, u32[]{:S(2)}) collective-permute-start(bf16[256,512]{1,0:T(8,128)(2,1)S(1)} %get-tuple-element.43), channel_id=1, source_target_pairs={{0,1},{1,0},{2,3},{3,2},{4,5},{5,4},{6,7},{7,6},{8,9},{9,8},{10,11... | collective-permute-start | bytes 786440 | tf_op jit(solution)/shard_map/ppermute | solution.py:45
  2.6 0.2 collective-permute-start.1
  2.8 1.3 %collective-permute-start.2 = (bf16[128,512]{1,0:T(8,128)(2,1)S(1)}, bf16[128,512]{1,0:T(8,128)(2,1)S(1)}, u32[]{:S(2)}, u32[]{:S(2)}) collective-permute-start(bf16[128,512]{1,0:T(8,128)(2,1)S(1)} %get-tuple-element.45), channel_id=1, source_target_pairs={{0,3},{1,2},{2,0},{3,1},{4,7},{5,6},{6,4},{7,5},{8,11},{9,10},{10,... | collective-permute-start | bytes 393224 | tf_op jit(solution)/shard_map/ppermute | solution.py:45
  4.1 0.0 collective-permute-done.refs_0_.theirs.rest_1_
  4.1 0.0 copy-done
  4.1 0.0 copy-done.1
  4.1 0.1 stack_values.1
  4.2 0.0 copy-start.4
  4.2 1.4 %collective-permute-start.4 = (bf16[256,512]{1,0:T(8,128)(2,1)S(1)}, bf16[256,512]{1,0:T(8,128)(2,1)S(1)}, u32[]{:S(2)}, u32[]{:S(2)}) collective-permute-start(bf16[256,512]{1,0:T(8,128)(2,1)S(1)} %get-tuple-element.48), channel_id=1, source_target_pairs={{0,4},{1,5},{2,6},{3,7},{4,0},{5,1},{6,2},{7,3},{8,12},{9,13},{10,... | collective-permute-start | bytes 786440 | tf_op jit(solution)/shard_map/ppermute | solution.py:60
  5.5 0.0 copy-start.2
  5.5 0.0 copy-start.3
  5.6 0.0 collective-permute-start.5
  5.6 0.0 copy-done.4
  5.6 0.7 %stack_far_values.1 = (f32[256,256]{1,0:T(8,128)S(1)}, f32[256,256]{1,0:T(8,128)S(1)}, f32[256,256]{1,0:T(8,128)S(1)}, bf16[128,512]{1,0:T(8,128)(2,1)S(1)}) custom-call(bf16[64,2048]{1,0:T(8,128)(2,1)S(1)} %copy-done, bf16[256,512]{1,0:T(8,128)(2,1)S(1)} %collective-permute-done.refs_0_.theirs.rest_1_, s32[4]{0:T(128)S(1)} %copy-done.4), custom_call_target="tpu_custom_call" | custom-call | flops 5000000000 | tf_op jit(solution)/shard_map/stack_far_values/pallas_call | solution.py:131
  6.3 0.6 %collective-permute-start.6 = (bf16[128,512]{1,0:T(8,128)(2,1)S(1)}, bf16[128,512]{1,0:T(8,128)(2,1)S(1)}, u32[]{:S(2)}, u32[]{:S(2)}) collective-permute-start(bf16[128,512]{1,0:T(8,128)(2,1)S(1)} %get-tuple-element.53), channel_id=1, source_target_pairs={{0,2},{1,3},{2,0},{3,1},{4,6},{5,7},{6,4},{7,5},{8,10},{9,11},{10,... | collective-permute-start | bytes 393224 | tf_op jit(solution)/shard_map/ppermute | solution.py:29
  6.9 0.8 %collective-permute-done.1.refs_1_ = bf16[128,512]{1,0:T(8,128)(2,1)S(1)} collective-permute-done((bf16[128,512]{1,0:T(8,128)(2,1)S(1)}, bf16[128,512]{1,0:T(8,128)(2,1)S(1)}, u32[]{:S(2)}, u32[]{:S(2)}) %collective-permute-start.1) | collective-permute-done | bytes 131104 | tf_op jit(solution)/shard_map/ppermute | solution.py:45
  7.7 3.7 %collective-permute-done.2.refs_2_ = bf16[128,512]{1,0:T(8,128)(2,1)S(1)} collective-permute-done((bf16[128,512]{1,0:T(8,128)(2,1)S(1)}, bf16[128,512]{1,0:T(8,128)(2,1)S(1)}, u32[]{:S(2)}, u32[]{:S(2)}) %collective-permute-start.2) | collective-permute-done | bytes 131104 | tf_op jit(solution)/shard_map/ppermute | solution.py:45
  11.4 0.0 copy-done.2
  11.4 0.0 copy-done.3
  11.4 0.1 join_keys_queries.1
  11.5 1.4 %collective-permute-start.9 = (bf16[256,512]{1,0:T(8,128)(2,1)S(1)}, bf16[256,512]{1,0:T(8,128)(2,1)S(1)}, u32[]{:S(2)}, u32[]{:S(2)}) collective-permute-start(bf16[256,512]{1,0:T(8,128)(2,1)S(1)} %get-tuple-element.70), channel_id=1, source_target_pairs={{0,4},{1,5},{2,6},{3,7},{4,0},{5,1},{6,2},{7,3},{8,12},{9,13},{10,... | collective-permute-start | bytes 786440 | tf_op jit(solution)/shard_map/ppermute | solution.py:60
  12.9 0.0 collective-permute-start.3
  12.9 0.0 collective-permute-done.4.first
  12.9 0.0 collective-permute-done.5.second
  12.9 0.1 cut_previous_values.1
  12.9 0.8 %collective-permute-start.8 = (bf16[128,512]{1,0:T(8,128)(2,1)S(1)}, bf16[128,512]{1,0:T(8,128)(2,1)S(1)}, u32[]{:S(2)}, u32[]{:S(2)}) collective-permute-start(bf16[128,512]{1,0:T(8,128)(2,1)S(1)} %get-tuple-element.66), channel_id=1, source_target_pairs={{0,2},{1,3},{2,0},{3,1},{4,6},{5,7},{6,4},{7,5},{8,10},{9,11},{10,... | collective-permute-start | bytes 393224 | tf_op jit(solution)/shard_map/ppermute | solution.py:29
  13.7 0.0 collective-permute-done.6.rest_2_
  13.7 0.7 %own_scores.1 = (bf16[256,512]{1,0:T(8,128)(2,1)S(1)}, f32[8,256]{1,0:T(8,128)S(1)}, f32[4,256]{1,0:T(4,128)S(1)}, bf16[4,256,256]{2,1,0:T(8,128)(2,1)S(1)}, bf16[4,256,256]{2,1,0:T(8,128)(2,1)S(1)}) custom-call(bf16[256,512]{1,0:T(8,128)(2,1)S(1)} %get-tuple-element.46.k, bf16[256,512]{1,0:T(8,128)(2,1)S(1)} %get-tuple-element.51.q.rest_0_, ...), custom_call_target="tpu_custom_call" | custom-call | tf_op jit(solution)/shard_map/own_scores/pallas_call | solution.py:299
  14.4 0.9 %collective-permute-start.10 = (f32[8,256]{1,0:T(8,128)S(1)}, f32[8,256]{1,0:T(8,128)S(1)}, u32[]{:S(2)}, u32[]{:S(2)}) collective-permute-start(f32[8,256]{1,0:T(8,128)S(1)} %get-tuple-element.54.own_stats.rest_1_), channel_id=1, source_target_pairs={{0,4},{1,5},{2,6},{3,7},{4,0},{5,1},{6,2},{7,3},{8,12},{9,13},{10,... | collective-permute-start | bytes 24584 | tf_op jit(solution)/shard_map/ppermute | solution.py:60
  15.4 0.0 collective-permute-start.7
  15.4 0.5 %own_products.1 = (f32[4,256,256]{2,1,0:T(8,128)S(1)}, f32[4,128,256]{2,1,0:T(8,128)S(1)}, f32[4,128,256]{2,1,0:T(8,128)S(1)}, f32[4,128,256]{2,1,0:T(8,128)S(1)}, f32[4,256,256]{2,1,0:T(8,128)S(1)}) custom-call(bf16[256,512]{1,0:T(8,128)(2,1)S(1)} %get-tuple-element.46.k, bf16[256,512]{1,0:T(8,128)(2,1)S(1)} %get-tuple-element.51.q.rest_0_, ...), custom_call_target="tpu_custom_call" | custom-call | flops 1000000000 | tf_op jit(solution)/shard_map/own_products/pallas_call | solution.py:333
  15.9 1.2 %collective-permute-done.8.rest_1_ = bf16[128,512]{1,0:T(8,128)(2,1)S(1)} collective-permute-done((bf16[128,512]{1,0:T(8,128)(2,1)S(1)}, bf16[128,512]{1,0:T(8,128)(2,1)S(1)}, u32[]{:S(2)}, u32[]{:S(2)}) %collective-permute-start.8) | collective-permute-done | bytes 131104 | tf_op jit(solution)/shard_map/ppermute | solution.py:29
  17.1 0.3 %before_exchanges.1 = (bf16[4,128,256]{2,1,0:T(8,128)(2,1)S(1)}, f32[4,256,256]{2,1,0:T(8,128)S(1)}, bf16[256,512]{1,0:T(8,128)(2,1)S(1)}, bf16[256,512]{1,0:T(8...) custom-call(bf16[256,512]{1,0:T(8,128)(2,1)S(1)} %copy-done.1, ...), custom_call_target="tpu_custom_call" | custom-call | flops 1000000000 | tf_op jit(solution)/shard_map/before_exchanges/pallas_call | solution.py:431
  17.4 2.5 %collective-permute-done.9.first = bf16[256,512]{1,0:T(8,128)(2,1)S(1)} collective-permute-done((bf16[256,512]{1,0:T(8,128)(2,1)S(1)}, bf16[256,512]{1,0:T(8,128)(2,1)S(1)}, u32[]{:S(2)}, u32[]{:S(2)}) %collective-permute-start.9) | collective-permute-done | bytes 262176 | tf_op jit(solution)/shard_map/ppermute | solution.py:60
  19.9 0.1 collective-permute-done.10.stats
  20.0 1.0 %first_half.1 = (bf16[256,512]{1,0:T(8,128)(2,1)S(1)}, bf16[256,512]{1,0:T(8,128)(2,1)S(1)}, bf16[4,128,256]{2,1,0:T(8,128)(2,1)S(1)}, bf16[4,128,256]{2,1,0:T(8...) custom-call(bf16[256,512]{1,0:T(8,128)(2,1)S(1)} %get-tuple-element.46.k, ...), custom_call_target="tpu_custom_call" | custom-call | tf_op jit(solution)/shard_map/first_half/pallas_call | solution.py:505
  21.0 0.0 collective-permute-done.3.second
  21.0 0.1 collective-permute-done.7.stats
  21.1 2.2 %second_half.1 = (bf16[256,512]{1,0:T(8,128)(2,1)}, bf16[256,512]{1,0:T(8,128)(2,1)}, bf16[256,512]{1,0:T(8,128)(2,1)}, bf16[256,512]{1,0:T(8,128)(2,1)}) custom-call(bf16[256,512]{1,0:T(8,128)(2,1)S(1)} %get-tuple-element.46.k, bf16[256,512]{1,0:T(8,128)(2,1)S(1)} %collective-permute-done.3.second, bf16[256,512]{1,0:T(8,128)(2,1)S(1)} %get-tuple-element.50._.nu, ...), custom_call_target="tpu_custom_call" | custom-call | tf_op jit(solution)/shard_map/second_half/pallas_call | solution.py:600
Async XLA Ops:
  0.6 3.5 %copy-start = (bf16[64,2048]{1,0:T(8,128)(2,1)S(1)}, bf16[64,2048]{1,0:T(8,128)(2,1)}, u32[]{:S(2)}) copy-start(bf16[64,2048]{1,0:T(8,128)(2,1)} %rest_0_.1) | copy-start | bytes 786436
  0.6 3.5 %copy-start.1 = (bf16[256,512]{1,0:T(8,128)(2,1)S(1)}, bf16[256,512]{1,0:T(8,128)(2,1)}, u32[]{:S(2)}) copy-start(bf16[256,512]{1,0:T(8,128)(2,1)} %u.7) | copy-start | bytes 786436
  1.9 2.2 %collective-permute-start = (bf16[256,512]{1,0:T(8,128)(2,1)S(1)}, bf16[256,512]{1,0:T(8,128)(2,1)S(1)}, u32[]{:S(2)}, u32[]{:S(2)}) collective-permute-start(bf16[256,512]{1,0:T(8,128)(2,1)S(1)} %get-tuple-element.43), channel_id=1, source_target_pairs={{0,1},{1,0},{2,3},{3,2},{4,5},{5,4},{6,7},{7,6},{8,9},{9,8},{10,11... | collective-permute-start | bytes 786440 | tf_op jit(solution)/shard_map/ppermute | solution.py:45
  2.6 5.1 %collective-permute-start.1 = (bf16[128,512]{1,0:T(8,128)(2,1)S(1)}, bf16[128,512]{1,0:T(8,128)(2,1)S(1)}, u32[]{:S(2)}, u32[]{:S(2)}) collective-permute-start(bf16[128,512]{1,0:T(8,128)(2,1)S(1)} %get-tuple-element.44), channel_id=1, source_target_pairs={{0,2},{1,3},{2,1},{3,0},{4,6},{5,7},{6,5},{7,4},{8,10},{9,11},{10,... | collective-permute-start | bytes 393224 | tf_op jit(solution)/shard_map/ppermute | solution.py:45
  2.8 8.6 %collective-permute-start.2 = (bf16[128,512]{1,0:T(8,128)(2,1)S(1)}, bf16[128,512]{1,0:T(8,128)(2,1)S(1)}, u32[]{:S(2)}, u32[]{:S(2)}) collective-permute-start(bf16[128,512]{1,0:T(8,128)(2,1)S(1)} %get-tuple-element.45), channel_id=1, source_target_pairs={{0,3},{1,2},{2,0},{3,1},{4,7},{5,6},{6,4},{7,5},{8,11},{9,10},{10,... | collective-permute-start | bytes 393224 | tf_op jit(solution)/shard_map/ppermute | solution.py:45
  4.2 1.4 %copy-start.4 = (s32[4]{0:T(128)S(1)}, s32[4]{0:T(128)}, u32[]{:S(2)}) copy-start(s32[4]{0:T(128)} %lengths.1) | copy-start | bytes 52
  4.2 8.7 %collective-permute-start.4 = (bf16[256,512]{1,0:T(8,128)(2,1)S(1)}, bf16[256,512]{1,0:T(8,128)(2,1)S(1)}, u32[]{:S(2)}, u32[]{:S(2)}) collective-permute-start(bf16[256,512]{1,0:T(8,128)(2,1)S(1)} %get-tuple-element.48), channel_id=1, source_target_pairs={{0,4},{1,5},{2,6},{3,7},{4,0},{5,1},{6,2},{7,3},{8,12},{9,13},{10,... | collective-permute-start | bytes 786440 | tf_op jit(solution)/shard_map/ppermute | solution.py:60
  5.5 5.9 %copy-start.2 = (bf16[64,2048]{1,0:T(8,128)(2,1)S(1)}, bf16[64,2048]{1,0:T(8,128)(2,1)}, u32[]{:S(2)}) copy-start(bf16[64,2048]{1,0:T(8,128)(2,1)} %k.3) | copy-start | bytes 786436
  5.5 5.9 %copy-start.3 = (bf16[64,2048]{1,0:T(8,128)(2,1)S(1)}, bf16[64,2048]{1,0:T(8,128)(2,1)}, u32[]{:S(2)}) copy-start(bf16[64,2048]{1,0:T(8,128)(2,1)} %q.3) | copy-start | bytes 786436
  5.6 7.3 %collective-permute-start.5 = (bf16[256,512]{1,0:T(8,128)(2,1)S(1)}, bf16[256,512]{1,0:T(8,128)(2,1)S(1)}, u32[]{:S(2)}, u32[]{:S(2)}) collective-permute-start(bf16[256,512]{1,0:T(8,128)(2,1)S(1)} %get-tuple-element.49), channel_id=1, source_target_pairs={{0,1},{1,0},{2,3},{3,2},{4,8},{5,9},{6,10},{7,11},{8,4},{9,5},{10,... | collective-permute-start | bytes 786440 | tf_op jit(solution)/shard_map/ppermute | solution.py:60
  6.3 7.4 %collective-permute-start.6 = (bf16[128,512]{1,0:T(8,128)(2,1)S(1)}, bf16[128,512]{1,0:T(8,128)(2,1)S(1)}, u32[]{:S(2)}, u32[]{:S(2)}) collective-permute-start(bf16[128,512]{1,0:T(8,128)(2,1)S(1)} %get-tuple-element.53), channel_id=1, source_target_pairs={{0,2},{1,3},{2,0},{3,1},{4,6},{5,7},{6,4},{7,5},{8,10},{9,11},{10,... | collective-permute-start | bytes 393224 | tf_op jit(solution)/shard_map/ppermute | solution.py:29
  11.5 8.4 %collective-permute-start.9 = (bf16[256,512]{1,0:T(8,128)(2,1)S(1)}, bf16[256,512]{1,0:T(8,128)(2,1)S(1)}, u32[]{:S(2)}, u32[]{:S(2)}) collective-permute-start(bf16[256,512]{1,0:T(8,128)(2,1)S(1)} %get-tuple-element.70), channel_id=1, source_target_pairs={{0,4},{1,5},{2,6},{3,7},{4,0},{5,1},{6,2},{7,3},{8,12},{9,13},{10,... | collective-permute-start | bytes 786440 | tf_op jit(solution)/shard_map/ppermute | solution.py:60
  12.9 8.1 %collective-permute-start.3 = (bf16[256,512]{1,0:T(8,128)(2,1)S(1)}, bf16[256,512]{1,0:T(8,128)(2,1)S(1)}, u32[]{:S(2)}, u32[]{:S(2)}) collective-permute-start(bf16[256,512]{1,0:T(8,128)(2,1)S(1)} %get-tuple-element.47), channel_id=1, source_target_pairs={{0,1},{1,0},{2,3},{3,2},{4,8},{5,9},{6,10},{7,11},{8,4},{9,5},{10,... | collective-permute-start | bytes 786440 | tf_op jit(solution)/shard_map/ppermute | solution.py:60
  12.9 4.2 %collective-permute-start.8 = (bf16[128,512]{1,0:T(8,128)(2,1)S(1)}, bf16[128,512]{1,0:T(8,128)(2,1)S(1)}, u32[]{:S(2)}, u32[]{:S(2)}) collective-permute-start(bf16[128,512]{1,0:T(8,128)(2,1)S(1)} %get-tuple-element.66), channel_id=1, source_target_pairs={{0,2},{1,3},{2,0},{3,1},{4,6},{5,7},{6,4},{7,5},{8,10},{9,11},{10,... | collective-permute-start | bytes 393224 | tf_op jit(solution)/shard_map/ppermute | solution.py:29
  14.4 5.6 %collective-permute-start.10 = (f32[8,256]{1,0:T(8,128)S(1)}, f32[8,256]{1,0:T(8,128)S(1)}, u32[]{:S(2)}, u32[]{:S(2)}) collective-permute-start(f32[8,256]{1,0:T(8,128)S(1)} %get-tuple-element.54.own_stats.rest_1_), channel_id=1, source_target_pairs={{0,4},{1,5},{2,6},{3,7},{4,0},{5,1},{6,2},{7,3},{8,12},{9,13},{10,... | collective-permute-start | bytes 24584 | tf_op jit(solution)/shard_map/ppermute | solution.py:60
  15.4 5.8 %collective-permute-start.7 = (f32[8,256]{1,0:T(8,128)S(1)}, f32[8,256]{1,0:T(8,128)S(1)}, u32[]{:S(2)}, u32[]{:S(2)}) collective-permute-start(f32[8,256]{1,0:T(8,128)S(1)} %get-tuple-element.54.own_stats.rest_1_), channel_id=1, source_target_pairs={{0,1},{1,0},{2,3},{3,2},{4,8},{5,9},{6,10},{7,11},{8,4},{9,5},{10,... | collective-permute-start | bytes 24584 | tf_op jit(solution)/shard_map/ppermute | solution.py:60
